TPU v7x, 32 devices: a whole 2x2x4 slice. The times are simulated.
32 devices in a mesh: rows: 4 (over z), cols: 8 (over y, x, core).
Axes of the slice: x: 2, y: 2, z: 4, core: 2. Of those that a mesh axis runs over, the one named last changes fastest.
Arguments:
- latents: bfloat16 [2048, 1024], P(('rows', 'cols')), may hold values from -6 to 6
- pixel_colors: bfloat16 [3, 4, 288, 72], P(None, None, 'rows', 'cols'), may hold values from -4 to 4
- image_boxes: int32 [4, 4], replicated, may hold values from 0 to 288, as said below
- cotangent: bfloat16 [2048, 1024], P(('rows', 'cols')), may hold values from -6 to 6
- cross_matrices: bfloat16 [3, 1024, 1024], replicated, may hold values from -0.1875 to 0.1875
- cross_out: bfloat16 [1024, 1024], replicated, may hold values from -0.5 to 0.5
- input_matrices: bfloat16 [2, 261, 1024], replicated, may hold values from -0.375 to 0.375
- in_gain: bfloat16 [261], replicated, may hold values from 0.5 to 1.5
- in_bias: bfloat16 [261], replicated, may hold values from -1.5 to 1.5
- cross_gains: bfloat16 [2, 1024], replicated, may hold values from 0.5 to 1.5
- cross_biases: bfloat16 [7, 1024], replicated, may hold values from -1.5 to 1.5
- self_matrices: bfloat16 [5, 1024, 1024], replicated, may hold values from -0.1875 to 0.1875
- self_out: bfloat16 [1024, 1024], replicated, may hold values from -0.25 to 0.25
- self_gains: bfloat16 [2, 1024], replicated, may hold values from 0.5 to 1.5
- self_biases: bfloat16 [7, 1024], replicated, may hold values from -1.5 to 1.5
- prior_cross_matrices: float32 [3, 1024, 1024], P(None, None, ('rows', 'cols')), may hold values from -6 to 6
- prior_cross_out: float32 [1024, 1024], P(None, ('rows', 'cols')), may hold values from -6 to 6
- prior_input_matrices: float32 [2, 261, 1024], P(None, None, ('rows', 'cols')), may hold values from -96 to 96
Outputs:
- new_latents: bfloat16 [2048, 1024], P(('rows', 'cols'))
- latent_grad: float32 [2048, 1024], P(('rows', 'cols'))
- color_grad: float32 [3, 4, 288, 72], P(None, None, 'rows', 'cols')
- cross_matrices_total: float32 [3, 1024, 1024], P(None, None, ('rows', 'cols'))
- cross_out_total: float32 [1024, 1024], P(None, ('rows', 'cols'))
- input_matrices_total: float32 [2, 261, 1024], P(None, None, ('rows', 'cols'))
- in_gain_grad: float32 [261], replicated
- in_bias_grad: float32 [261], replicated
- cross_gains_grad: float32 [2, 1024], P(None, ('rows', 'cols'))
- cross_biases_grad: float32 [7, 1024], P(None, ('rows', 'cols'))
- self_matrices_grad: float32 [5, 1024, 1024], P(None, None, ('rows', 'cols'))
- self_out_grad: float32 [1024, 1024], P(None, ('rows', 'cols'))
- self_gains_grad: float32 [2, 1024], P(None, ('rows', 'cols'))
- self_biases_grad: float32 [7, 1024], P(None, ('rows', 'cols'))
Inputs may be any that keep to these rules, and one draw needn't show every extreme that they name: `image_boxes`: each row is an image's top row, left column, height and width on the canvas of 288 x 72 pixels; height is (288 * j) // 9 and width (72 * j) // 9 for one j of 5, 7, 9; every box lies inside the canvas, and at least one image fills the whole canvas.
All inputs are finite; a program needn't handle non-finite values.
Results may differ from a plain program's by a relative error of at most 0.019.
Values may be sent and summed in bfloat16 or wider, within the bound.
A program may use at most 256 MiB of HBM per device.

v0:
```python
import jax
import jax.numpy as jnp
from jax import lax
from jax.sharding import PartitionSpec as P

HEADS = 8
LATENTS = 512
NBANDS = 64
HEAD_DIM = 128


EPS = 1e-05
NEG = -1e30
FREQ_TOP = 112.0


def narrow(values):
    return values.astype(jnp.bfloat16)


def to_float(values):
    return values.astype(jnp.float32)


def matmul(former, latter):
    return jnp.dot(former, latter, preferred_element_type=jnp.float32)


def inner_left(former, latter):
    return lax.dot_general(
        former, latter, (((0,), (0,)), ((), ())), preferred_element_type=jnp.float32
    )


def inner_right(former, latter):
    return lax.dot_general(
        former, latter, (((1,), (1,)), ((), ())), preferred_element_type=jnp.float32
    )


def layer_norm(values, gain, offset):
    middle = jnp.mean(values, axis=-1, keepdims=True)
    centered = values - middle
    spread = jnp.mean(centered * centered, axis=-1, keepdims=True)
    return centered * lax.rsqrt(spread + EPS) * gain + offset


def norm_back(values, gain, offset, gradient):
    result, pullback = jax.vjp(layer_norm, values, gain, offset)
    return pullback(gradient)


def gelu_tanh(values):
    return jax.nn.gelu(values, approximate=True)


def gelu_back(pre_gelu, gradient):
    result, pullback = jax.vjp(gelu_tanh, pre_gelu)
    return pullback(gradient)[0]


def pixel_features(colors, image_box, row_start, col_start):
    channels = colors.shape[0]
    tile_rows = colors.shape[1]
    tile_cols = colors.shape[2]
    box_top = image_box[0]
    box_left = image_box[1]
    box_height = image_box[2]
    box_width = image_box[3]
    rows_here = row_start + jnp.arange(tile_rows, dtype=jnp.int32)
    cols_here = col_start + jnp.arange(tile_cols, dtype=jnp.int32)
    grid_rows = jnp.repeat(rows_here, tile_cols)
    grid_cols = jnp.tile(cols_here, tile_rows)
    inside = (
        (grid_rows >= box_top)
        & (grid_rows < box_top + box_height)
        & (grid_cols >= box_left)
        & (grid_cols < box_left + box_width)
    )
    y_place = -1.0 + 2.0 * (grid_rows - box_top).astype(jnp.float32) / (box_height - 1).astype(
        jnp.float32
    )
    x_place = -1.0 + 2.0 * (grid_cols - box_left).astype(jnp.float32) / (box_width - 1).astype(
        jnp.float32
    )
    frequency = 1.0 + jnp.arange(NBANDS, dtype=jnp.float32) * ((FREQ_TOP - 1.0) / (NBANDS - 1))
    y_angle = jnp.pi * y_place[:, None] * frequency[None, :]
    x_angle = jnp.pi * x_place[:, None] * frequency[None, :]
    color_rows = jnp.transpose(colors.reshape(channels, tile_rows * tile_cols)).astype(jnp.float32)
    features = jnp.concatenate(
        [
            color_rows,
            y_place[:, None],
            x_place[:, None],
            jnp.sin(y_angle),
            jnp.sin(x_angle),
            jnp.cos(y_angle),
            jnp.cos(x_angle),
        ],
        axis=1,
    )
    return (features, inside)


def mlp_forward(row_values, gain, offset, w_in, b_in, w_out, b_out):
    normed = narrow(layer_norm(row_values, gain, offset))
    pre_gelu = matmul(normed, w_in) + b_in
    hidden = narrow(gelu_tanh(pre_gelu))
    return (matmul(hidden, w_out) + b_out, (normed, pre_gelu, hidden))


def mlp_backward(row_values, gain, offset, w_in, w_out, stored, gradient):
    normed, pre_gelu, hidden = stored
    grad_low = narrow(gradient)
    d_w_out = inner_left(hidden, grad_low)
    d_b_out = jnp.sum(gradient, axis=0)
    d_pre = gelu_back(pre_gelu, inner_right(grad_low, w_out))
    pre_low = narrow(d_pre)
    d_w_in = inner_left(normed, pre_low)
    d_b_in = jnp.sum(d_pre, axis=0)
    d_rows, d_gain, d_offset = norm_back(row_values, gain, offset, inner_right(pre_low, w_in))
    return (
        gradient + d_rows,
        (d_w_in, d_w_out),
        (d_gain, d_offset, d_b_in, d_b_out),
        (pre_low, grad_low),
    )


def combine_parts(mixed_parts, peak_parts, total_parts):
    best_score = jnp.max(peak_parts, axis=0)
    factor = jnp.exp(peak_parts - best_score[None])
    return (
        jnp.sum(mixed_parts * factor[..., None], axis=0),
        best_score,
        jnp.sum(total_parts * factor, axis=0),
    )


def local(
    latents,
    pixel_colors,
    image_boxes,
    cotangent,
    cross_matrices,
    cross_out,
    input_matrices,
    in_gain,
    in_bias,
    cross_gains,
    cross_biases,
    self_matrices,
    self_out,
    self_gains,
    self_biases,
    prior_cross_matrices,
    prior_cross_out,
    prior_input_matrices,
):
    rows_dev = latents.shape[0]
    model_width = latents.shape[1]
    image_count = image_boxes.shape[0]
    tile_rows = pixel_colors.shape[2]
    tile_cols = pixel_colors.shape[3]
    input_width = input_matrices.shape[1]
    grid_rows = lax.axis_size("rows")
    grid_cols = lax.axis_size("cols")
    all_rows = rows_dev * grid_rows * grid_cols
    row_place = lax.axis_index("rows")
    col_place = lax.axis_index("cols")
    row_start = row_place * tile_rows
    col_start = col_place * tile_cols
    score_scale = model_width ** (-0.5)
    head_scale = HEAD_DIM ** (-0.5)
    g_cross = to_float(cross_gains)
    b_cross = to_float(cross_biases)
    g_self = to_float(self_gains)
    b_self = to_float(self_biases)
    g_input = to_float(in_gain)
    b_input = to_float(in_bias)
    latent_state = to_float(latents)
    normed_q = narrow(layer_norm(latent_state, g_cross[0], b_cross[0]))
    query_rows = narrow(matmul(normed_q, cross_matrices[0]) + b_cross[2])
    queries = lax.all_gather(query_rows, ("rows", "cols"), axis=0, tiled=True).reshape(
        image_count, LATENTS, model_width
    )
    colors = jnp.transpose(pixel_colors, (1, 0, 2, 3))
    key_weight = input_matrices[0]
    value_weight = input_matrices[1]

    def image_inputs(color_image, image_box):
        features, inside = pixel_features(color_image, image_box, row_start, col_start)
        normed = narrow(layer_norm(features, g_input, b_input))
        keys_here = narrow(matmul(normed, key_weight))
        values_here = narrow(matmul(normed, value_weight) + b_cross[3])
        return (features, inside, normed, keys_here, values_here)

    def forward_image(unused_carry, image_items):
        features, inside, normed, keys_here, values_here = image_inputs(
            image_items[0], image_items[1]
        )
        scores = jnp.where(
            inside[None, :], inner_right(image_items[2], keys_here) * score_scale, NEG
        )
        peak_score = jnp.max(scores, axis=1)
        weights = jnp.where(inside[None, :], jnp.exp(scores - peak_score[:, None]), 0.0)
        return (
            unused_carry,
            (matmul(narrow(weights), values_here), peak_score, jnp.sum(weights, axis=1)),
        )

    final_carry, image_parts = lax.scan(
        forward_image, jnp.zeros((), jnp.float32), (colors, image_boxes, queries)
    )
    partial_mixed = image_parts[0].reshape(1, all_rows, model_width)
    partial_peak = image_parts[1].reshape(1, all_rows)
    partial_total = image_parts[2].reshape(1, all_rows)
    mixed_parts, peak_parts, total_parts = (
        lax.all_to_all(
            partial_mixed.astype(jnp.bfloat16),
            ("rows", "cols"),
            split_axis=1,
            concat_axis=0,
            tiled=True,
        ).astype(partial_mixed.dtype),
        lax.all_to_all(
            partial_peak.astype(jnp.bfloat16),
            ("rows", "cols"),
            split_axis=1,
            concat_axis=0,
            tiled=True,
        ).astype(partial_peak.dtype),
        lax.all_to_all(
            partial_total.astype(jnp.bfloat16),
            ("rows", "cols"),
            split_axis=1,
            concat_axis=0,
            tiled=True,
        ).astype(partial_total.dtype),
    )
    mixed_sum, best_score, total_sum = combine_parts(mixed_parts, peak_parts, total_parts)
    attended = mixed_sum / total_sum[:, None]
    log_total = best_score + jnp.log(total_sum)
    attended_low = narrow(attended)
    first = latent_state + matmul(attended_low, cross_out) + b_cross[4]
    branch, cross_stored = mlp_forward(
        first, g_cross[1], b_cross[1], cross_matrices[1], b_cross[5], cross_matrices[2], b_cross[6]
    )
    second = first + branch
    normed_t = narrow(layer_norm(second, g_self[0], b_self[0]))
    tower_queries = narrow(matmul(normed_t, self_matrices[0]) + b_self[2])
    tower_keys = narrow(matmul(normed_t, self_matrices[1]))
    tower_values = narrow(matmul(normed_t, self_matrices[2]) + b_self[3])
    keys_group, values_group = (
        lax.all_gather(tower_keys, "cols", axis=0, tiled=True),
        lax.all_gather(tower_values, "cols", axis=0, tiled=True),
    )
    group_rows = keys_group.shape[0]
    query_image = (
        (row_place * grid_cols + col_place) * rows_dev + jnp.arange(rows_dev, dtype=jnp.int32)
    ) // LATENTS
    key_image = (row_place * group_rows + jnp.arange(group_rows, dtype=jnp.int32)) // LATENTS
    same_image = (query_image[:, None] == key_image[None, :])[None]
    query_heads = tower_queries.reshape(rows_dev, HEADS, HEAD_DIM)
    key_heads = keys_group.reshape(group_rows, HEADS, HEAD_DIM)
    value_heads = values_group.reshape(group_rows, HEADS, HEAD_DIM)
    head_scores = jnp.where(
        same_image,
        jnp.einsum("qhd,khd->hqk", query_heads, key_heads, preferred_element_type=jnp.float32)
        * head_scale,
        NEG,
    )
    head_weights = jnp.where(
        same_image, jnp.exp(head_scores - jnp.max(head_scores, axis=2, keepdims=True)), 0.0
    )
    head_probs = head_weights / jnp.sum(head_weights, axis=2, keepdims=True)
    probs_low = narrow(head_probs)
    tower_mixed = narrow(
        jnp.einsum(
            "hqk,khd->qhd", probs_low, value_heads, preferred_element_type=jnp.float32
        ).reshape(rows_dev, model_width)
    )
    third = second + matmul(tower_mixed, self_out) + b_self[4]
    branch, tower_stored = mlp_forward(
        third, g_self[1], b_self[1], self_matrices[3], b_self[5], self_matrices[4], b_self[6]
    )
    new_latents = narrow(third + branch)
    gradient = to_float(cotangent)
    gradient, tower_mlp_w, tower_mlp_v, tower_lows = mlp_backward(
        third, g_self[1], b_self[1], self_matrices[3], self_matrices[4], tower_stored, gradient
    )
    tower_out_low = narrow(gradient)
    d_self_out = inner_left(tower_mixed, tower_out_low)
    d_self_out_bias = jnp.sum(gradient, axis=0)
    d_mixed = narrow(inner_right(tower_out_low, self_out)).reshape(rows_dev, HEADS, HEAD_DIM)
    d_probs = jnp.einsum("qhd,khd->hqk", d_mixed, value_heads, preferred_element_type=jnp.float32)
    d_value_heads = jnp.einsum(
        "hqk,qhd->khd", probs_low, d_mixed, preferred_element_type=jnp.float32
    )
    d_scores = head_probs * (d_probs - jnp.sum(head_probs * d_probs, axis=2, keepdims=True))
    d_scores_low = narrow(d_scores * head_scale)
    d_query_heads = jnp.einsum(
        "hqk,khd->qhd", d_scores_low, key_heads, preferred_element_type=jnp.float32
    ).reshape(rows_dev, model_width)
    d_key_heads = jnp.einsum(
        "hqk,qhd->khd", d_scores_low, query_heads, preferred_element_type=jnp.float32
    )
    d_tower_keys, d_tower_values = (
        lax.psum_scatter(
            d_key_heads.reshape(group_rows, model_width).astype(jnp.bfloat16),
            "cols",
            scatter_dimension=0,
            tiled=True,
        ).astype(jnp.float32),
        lax.psum_scatter(
            d_value_heads.reshape(group_rows, model_width).astype(jnp.bfloat16),
            "cols",
            scatter_dimension=0,
            tiled=True,
        ).astype(jnp.float32),
    )
    tq_low = narrow(d_query_heads)
    tk_low = narrow(d_tower_keys)
    tv_low = narrow(d_tower_values)
    d_normed_t = (
        inner_right(tq_low, self_matrices[0])
        + inner_right(tk_low, self_matrices[1])
        + inner_right(tv_low, self_matrices[2])
    )
    d_second, d_self_gain, d_self_bias = norm_back(second, g_self[0], b_self[0], d_normed_t)
    gradient = gradient + d_second
    self_gain_grad = jnp.stack([d_self_gain, tower_mlp_v[0]])
    self_bias_grad = jnp.stack(
        [
            d_self_bias,
            tower_mlp_v[1],
            jnp.sum(d_query_heads, axis=0),
            jnp.sum(d_tower_values, axis=0),
            d_self_out_bias,
            tower_mlp_v[2],
            tower_mlp_v[3],
        ]
    )
    gradient, cross_mlp_w, cross_mlp_v, cross_lows = mlp_backward(
        first, g_cross[1], b_cross[1], cross_matrices[1], cross_matrices[2], cross_stored, gradient
    )
    cross_out_low = narrow(gradient)
    d_cross_out = inner_left(attended_low, cross_out_low)
    d_cross_out_bias = jnp.sum(gradient, axis=0)
    d_attended = narrow(inner_right(cross_out_low, cross_out))
    row_delta = jnp.sum(to_float(d_attended) * attended, axis=1)
    d_attended_all = lax.all_gather(d_attended, ("rows", "cols"), axis=0, tiled=True).reshape(
        image_count, LATENTS, model_width
    )
    log_total_all, delta_all = (
        lax.all_gather(log_total, ("rows", "cols"), axis=0, tiled=True),
        lax.all_gather(row_delta, ("rows", "cols"), axis=0, tiled=True),
    )

    def backward_image(sums, image_items):
        color_image, image_box, query_image, d_out_image, log_image, delta_image = image_items
        features, inside, normed, keys_here, values_here = image_inputs(color_image, image_box)
        scores = jnp.where(inside[None, :], inner_right(query_image, keys_here) * score_scale, NEG)
        weights = jnp.where(inside[None, :], jnp.exp(scores - log_image[:, None]), 0.0)
        d_weights = inner_right(d_out_image, values_here)
        d_values_here = inner_left(narrow(weights), d_out_image)
        d_scores_here = narrow(weights * (d_weights - delta_image[:, None]) * score_scale)
        d_query_part = matmul(d_scores_here, keys_here)
        d_keys_low = narrow(inner_left(d_scores_here, query_image))
        d_values_low = narrow(d_values_here)
        d_normed = inner_right(d_keys_low, key_weight) + inner_right(d_values_low, value_weight)
        d_features, d_gain_part, d_bias_part = norm_back(features, g_input, b_input, d_normed)
        new_sums = (
            sums[0] + inner_left(normed, d_keys_low),
            sums[1] + inner_left(normed, d_values_low),
            sums[2] + jnp.sum(d_values_here, axis=0),
            sums[3] + d_gain_part,
            sums[4] + d_bias_part,
        )
        return (new_sums, (d_query_part, jnp.transpose(d_features[:, :3])))

    start_sums = (
        jnp.zeros((input_width, model_width), jnp.float32),
        jnp.zeros((input_width, model_width), jnp.float32),
        jnp.zeros((model_width,), jnp.float32),
        jnp.zeros((input_width,), jnp.float32),
        jnp.zeros((input_width,), jnp.float32),
    )
    pixel_sums, image_grads = lax.scan(
        backward_image,
        start_sums,
        (
            colors,
            image_boxes,
            queries,
            d_attended_all,
            log_total_all.reshape(image_count, LATENTS),
            delta_all.reshape(image_count, LATENTS),
        ),
    )
    d_query_rows = lax.psum_scatter(
        image_grads[0].reshape(all_rows, model_width),
        ("rows", "cols"),
        scatter_dimension=0,
        tiled=True,
    )
    color_grad = jnp.transpose(
        image_grads[1].reshape(image_count, 3, tile_rows, tile_cols), (1, 0, 2, 3)
    )
    query_low = narrow(d_query_rows)
    d_latent, d_cross_gain, d_cross_bias = norm_back(
        latent_state, g_cross[0], b_cross[0], inner_right(query_low, cross_matrices[0])
    )
    latent_grad = gradient + d_latent
    in_gain_grad, in_bias_grad = lax.psum((pixel_sums[3], pixel_sums[4]), ("rows", "cols"))
    input_mat_grad = jnp.stack([pixel_sums[0], pixel_sums[1]])
    cross_gain_grad = jnp.stack([d_cross_gain, cross_mlp_v[0]])
    cross_bias_grad = jnp.stack(
        [
            d_cross_bias,
            cross_mlp_v[1],
            jnp.sum(d_query_rows, axis=0),
            pixel_sums[2],
            d_cross_out_bias,
            cross_mlp_v[2],
            cross_mlp_v[3],
        ]
    )
    cross_mat_grad = jnp.stack([inner_left(normed_q, query_low), cross_mlp_w[0], cross_mlp_w[1]])
    self_mat_grad = jnp.stack(
        [
            inner_left(normed_t, tq_low),
            inner_left(normed_t, tk_low),
            inner_left(normed_t, tv_low),
            tower_mlp_w[0],
            tower_mlp_w[1],
        ]
    )
    all_sums = (
        lax.psum_scatter(cross_mat_grad, ("rows", "cols"), scatter_dimension=2, tiled=True),
        lax.psum_scatter(d_cross_out, ("rows", "cols"), scatter_dimension=1, tiled=True),
        lax.psum_scatter(input_mat_grad, ("rows", "cols"), scatter_dimension=2, tiled=True),
        lax.psum_scatter(cross_gain_grad, ("rows", "cols"), scatter_dimension=1, tiled=True),
        lax.psum_scatter(cross_bias_grad, ("rows", "cols"), scatter_dimension=1, tiled=True),
        lax.psum_scatter(self_mat_grad, ("rows", "cols"), scatter_dimension=2, tiled=True),
        lax.psum_scatter(d_self_out, ("rows", "cols"), scatter_dimension=1, tiled=True),
        lax.psum_scatter(self_gain_grad, ("rows", "cols"), scatter_dimension=1, tiled=True),
        lax.psum_scatter(self_bias_grad, ("rows", "cols"), scatter_dimension=1, tiled=True),
    )
    cross_sums = all_sums[:5]
    self_sums = all_sums[5:]
    return (
        new_latents,
        latent_grad,
        color_grad,
        prior_cross_matrices + cross_sums[0],
        prior_cross_out + cross_sums[1],
        prior_input_matrices + cross_sums[2],
        in_gain_grad,
        in_bias_grad,
        cross_sums[3],
        cross_sums[4],
        self_sums[0],
        self_sums[1],
        self_sums[2],
        self_sums[3],
    )


def solution(mesh):
    placed = (
        P(("rows", "cols"), None),
        P(None, None, "rows", "cols"),
        P(),
        P(("rows", "cols"), None),
        P(),
        P(),
        P(),
        P(),
        P(),
        P(),
        P(),
        P(),
        P(),
        P(),
        P(),
        P(None, None, ("rows", "cols")),
        P(None, ("rows", "cols")),
        P(None, None, ("rows", "cols")),
    )
    return jax.shard_map(
        local,
        mesh=mesh,
        in_specs=placed,
        out_specs=(
            P(("rows", "cols"), None),
            P(("rows", "cols"), None),
            P(None, None, "rows", "cols"),
            P(None, None, ("rows", "cols")),
            P(None, ("rows", "cols")),
            P(None, None, ("rows", "cols")),
            P(),
            P(),
            P(None, ("rows", "cols")),
            P(None, ("rows", "cols")),
            P(None, None, ("rows", "cols")),
            P(None, ("rows", "cols")),
            P(None, ("rows", "cols")),
            P(None, ("rows", "cols")),
        ),
        check_vma=False,
    )
```

profile of v0, /device:TPU:0, one launch (start us, length us, event | category | flops | bytes accessed | tf_op | source)
XLA Modules:
  0.0 2470.2 jit_solution(18067676819278457319)
XLA Ops:
  22.3 57.9 %all-gather.5.cloned.1.call-done = bf16[2048,1024]{1,0:T(8,128)(2,1)} async-done(((bf16[64,1024]{1,0:T(8,128)(2,1)}), bf16[2048,1024]{1,0:T(8,128)(2,1)}) %all-gather.5.cloned.1.call-update) | async-done | bytes 4194320 | tf_op jit(solution)/shard_map/all_gather | solution.py:184
  80.3 100.7 %while.45 = (s32[]{:T(128)}, bf16[4,512,1024]{2,1,0:T(8,128)(2,1)}, bf16[4,512]{1,0:T(4,128)(2,1)S(1)}, bf16[4,512]{1,0:T(4,128)(2,1)S(1)}, s32[]{:T(128)}, /*in...) while((s32[]{:T(128)}, bf16[4,512,1024]{2,1,0:T(8,128)(2,1)}, ...), condition=%wide.region_11.12_spmd.clone, body=%wide.region_2.11_spmd.sunk.clone | while | flops 2059136000 | bytes 14553185 | solution.py:212
  95.3 4.2 fusion.416
  101.2 4.3 bitcast_dynamic-update-slice_fusion.11
  120.5 4.2 fusion.416
  126.5 4.2 bitcast_dynamic-update-slice_fusion.11
  145.7 4.2 fusion.416
  151.6 4.2 bitcast_dynamic-update-slice_fusion.11
  170.9 4.2 fusion.416
  176.8 4.2 bitcast_dynamic-update-slice_fusion.11
  181.7 3.2 all-to-all-start.2
  185.5 6.4 all-to-all-done.2
  194.4 8.6 copy.274
  203.6 26.0 %reduce.61 = bf16[2048,1024]{1,0:T(8,128)(2,1)} reduce(bf16[2048,1,1024]{2,1,0:T(2,128)(2,1)} %bitcast.455, bf16[]{:T(256)} %broadcast.1328), dimensions={1}, to_apply=%bitcast.328.reduce_sub_computation | reduce | bytes 8388610
  229.5 7.8 reshape.885
  237.3 6.0 all-to-all-start
  244.5 92.7 %all-to-all-done = bf16[32,2,32768]{2,1,0:T(2,128)(2,1)} async-done(((bf16[32,2,32768]{2,1,0:T(2,128)(2,1)}), bf16[32,2,32768]{2,1,0:T(2,128)(2,1)}, u32[]{:S(2)}, u32[]{:S(2)}) %all-to-all-start) | async-done | bytes 4194336 | tf_op jit(solution)/shard_map/all_to_all | solution.py:219
  337.2 19.8 reshape.886
  357.0 5.5 copy.170
  374.9 18.0 all-gather.9.cloned.1.call-done
  396.9 22.0 all-gather.7.cloned.1.call-done
  418.9 3.5 fusion.162
  427.8 3.0 fusion.278
  430.8 3.1 multiply_reduce_fusion.6
  436.7 5.9 convolution_convert_fusion.4
  445.0 3.7 convolution_convert_fusion.3
  451.0 5.8 fusion.267
  456.9 24.2 reduce-scatter.34.cloned.1.call-done
  483.5 3.0 fusion.129
  486.6 33.6 %reduce-scatter.36.cloned.1.call-done = bf16[64,1024]{1,0:T(8,128)(2,1)} async-done(((bf16[512,1024]{1,0:T(8,128)(2,1)}), bf16[64,1024]{1,0:T(8,128)(2,1)}) %reduce-scatter.36.cloned.1.call-update) | async-done | bytes 131088
  520.2 3.1 multiply_reduce_fusion.7
  524.3 3.1 fusion.277
  527.4 3.0 multiply_reduce_fusion.8
  534.5 39.8 %all-reduce.4 = (f32[2048]{0:T(1024)S(1)}, f32[2048]{0:T(1024)S(1)}) all-reduce(f32[2048]{0:T(1024)S(1)} %add_dynamic-update-slice_fusion, f32[2048]{0:T(1024)S(1)} %dynamic-update-slice.1), channel_id=1, replica_groups=mesh['rows'=4,'cols'=8] {'rows','cols'}, use_global_device_ids=true, to_apply=%add | all-reduce | flops 4096 | bytes 32768
  574.4 21.8 all-gather.11.cloned.1.call-done
  596.2 158.2 %while.46 = (s32[]{:T(128)}, f32[261,1024]{1,0:T(8,128)}, f32[261,1024]{1,0:T(8,128)S(1)}, f32[1024]{0:T(1024)S(1)}, f32[261]{0:T(512)S(1)}, /*index=5*/f32[261]...) while((s32[]{:T(128)}, f32[261,1024]{1,0:T(8,128)}, ...), condition=%wide.region_45.46_spmd.clone.clone, body=%wide.region_33.0_spmd.clone.sunk.clone | while | flops 5487993344 | bytes 59466284 | solution.py:389
  614.1 3.3 fusion.443
  617.5 4.1 fusion.444
  631.8 3.9 bitcast_dynamic-update-slice_fusion.12
  653.7 3.3 fusion.443
  657.1 4.1 fusion.444
  671.4 3.9 bitcast_dynamic-update-slice_fusion.12
  693.2 3.3 fusion.443
  696.6 4.1 fusion.444
  710.9 3.9 bitcast_dynamic-update-slice_fusion.12
  732.8 3.3 fusion.443
  736.1 4.1 fusion.444
  750.5 3.9 bitcast_dynamic-update-slice_fusion.12
  765.3 3.8 pad_maximum_fusion.1
  772.9 128.9 %reduce-scatter.24.cloned.1.call-done = f32[64,1024]{1,0:T(8,128)} async-done(((f32[2048,1024]{1,0:T(8,128)}), f32[64,1024]{1,0:T(8,128)}) %reduce-scatter.24.cloned.1.call-update) | async-done | bytes 262160 | tf_op jit(solution)/shard_map/reduce_scatter | solution.py:401
  912.2 6.5 pad_maximum_fusion
  918.7 18.5 copy.148
  951.8 28.4 %copy.152 = f32[5,1024,1024]{1,0,2:T(8,128)} copy(f32[5,1024,1024]{2,1,0:T(8,128)} %bitcast_dynamic-update-slice_fusion.2) | data formatting | bytes 41943040 | tf_op jit(solution)/shard_map/stack | solution.py:430
  981.2 2.9 fusion.209
  987.5 46.4 %reduce-scatter.42.cloned.1.call-done = f32[32,2]{1,0:T(8,128)} async-done(((f32[1024,2]{1,0:T(8,128)}), f32[32,2]{1,0:T(8,128)}) %reduce-scatter.42.cloned.1.call-update) | async-done | bytes 272
  1035.3 130.7 %reduce-scatter.44.cloned.1.call-done = f32[32,7]{1,0:T(8,128)} async-done(((f32[1024,7]{1,0:T(8,128)}), f32[32,7]{1,0:T(8,128)}) %reduce-scatter.44.cloned.1.call-update) | async-done | bytes 912
  1168.4 37.5 %all-reduce.3 = (f32[261]{0:T(512)}, f32[261]{0:T(512)}) all-reduce(f32[261]{0:T(512)S(1)} %get-tuple-element.541, f32[261]{0:T(512)S(1)} %get-tuple-element.542), channel_id=1, replica_groups=mesh['rows'=4,'cols'=8] {'rows','cols'}, use_global_device_ids=true, to_apply=%region_52.53 | all-reduce | flops 522 | bytes 4176 | tf_op jit(solution)/shard_map/psum | solution.py:415
  1205.9 99.2 %reduce-scatter.26.cloned.1.call-done = f32[1024,32]{0,1:T(8,128)} async-done(((f32[1024,1024]{0,1:T(8,128)}), f32[1024,32]{0,1:T(8,128)}) %reduce-scatter.26.cloned.1.call-update) | async-done | bytes 131088 | tf_op jit(solution)/shard_map/reduce_scatter | solution.py:441
  1306.7 101.4 %reduce-scatter.28.cloned.1.call-done = f32[2,261,32]{1,2,0:T(8,128)} async-done(((f32[2,261,1024]{1,2,0:T(8,128)}), f32[2,261,32]{1,2,0:T(8,128)}) %reduce-scatter.28.cloned.1.call-update) | async-done | bytes 66832 | tf_op jit(solution)/shard_map/reduce_scatter | solution.py:442
  1411.6 132.2 %reduce-scatter.38.cloned.1.call-done = f32[32,2]{1,0:T(8,128)} async-done(((f32[1024,2]{1,0:T(8,128)}), f32[32,2]{1,0:T(8,128)}) %reduce-scatter.38.cloned.1.call-update) | async-done | bytes 272
  1545.1 130.8 %reduce-scatter.40.cloned.1.call-done = f32[32,7]{1,0:T(8,128)} async-done(((f32[1024,7]{1,0:T(8,128)}), f32[32,7]{1,0:T(8,128)}) %reduce-scatter.40.cloned.1.call-update) | async-done | bytes 912
  1677.3 278.4 %all-reduce.7.cloned.1.call-done = f32[3,1024,1024]{1,0,2:T(4,128)} async-done(((f32[3,1024,1024]{1,0,2:T(4,128)}), f32[3,1024,1024]{1,0,2:T(4,128)}) %all-reduce.7.cloned.1.call-update) | async-done | bytes 12582928
  1958.2 353.9 %reduce-scatter.30.cloned.1.call-done = f32[5,1024,32]{1,0,2:T(8,128)} async-done(((f32[5,1024,1024]{1,0,2:T(8,128)}), f32[5,1024,32]{1,0,2:T(8,128)}) %reduce-scatter.30.cloned.1.call-update) | async-done | bytes 655376 | tf_op jit(solution)/shard_map/reduce_scatter | solution.py:445
  2314.5 148.7 %reduce-scatter.32.cloned.1.call-done = f32[1024,32]{0,1:T(8,128)} async-done(((f32[1024,1024]{0,1:T(8,128)}), f32[1024,32]{0,1:T(8,128)}) %reduce-scatter.32.cloned.1.call-update) | async-done | bytes 131088 | tf_op jit(solution)/shard_map/reduce_scatter | solution.py:446
  (768 shorter events, 264.2 us)
Async XLA Ops:
  7.2 356.0 %copy-start = (bf16[1024,1024]{1,0:T(8,128)(2,1)S(1)}, bf16[1024,1024]{1,0:T(8,128)(2,1)}, u32[]{:S(2)}) copy-start(bf16[1024,1024]{1,0:T(8,128)(2,1)} %param.27) | copy-start | bytes 6291460
  7.2 8.8 copy-start.106
  7.2 8.8 copy-start.107
  7.2 8.8 copy-start.62
  7.2 73.0 %all-gather.5.cloned.1.call-start = ((), (), s32[]{:S(2)}) async-start(), calls=%async_computation.14 | async-start | bytes 4325376 | tf_op jit(solution)/shard_map/all_gather | solution.py:184
  8.5 10.9 copy-start.78
  10.1 9.3 copy-start.80
  20.9 59.3 %copy-start.110 = (s32[4,4]{1,0:T(4,128)S(1)}, s32[4,4]{1,0:T(4,128)}, u32[]{:S(2)}) copy-start(s32[4,4]{1,0:T(4,128)} %param.24) | copy-start | bytes 196
  181.7 10.2 all-to-all-start.2
  191.9 45.4 %all-to-all-start.1 = ((bf16[1,32,64]{2,0,1:T(2,128)(2,1)}), bf16[1,32,64]{2,0,1:T(2,128)(2,1)S(1)}, u32[]{:S(2)}, u32[]{:S(2)}) async-start(bf16[1,32,64]{2,0,1:T(2,128)(2,1)} %convert_element_type.522), calls=%async_computation.1 | async-start | bytes 32768 | tf_op jit(solution)/shard_map/all_to_all | solution.py:226
  237.3 99.8 %all-to-all-start = ((bf16[32,2,32768]{2,1,0:T(2,128)(2,1)}), bf16[32,2,32768]{2,1,0:T(2,128)(2,1)}, u32[]{:S(2)}, u32[]{:S(2)}) async-start(bf16[32,2,32768]{2,1,0:T(2,128)(2,1)} %reshape.885), calls=%async_computation | async-start | bytes 8388608 | tf_op jit(solution)/shard_map/all_to_all | solution.py:219
  243.3 149.6 %all-gather.9.cloned.1.call-start = ((), (), s32[]{:S(2)}) async-start(), calls=%async_computation.16 | async-start | bytes 1179648 | tf_op jit(solution)/shard_map/all_gather | solution.py:255
  243.7 190.2 %copy-start.59 = (f32[1,1024]{1,0:T(1,128)}, f32[1,1024]{1,0:T(1,128)S(1)}, u32[]{:S(2)}) copy-start(f32[1,1024]{1,0:T(1,128)S(1)} %get-tuple-element.866) | copy-start | bytes 12292
  244.4 180.6 %copy-start.64 = (f32[1,1024]{1,0:T(1,128)}, f32[1,1024]{1,0:T(1,128)S(1)}, u32[]{:S(2)}) copy-start(f32[1,1024]{1,0:T(1,128)S(1)} %get-tuple-element.851) | copy-start | bytes 12292
  244.4 112.5 %copy-start.104 = (bf16[64]{0:T(256)(128)(2,1)}, bf16[64]{0:T(256)(128)(2,1)S(1)}, u32[]{:S(2)}) copy-start(bf16[64]{0:T(256)(128)(2,1)S(1)} %get-tuple-element.864) | copy-start | bytes 388
  244.5 289.7 %copy-start.76 = (f32[64]{0:T(128)}, f32[64]{0:T(128)S(1)}, u32[]{:S(2)}) copy-start(f32[64]{0:T(128)S(1)} %get-tuple-element.818) | copy-start | bytes 772
  363.1 169.3 %copy-start.11 = (f32[64,1024]{1,0:T(8,128)}, f32[64,1024]{1,0:T(8,128)S(1)}, u32[]{:S(2)}) copy-start(f32[64,1024]{1,0:T(8,128)S(1)} %multiply_reduce_fusion.4) | copy-start | bytes 786436
  364.1 163.2 %copy-start.15 = (f32[64,1024]{1,0:T(8,128)}, f32[64,1024]{1,0:T(8,128)S(1)}, u32[]{:S(2)}) copy-start(f32[64,1024]{1,0:T(8,128)S(1)} %get-tuple-element.871) | copy-start | bytes 786436
  364.2 166.3 %copy-start.82 = (f32[64]{0:T(128)}, f32[64]{0:T(128)S(1)}, u32[]{:S(2)}) copy-start(f32[64]{0:T(128)S(1)} %broadcast_multiply_fusion.6) | copy-start | bytes 772
  364.4 166.1 %copy-start.100 = (f32[64]{0:T(128)}, f32[64]{0:T(128)S(1)}, u32[]{:S(2)}) copy-start(f32[64]{0:T(128)S(1)} %fusion.246) | copy-start | bytes 772
  369.8 49.1 %all-gather.7.cloned.1.call-start = ((), (), s32[]{:S(2)}) async-start(), calls=%async_computation.15 | async-start | bytes 1179648 | tf_op jit(solution)/shard_map/all_gather | solution.py:256
  372.7 108.5 %reduce-scatter.34.cloned.1.call-start = ((), (), s32[]{:S(2)}) async-start(), calls=%async_computation.23 | async-start | bytes 1179648
  374.9 22.0 copy-start.48
  424.7 9.3 copy-start.13
  424.7 9.3 copy-start.84
  424.9 9.1 copy-start.102
  434.3 89.2 %copy-start.86 = (f32[64]{0:T(128)}, f32[64]{0:T(128)S(1)}, u32[]{:S(2)}) copy-start(f32[64]{0:T(128)S(1)} %negate_multiply_fusion.4) | copy-start | bytes 772
  444.9 75.3 %reduce-scatter.36.cloned.1.call-start = ((), (), s32[]{:S(2)}) async-start(), calls=%async_computation.24 | async-start | bytes 1179648
  451.0 145.2 %all-gather.11.cloned.1.call-start = ((), (), s32[]{:S(2)}) async-start(), calls=%async_computation.17 | async-start | bytes 4325376 | tf_op jit(solution)/shard_map/all_gather | solution.py:352
  456.9 26.7 %copy-start.35 = (bf16[8,8,8,128]{3,2,1,0:T(8,128)(2,1)}, bf16[8,8,8,128]{3,2,1,0:T(8,128)(2,1)S(1)}, u32[]{:S(2)}) copy-start(bf16[8,8,8,128]{3,2,1,0:T(8,128)(2,1)S(1)} %get-tuple-element.850) | copy-start | bytes 393220
  486.6 36.9 %copy-start.22 = (f32[64,1024]{1,0:T(8,128)S(1)}, f32[64,1024]{1,0:T(8,128)}, u32[]{:S(2)}) copy-start(f32[64,1024]{1,0:T(8,128)} %copy-done.21) | copy-start | bytes 786436
  530.5 65.7 %copy-start.6 = (bf16[261,1024]{1,0:T(8,128)(2,1)S(1)}, bf16[261,1024]{1,0:T(8,128)(2,1)}, u32[]{:S(2)}) copy-start(bf16[261,1024]{1,0:T(8,128)(2,1)} %get-tuple-element.1514) | copy-start | bytes 1603588
  532.4 63.7 %copy-start.17 = (f32[64,1024]{1,0:T(8,128)}, f32[64,1024]{1,0:T(8,128)S(1)}, u32[]{:S(2)}) copy-start(f32[64,1024]{1,0:T(8,128)S(1)} %get-tuple-element.811) | copy-start | bytes 786436
  534.0 367.8 %reduce-scatter.24.cloned.1.call-start = ((), (), s32[]{:S(2)}) async-start(), calls=%async_computation.18 | async-start | bytes 8650752 | tf_op jit(solution)/shard_map/reduce_scatter | solution.py:401
  596.2 11.2 copy-start.55
  635.8 8.6 copy-start.57
  635.8 11.2 copy-start.55
  675.3 11.2 copy-start.55
  714.8 8.6 copy-start.57
  714.8 11.2 copy-start.55
  754.5 279.5 %reduce-scatter.42.cloned.1.call-start = ((), (), s32[]{:S(2)}) async-start(), calls=%async_computation.27 | async-start | bytes 540672
  756.1 409.9 %reduce-scatter.44.cloned.1.call-start = ((), (), s32[]{:S(2)}) async-start(), calls=%async_computation.28 | async-start | bytes 540672
  757.9 547.2 %reduce-scatter.26.cloned.1.call-start = ((), (), s32[]{:S(2)}) async-start(), calls=%async_computation.19 | async-start | bytes 4325376 | tf_op jit(solution)/shard_map/reduce_scatter | solution.py:441
  760.7 647.4 %reduce-scatter.28.cloned.1.call-start = ((), (), s32[]{:S(2)}) async-start(), calls=%async_computation.20 | async-start | bytes 3244032 | tf_op jit(solution)/shard_map/reduce_scatter | solution.py:442
  769.1 132.7 %copy-start.53 = (f32[1,1024]{1,0:T(1,128)S(1)}, f32[1,1024]{1,0:T(1,128)}, u32[]{:S(2)}) copy-start(f32[1,1024]{1,0:T(1,128)} %copy-done.52) | copy-start | bytes 12292
  769.1 132.7 %copy-start.79 = (f32[64]{0:T(128)S(1)}, f32[64]{0:T(128)}, u32[]{:S(2)}) copy-start(f32[64]{0:T(128)} %copy-done.78) | copy-start | bytes 772
  769.1 774.7 %reduce-scatter.38.cloned.1.call-start = ((), (), s32[]{:S(2)}) async-start(), calls=%async_computation.25 | async-start | bytes 540672
  772.8 131.6 %copy-start.109 = (f32[64]{0:T(128)S(1)}, f32[64]{0:T(128)}, u32[]{:S(2)}) copy-start(f32[64]{0:T(128)} %copy-done.108) | copy-start | bytes 772
  772.8 131.6 %copy-start.81 = (f32[64]{0:T(128)S(1)}, f32[64]{0:T(128)}, u32[]{:S(2)}) copy-start(f32[64]{0:T(128)} %copy-done.80) | copy-start | bytes 772
  772.8 131.9 %copy-start.92 = (f32[1024]{0:T(1024)S(1)}, f32[1024]{0:T(1024)}, u32[]{:S(2)}) copy-start(f32[1024]{0:T(1024)} %get-tuple-element.713) | copy-start | bytes 12292
  772.8 133.1 %copy-start.16 = (f32[64,1024]{1,0:T(8,128)S(1)}, f32[64,1024]{1,0:T(8,128)}, u32[]{:S(2)}) copy-start(f32[64,1024]{1,0:T(8,128)} %copy-done.15) | copy-start | bytes 786436
  772.8 133.1 %copy-start.47 = (bf16[64,1024]{1,0:T(8,128)(2,1)S(1)}, bf16[64,1024]{1,0:T(8,128)(2,1)}, u32[]{:S(2)}) copy-start(bf16[64,1024]{1,0:T(8,128)(2,1)} %copy-done.46) | copy-start | bytes 393220
  772.8 133.1 %copy-start.69 = (f32[1,1024]{1,0:T(1,128)S(1)}, f32[1,1024]{1,0:T(1,128)}, u32[]{:S(2)}) copy-start(f32[1,1024]{1,0:T(1,128)} %get-tuple-element.858) | copy-start | bytes 12292
  772.8 133.1 %copy-start.83 = (f32[64]{0:T(128)S(1)}, f32[64]{0:T(128)}, u32[]{:S(2)}) copy-start(f32[64]{0:T(128)} %copy-done.82) | copy-start | bytes 772
  772.8 133.1 %copy-start.101 = (f32[64]{0:T(128)S(1)}, f32[64]{0:T(128)}, u32[]{:S(2)}) copy-start(f32[64]{0:T(128)} %copy-done.100) | copy-start | bytes 772
  905.8 770.1 %reduce-scatter.40.cloned.1.call-start = ((), (), s32[]{:S(2)}) async-start(), calls=%async_computation.26 | async-start | bytes 540672
  909.9 1045.8 %all-reduce.7.cloned.1.call-start = ((), (), s32[]{:S(2)}) async-start(), calls=%async_computation.29 | async-start | bytes 33554432
  937.2 1374.9 %reduce-scatter.30.cloned.1.call-start = ((), (), s32[]{:S(2)}) async-start(), calls=%async_computation.21 | async-start | bytes 34603008 | tf_op jit(solution)/shard_map/reduce_scatter | solution.py:445
  980.2 1483.0 %reduce-scatter.32.cloned.1.call-start = ((), (), s32[]{:S(2)}) async-start(), calls=%async_computation.22 | async-start | bytes 4325376 | tf_op jit(solution)/shard_map/reduce_scatter | solution.py:446
  984.1 183.3 %copy-start.61 = (f32[4,3,648]{2,0,1:T(4,128)S(1)}, f32[4,3,648]{2,0,1:T(4,128)}, u32[]{:S(2)}) copy-start(f32[4,3,648]{2,0,1:T(4,128)} %get-tuple-element.538) | copy-start | bytes 93316
  984.7 320.4 %copy-start.42 = (f32[1024,32]{0,1:T(8,128)S(1)}, f32[1024,32]{0,1:T(8,128)}, u32[]{:S(2)}) copy-start(f32[1024,32]{0,1:T(8,128)} %param.38) | copy-start | bytes 393220
  984.7 423.3 %copy-start.51 = (f32[2,261,32]{1,2,0:T(8,128)S(1)}, f32[2,261,32]{1,2,0:T(8,128)}, u32[]{:S(2)}) copy-start(f32[2,261,32]{1,2,0:T(8,128)} %param.39) | copy-start | bytes 200452
  984.7 424.9 %copy-start.19 = (f32[64,1024]{1,0:T(8,128)S(1)}, f32[64,1024]{1,0:T(8,128)}, u32[]{:S(2)}) copy-start(f32[64,1024]{1,0:T(8,128)} %copy-done.17) | copy-start | bytes 786436
  1409.6 1053.6 %copy-start.1 = (bf16[1024,1024]{1,0:T(8,128)(2,1)S(1)}, bf16[1024,1024]{1,0:T(8,128)(2,1)}, u32[]{:S(2)}) copy-start(bf16[1024,1024]{1,0:T(8,128)(2,1)} %param.27) | copy-start | bytes 6291460
  (107 other events, 306.5 us)
Sparse Core Ops, SparseCore 0:
  15.5 64.7 all-gather.4
  370.0 22.9 all-gather.8
  395.4 23.4 all-gather.6
  445.0 36.0 reduce-scatter.33
  484.1 35.9 reduce-scatter.35
  534.1 62.0 all-gather.10
  754.6 147.1 reduce-scatter.23
  904.0 129.8 reduce-scatter.41
  1036.3 129.6 reduce-scatter.43
  1168.1 136.9 reduce-scatter.25
  1310.5 97.4 reduce-scatter.27
  1410.7 132.9 reduce-scatter.37
  1546.1 129.7 reduce-scatter.39
  1681.9 273.8 all-reduce.6
  1957.9 354.1 reduce-scatter.29
  2314.8 148.4 reduce-scatter.31
where the time goes:
time: 2490 us; the launch traced here: 2470 us
  waiting for transfers between devices  1830 us (73%)
  matrix products  211 us (8%)
  local copies, waits for them, and re-layouts  179 us (7%)
  other arithmetic  114 us (5%)
  blocking collectives  77.3 us (3%)
  loops' own time  32.7 us (1%)
    unnamed x23, waiting for transfers between devices  777 us
    reduce_scatter x1, waiting for transfers between devices, local(): lax.psum_scatter(self_mat_grad, ('rows', 'cols'), scatter_dimension=2, ti...  354 us
    reduce_scatter x1, waiting for transfers between devices, local(): lax.psum_scatter(d_self_out, ('rows', 'cols'), scatter_dimension=1, tiled...  149 us
    reduce_scatter x1, waiting for transfers between devices, local(): lax.psum_scatter(image_grads[0].reshape(all_rows, model_width), ('rows',...  129 us
    reduce_scatter x1, waiting for transfers between devices, local(): lax.psum_scatter(input_mat_grad, ('rows', 'cols'), scatter_dimension=2, t...  101 us
    reduce_scatter x1, waiting for transfers between devices, local(): lax.psum_scatter(d_cross_out, ('rows', 'cols'), scatter_dimension=1, tile...  99.2 us
    all_to_all x1, waiting for transfers between devices, local(): lax.all_to_all(partial_mixed.astype(jnp.bfloat16), ('rows', 'cols'), spli...  92.7 us
    dot_general x30, matrix products, inner_right(): lax.dot_general(former, latter, (((1,), (1,)), ((), ())), preferred_eleme...  78.8 us
  transfers between devices with their start and end apart: 19, of which 18 were waited for; matrix products, arithmetic and copies ran while one was open for 8% of the time, Pallas kernels for 0%

commit v1 on v0

--- a/solution.py
+++ b/solution.py
@@ -59,47 +59,94 @@
     return pullback(gradient)[0]
 
 
-def pixel_features(colors, image_box, row_start, col_start):
-    channels = colors.shape[0]
-    tile_rows = colors.shape[1]
-    tile_cols = colors.shape[2]
-    box_top = image_box[0]
-    box_left = image_box[1]
-    box_height = image_box[2]
-    box_width = image_box[3]
-    rows_here = row_start + jnp.arange(tile_rows, dtype=jnp.int32)
-    cols_here = col_start + jnp.arange(tile_cols, dtype=jnp.int32)
-    grid_rows = jnp.repeat(rows_here, tile_cols)
-    grid_cols = jnp.tile(cols_here, tile_rows)
-    inside = (
-        (grid_rows >= box_top)
-        & (grid_rows < box_top + box_height)
-        & (grid_cols >= box_left)
-        & (grid_cols < box_left + box_width)
-    )
-    y_place = -1.0 + 2.0 * (grid_rows - box_top).astype(jnp.float32) / (box_height - 1).astype(
-        jnp.float32
-    )
-    x_place = -1.0 + 2.0 * (grid_cols - box_left).astype(jnp.float32) / (box_width - 1).astype(
-        jnp.float32
-    )
+def axis_features(places, extent):
     frequency = 1.0 + jnp.arange(NBANDS, dtype=jnp.float32) * ((FREQ_TOP - 1.0) / (NBANDS - 1))
-    y_angle = jnp.pi * y_place[:, None] * frequency[None, :]
-    x_angle = jnp.pi * x_place[:, None] * frequency[None, :]
-    color_rows = jnp.transpose(colors.reshape(channels, tile_rows * tile_cols)).astype(jnp.float32)
-    features = jnp.concatenate(
+    angle = jnp.pi * places[:, None] * frequency[None, :]
+    return (places, jnp.sin(angle), jnp.cos(angle))
+
+
+def canvas_of(colors, image_box):
+    channels, wide, tall = colors.shape
+    top, left, height, width = image_box[0], image_box[1], image_box[2], image_box[3]
+    row_at = jnp.arange(tall, dtype=jnp.int32)
+    col_at = jnp.arange(wide, dtype=jnp.int32)
+    y_place = -1.0 + 2.0 * to_float(row_at - top) / to_float(height - 1)
+    x_place = -1.0 + 2.0 * to_float(col_at - left) / to_float(width - 1)
+    y_parts = axis_features(y_place, height)
+    x_parts = axis_features(x_place, width)
+    y_all = jnp.concatenate([y_parts[0][:, None], y_parts[1], y_parts[2]], axis=1)
+    x_all = jnp.concatenate([x_parts[0][:, None], x_parts[1], x_parts[2]], axis=1)
+    count = channels + 2 + 4 * NBANDS
+    color_sum = jnp.sum(colors, axis=0)
+    color_square = jnp.sum(colors * colors, axis=0)
+    mean = (color_sum + jnp.sum(y_all, axis=1)[None, :] + jnp.sum(x_all, axis=1)[:, None]) / count
+    square = (
+        color_square
+        + jnp.sum(y_all * y_all, axis=1)[None, :]
+        + jnp.sum(x_all * x_all, axis=1)[:, None]
+    ) / count
+    deviation = lax.rsqrt(square - mean * mean + EPS)
+    row_in = (row_at >= top) & (row_at < top + height)
+    col_in = (col_at >= left) & (col_at < left + width)
+    return (y_all, x_all, mean, deviation, row_in, col_in)
+
+
+def split_channels(rows, channels):
+    n = NBANDS
+    c = channels
+    y_part = jnp.concatenate(
+        [rows[:, c : c + 1], rows[:, c + 2 : c + 2 + n], rows[:, c + 2 + 2 * n : c + 2 + 3 * n]],
+        axis=1,
+    )
+    x_part = jnp.concatenate(
         [
-            color_rows,
-            y_place[:, None],
-            x_place[:, None],
-            jnp.sin(y_angle),
-            jnp.sin(x_angle),
-            jnp.cos(y_angle),
-            jnp.cos(x_angle),
+            rows[:, c + 1 : c + 2],
+            rows[:, c + 2 + n : c + 2 + 2 * n],
+            rows[:, c + 2 + 3 * n : c + 2 + 4 * n],
         ],
         axis=1,
     )
-    return (features, inside)
+    return (rows[:, :c], y_part, x_part)
+
+
+def join_channels(color_part, y_part, x_part):
+    n = NBANDS
+    return jnp.concatenate(
+        [
+            color_part,
+            y_part[:, :1],
+            x_part[:, :1],
+            y_part[:, 1 : n + 1],
+            x_part[:, 1 : n + 1],
+            y_part[:, n + 1 :],
+            x_part[:, n + 1 :],
+        ],
+        axis=1,
+    )
+
+
+def against_pixels(rows, colors, canvas):
+    y_all, x_all, mean, deviation = canvas[:4]
+    color_part, y_part, x_part = split_channels(rows, colors.shape[0])
+    by_row = inner_right(narrow(y_part), narrow(y_all))
+    by_col = inner_right(narrow(x_part), narrow(x_all))
+    total = by_row[:, None, :] + by_col[:, :, None]
+    for j in range(colors.shape[0]):
+        total = total + color_part[:, j][:, None, None] * colors[j][None]
+    total = total - jnp.sum(rows, axis=1)[:, None, None] * mean[None]
+    return total * deviation[None]
+
+
+def over_pixels(weights, colors, canvas):
+    y_all, x_all, mean, deviation = canvas[:4]
+    scaled = weights * deviation[None]
+    y_part = matmul(narrow(jnp.sum(scaled, axis=1)), narrow(y_all))
+    x_part = matmul(narrow(jnp.sum(scaled, axis=2)), narrow(x_all))
+    color_part = jnp.stack(
+        [jnp.sum(scaled * colors[j][None], axis=(1, 2)) for j in range(colors.shape[0])], axis=1
+    )
+    middle = jnp.sum(scaled * mean[None], axis=(1, 2))
+    return join_channels(color_part, y_part, x_part) - middle[:, None]
 
 
 def mlp_forward(row_values, gain, offset, w_in, b_in, w_out, b_out):
@@ -124,16 +171,6 @@
         (d_w_in, d_w_out),
         (d_gain, d_offset, d_b_in, d_b_out),
         (pre_low, grad_low),
-    )
-
-
-def combine_parts(mixed_parts, peak_parts, total_parts):
-    best_score = jnp.max(peak_parts, axis=0)
-    factor = jnp.exp(peak_parts - best_score[None])
-    return (
-        jnp.sum(mixed_parts * factor[..., None], axis=0),
-        best_score,
-        jnp.sum(total_parts * factor, axis=0),
     )
 
 
@@ -181,66 +218,35 @@
     latent_state = to_float(latents)
     normed_q = narrow(layer_norm(latent_state, g_cross[0], b_cross[0]))
     query_rows = narrow(matmul(normed_q, cross_matrices[0]) + b_cross[2])
-    queries = lax.all_gather(query_rows, ("rows", "cols"), axis=0, tiled=True).reshape(
-        image_count, LATENTS, model_width
-    )
-    colors = jnp.transpose(pixel_colors, (1, 0, 2, 3))
+    colors_low = lax.all_gather(pixel_colors, ("rows", "cols"), axis=0, tiled=False)
+    colors_low = lax.dynamic_index_in_dim(colors_low, row_place, axis=2, keepdims=False)
+    colors_low = colors_low.reshape(grid_rows, grid_cols, 3, tile_rows, tile_cols)
+    colors = to_float(
+        jnp.transpose(colors_low, (2, 1, 4, 0, 3)).reshape(
+            3, grid_cols * tile_cols, grid_rows * tile_rows
+        )
+    )
+    image_box = lax.dynamic_index_in_dim(image_boxes, row_place, axis=0, keepdims=False)
+    canvas = canvas_of(colors, image_box)
+    mean, deviation, row_in, col_in = canvas[2:]
+    inside = (col_in[:, None] & row_in[None, :])[None]
     key_weight = input_matrices[0]
     value_weight = input_matrices[1]
-
-    def image_inputs(color_image, image_box):
-        features, inside = pixel_features(color_image, image_box, row_start, col_start)
-        normed = narrow(layer_norm(features, g_input, b_input))
-        keys_here = narrow(matmul(normed, key_weight))
-        values_here = narrow(matmul(normed, value_weight) + b_cross[3])
-        return (features, inside, normed, keys_here, values_here)
-
-    def forward_image(unused_carry, image_items):
-        features, inside, normed, keys_here, values_here = image_inputs(
-            image_items[0], image_items[1]
-        )
-        scores = jnp.where(
-            inside[None, :], inner_right(image_items[2], keys_here) * score_scale, NEG
-        )
-        peak_score = jnp.max(scores, axis=1)
-        weights = jnp.where(inside[None, :], jnp.exp(scores - peak_score[:, None]), 0.0)
-        return (
-            unused_carry,
-            (matmul(narrow(weights), values_here), peak_score, jnp.sum(weights, axis=1)),
-        )
-
-    final_carry, image_parts = lax.scan(
-        forward_image, jnp.zeros((), jnp.float32), (colors, image_boxes, queries)
-    )
-    partial_mixed = image_parts[0].reshape(1, all_rows, model_width)
-    partial_peak = image_parts[1].reshape(1, all_rows)
-    partial_total = image_parts[2].reshape(1, all_rows)
-    mixed_parts, peak_parts, total_parts = (
-        lax.all_to_all(
-            partial_mixed.astype(jnp.bfloat16),
-            ("rows", "cols"),
-            split_axis=1,
-            concat_axis=0,
-            tiled=True,
-        ).astype(partial_mixed.dtype),
-        lax.all_to_all(
-            partial_peak.astype(jnp.bfloat16),
-            ("rows", "cols"),
-            split_axis=1,
-            concat_axis=0,
-            tiled=True,
-        ).astype(partial_peak.dtype),
-        lax.all_to_all(
-            partial_total.astype(jnp.bfloat16),
-            ("rows", "cols"),
-            split_axis=1,
-            concat_axis=0,
-            tiled=True,
-        ).astype(partial_total.dtype),
-    )
-    mixed_sum, best_score, total_sum = combine_parts(mixed_parts, peak_parts, total_parts)
-    attended = mixed_sum / total_sum[:, None]
-    log_total = best_score + jnp.log(total_sum)
+    query_inputs = inner_right(query_rows, key_weight)
+    query_lines = against_pixels(query_inputs * g_input, colors, canvas)
+    query_shift = jnp.sum(query_inputs * b_input, axis=1)
+    scores = jnp.where(
+        inside, (query_lines + query_shift[:, None, None]) * score_scale, NEG
+    )
+    peak_score = jnp.max(scores, axis=(1, 2), keepdims=True)
+    weights = jnp.where(inside, jnp.exp(scores - peak_score), 0.0)
+    cross_probs = weights / jnp.sum(weights, axis=(1, 2), keepdims=True)
+    plain_mixed = over_pixels(cross_probs, colors, canvas)
+    mixed_inputs = (
+        plain_mixed * g_input + jnp.sum(cross_probs, axis=(1, 2))[:, None] * b_input
+    )
+    mixed_low = narrow(mixed_inputs)
+    attended = matmul(mixed_low, value_weight) + b_cross[3]
     attended_low = narrow(attended)
     first = latent_state + matmul(attended_low, cross_out) + b_cross[4]
     branch, cross_stored = mlp_forward(
@@ -348,104 +354,131 @@
     d_cross_out = inner_left(attended_low, cross_out_low)
     d_cross_out_bias = jnp.sum(gradient, axis=0)
     d_attended = narrow(inner_right(cross_out_low, cross_out))
-    row_delta = jnp.sum(to_float(d_attended) * attended, axis=1)
-    d_attended_all = lax.all_gather(d_attended, ("rows", "cols"), axis=0, tiled=True).reshape(
-        image_count, LATENTS, model_width
-    )
-    log_total_all, delta_all = (
-        lax.all_gather(log_total, ("rows", "cols"), axis=0, tiled=True),
-        lax.all_gather(row_delta, ("rows", "cols"), axis=0, tiled=True),
-    )
-
-    def backward_image(sums, image_items):
-        color_image, image_box, query_image, d_out_image, log_image, delta_image = image_items
-        features, inside, normed, keys_here, values_here = image_inputs(color_image, image_box)
-        scores = jnp.where(inside[None, :], inner_right(query_image, keys_here) * score_scale, NEG)
-        weights = jnp.where(inside[None, :], jnp.exp(scores - log_image[:, None]), 0.0)
-        d_weights = inner_right(d_out_image, values_here)
-        d_values_here = inner_left(narrow(weights), d_out_image)
-        d_scores_here = narrow(weights * (d_weights - delta_image[:, None]) * score_scale)
-        d_query_part = matmul(d_scores_here, keys_here)
-        d_keys_low = narrow(inner_left(d_scores_here, query_image))
-        d_values_low = narrow(d_values_here)
-        d_normed = inner_right(d_keys_low, key_weight) + inner_right(d_values_low, value_weight)
-        d_features, d_gain_part, d_bias_part = norm_back(features, g_input, b_input, d_normed)
-        new_sums = (
-            sums[0] + inner_left(normed, d_keys_low),
-            sums[1] + inner_left(normed, d_values_low),
-            sums[2] + jnp.sum(d_values_here, axis=0),
-            sums[3] + d_gain_part,
-            sums[4] + d_bias_part,
-        )
-        return (new_sums, (d_query_part, jnp.transpose(d_features[:, :3])))
-
-    start_sums = (
-        jnp.zeros((input_width, model_width), jnp.float32),
-        jnp.zeros((input_width, model_width), jnp.float32),
-        jnp.zeros((model_width,), jnp.float32),
-        jnp.zeros((input_width,), jnp.float32),
-        jnp.zeros((input_width,), jnp.float32),
-    )
-    pixel_sums, image_grads = lax.scan(
-        backward_image,
-        start_sums,
-        (
-            colors,
-            image_boxes,
-            queries,
-            d_attended_all,
-            log_total_all.reshape(image_count, LATENTS),
-            delta_all.reshape(image_count, LATENTS),
-        ),
-    )
-    d_query_rows = lax.psum_scatter(
-        image_grads[0].reshape(all_rows, model_width),
-        ("rows", "cols"),
-        scatter_dimension=0,
-        tiled=True,
-    )
-    color_grad = jnp.transpose(
-        image_grads[1].reshape(image_count, 3, tile_rows, tile_cols), (1, 0, 2, 3)
-    )
+    value_shift = jnp.sum(to_float(d_attended) * b_cross[3], axis=1)
+    row_delta = jnp.sum(to_float(d_attended) * attended, axis=1) - value_shift
+    grad_inputs = inner_right(d_attended, value_weight)
+    grad_shift = jnp.sum(grad_inputs * b_input, axis=1)
+    grad_lines = against_pixels(grad_inputs * g_input, colors, canvas)
+    d_scores = (
+        cross_probs * (grad_lines + (grad_shift - row_delta)[:, None, None]) * score_scale
+    )
+    plain_scores = over_pixels(d_scores, colors, canvas)
+    score_sum = jnp.sum(d_scores, axis=(1, 2))
+    prob_sum = jnp.sum(cross_probs, axis=(1, 2))
+    score_inputs = plain_scores * g_input + score_sum[:, None] * b_input
+    score_low = narrow(score_inputs)
+    d_query_rows = matmul(score_low, key_weight)
+    in_gain_part = jnp.sum(query_inputs * plain_scores + grad_inputs * plain_mixed, axis=0)
+    in_bias_part = jnp.sum(
+        query_inputs * score_sum[:, None] + grad_inputs * prob_sum[:, None], axis=0
+    )
+    query_scaled = query_inputs * g_input
+    grad_scaled = grad_inputs * g_input
+    query_away = query_scaled[:, :3] - jnp.mean(query_scaled, axis=1, keepdims=True)
+    grad_away = grad_scaled[:, :3] - jnp.mean(grad_scaled, axis=1, keepdims=True)
+    along = jnp.sum(d_scores * query_lines + cross_probs * grad_lines, axis=0) / input_width
+    color_parts = jnp.einsum(
+        "rj,rcy->jcy", query_away, d_scores, precision=lax.Precision.HIGHEST
+    ) + jnp.einsum("rj,rcy->jcy", grad_away, cross_probs, precision=lax.Precision.HIGHEST)
+    color_parts = deviation[None] * (
+        color_parts - (colors - mean[None]) * deviation[None] * along[None]
+    )
+    color_parts = color_parts.reshape(3, grid_cols, tile_cols, grid_rows, tile_rows)
+    color_parts = jnp.transpose(color_parts, (3, 1, 0, 4, 2)).reshape(
+        grid_rows * grid_cols, 3, tile_rows, tile_cols
+    )
+    color_grad = lax.all_to_all(
+        color_parts, ("rows", "cols"), split_axis=0, concat_axis=0, tiled=True
+    ).reshape(image_count, grid_cols, 3, tile_rows, tile_cols)
+    color_grad = jnp.transpose(jnp.sum(color_grad, axis=1), (1, 0, 2, 3))
     query_low = narrow(d_query_rows)
     d_latent, d_cross_gain, d_cross_bias = norm_back(
         latent_state, g_cross[0], b_cross[0], inner_right(query_low, cross_matrices[0])
     )
     latent_grad = gradient + d_latent
-    in_gain_grad, in_bias_grad = lax.psum((pixel_sums[3], pixel_sums[4]), ("rows", "cols"))
-    input_mat_grad = jnp.stack([pixel_sums[0], pixel_sums[1]])
-    cross_gain_grad = jnp.stack([d_cross_gain, cross_mlp_v[0]])
-    cross_bias_grad = jnp.stack(
+    in_gain_grad, in_bias_grad = lax.psum((in_gain_part, in_bias_part), ("rows", "cols"))
+    vectors = jnp.stack(
         [
+            d_cross_gain,
+            cross_mlp_v[0],
             d_cross_bias,
             cross_mlp_v[1],
             jnp.sum(d_query_rows, axis=0),
-            pixel_sums[2],
+            jnp.sum(to_float(d_attended), axis=0),
             d_cross_out_bias,
             cross_mlp_v[2],
             cross_mlp_v[3],
+            d_self_gain,
+            tower_mlp_v[0],
+            d_self_bias,
+            tower_mlp_v[1],
+            jnp.sum(d_query_heads, axis=0),
+            jnp.sum(d_tower_values, axis=0),
+            d_self_out_bias,
+            tower_mlp_v[2],
+            tower_mlp_v[3],
         ]
     )
-    cross_mat_grad = jnp.stack([inner_left(normed_q, query_low), cross_mlp_w[0], cross_mlp_w[1]])
-    self_mat_grad = jnp.stack(
+    vector_sums = lax.psum_scatter(vectors, ("rows", "cols"), scatter_dimension=1, tiled=True)
+    lefts = jnp.stack(
         [
-            inner_left(normed_t, tq_low),
-            inner_left(normed_t, tk_low),
-            inner_left(normed_t, tv_low),
-            tower_mlp_w[0],
-            tower_mlp_w[1],
+            normed_q,
+            cross_stored[0],
+            cross_stored[2],
+            attended_low,
+            normed_t,
+            tower_stored[0],
+            tower_stored[2],
+            tower_mixed,
         ]
     )
+    rights = jnp.stack(
+        [
+            query_low,
+            cross_lows[0],
+            cross_lows[1],
+            cross_out_low,
+            d_attended,
+            query_rows,
+            tq_low,
+            tk_low,
+            tv_low,
+            tower_lows[0],
+            tower_lows[1],
+            tower_out_low,
+        ]
+    )
+    small_lefts = jnp.stack([mixed_low, score_low])
+    lefts = lax.all_gather(lefts, "cols", axis=1, tiled=True)
+    small_lefts = lax.all_gather(small_lefts, "cols", axis=1, tiled=True)
+    own = model_width // (grid_rows * grid_cols)
+    rights = rights.reshape(rights.shape[0], rows_dev, grid_rows, grid_cols, own)
+    rights = lax.all_to_all(
+        jnp.transpose(rights, (3, 0, 1, 2, 4)), "cols", split_axis=0, concat_axis=0, tiled=False
+    )
+    rights = jnp.transpose(rights, (1, 0, 2, 3, 4)).reshape(
+        rights.shape[1], grid_cols * rows_dev, grid_rows * own
+    )
+    pairs = ((0, 0), (1, 1), (2, 2), (3, 3), (4, 6), (4, 7), (4, 8), (5, 9), (6, 10), (7, 11))
+    big = [inner_left(rights[k], lefts[i]).reshape(grid_rows, own, model_width) for i, k in pairs]
+    small = [
+        inner_left(rights[k], small_lefts[i]).reshape(grid_rows, own, input_width)
+        for i, k in ((1, 5), (0, 4))
+    ]
+    big = lax.psum_scatter(jnp.stack(big, axis=1), "rows", scatter_dimension=0, tiled=False)
+    small = lax.psum_scatter(jnp.stack(small, axis=1), "rows", scatter_dimension=0, tiled=False)
+    big = jnp.transpose(big, (0, 2, 1))
+    small = jnp.transpose(small, (0, 2, 1))
     all_sums = (
-        lax.psum_scatter(cross_mat_grad, ("rows", "cols"), scatter_dimension=2, tiled=True),
-        lax.psum_scatter(d_cross_out, ("rows", "cols"), scatter_dimension=1, tiled=True),
-        lax.psum_scatter(input_mat_grad, ("rows", "cols"), scatter_dimension=2, tiled=True),
-        lax.psum_scatter(cross_gain_grad, ("rows", "cols"), scatter_dimension=1, tiled=True),
-        lax.psum_scatter(cross_bias_grad, ("rows", "cols"), scatter_dimension=1, tiled=True),
-        lax.psum_scatter(self_mat_grad, ("rows", "cols"), scatter_dimension=2, tiled=True),
-        lax.psum_scatter(d_self_out, ("rows", "cols"), scatter_dimension=1, tiled=True),
-        lax.psum_scatter(self_gain_grad, ("rows", "cols"), scatter_dimension=1, tiled=True),
-        lax.psum_scatter(self_bias_grad, ("rows", "cols"), scatter_dimension=1, tiled=True),
+        big[:3],
+        big[3],
+        small,
+        vector_sums[:2],
+        vector_sums[2:9],
+        big[4:9],
+        big[9],
+        vector_sums[9:11],
+        vector_sums[11:],
     )
     cross_sums = all_sums[:5]
     self_sums = all_sums[5:]

time: 2490 us -> 749 us (0.30)
  waiting for transfers between devices: 1830 us -> 286 us
  matrix products: 211 us -> 115 us
  local copies, waits for them, and re-layouts: 179 us -> 125 us
  other arithmetic: 114 us -> 79.3 us
  loops' own time: 32.7 us -> 0 us
    reduce_scatter x5 -> x0, waiting for transfers between devices: 832 us -> none  [the longest x1 354 us: local(): lax.psum_scatter(self_mat_grad, ('rows', 'cols'), scatter_dimension=2, ti...]
    unnamed x23 -> x11, waiting for transfers between devices: 777 us -> 250 us
    all_to_all x3 -> x2, waiting for transfers between devices: 99.1 us -> 0.01 us  [the longest x1 0.01 us: local(): lax.all_to_all(jnp.transpose(rights, (3, 0, 1, 2, 4)), 'cols', split_axis...]
    all_gather x2 -> x1, waiting for transfers between devices: 79.7 us -> 0.01 us  [local(): lefts = lax.all_gather(lefts, 'cols', axis=1, tiled=True)]
    all_gather x0 -> x2, blocking collectives: none -> 60.6 us  [the longest x1 45.9 us: local(): lax.all_gather(pixel_colors, ('rows', 'cols'), axis=0, tiled=False)]
    dot_general x30 -> x16, matrix products: 78.8 us -> 33.4 us  [inner_right(): lax.dot_general(former, latter, (((1,), (1,)), ((), ())), preferred_eleme...]
    another operation x20 -> x4, local copies, waits for them, and re-layouts: 47.1 us -> 1.91 us  [the longest x1 1.57 us: local(): jnp.stack([normed_q, cross_stored[0], cross_stored[2], attended_low, norm...]
    unnamed x1 -> x0, blocking collectives: 39.8 us -> none
  transfers between devices with their start and end apart: 19 -> 9, of which waited for: 18 -> 6; matrix products, arithmetic and copies ran while one was open for 8% -> 28% of each run, Pallas kernels for 0% -> 0%
where the time goes in v1:
time: 749 us; the launch traced here: 737 us
  waiting for transfers between devices  286 us (38%)
  local copies, waits for them, and re-layouts  125 us (17%)
  matrix products  115 us (15%)
  blocking collectives  101 us (13%)
  other arithmetic  79.3 us (11%)
  between operations  20.8 us (3%)
  starting transfers between devices  9.23 us (1%)
    unnamed x11, waiting for transfers between devices  250 us
    all_gather x1, blocking collectives, local(): lax.all_gather(pixel_colors, ('rows', 'cols'), axis=0, tiled=False)  45.9 us
    unnamed x313, local copies, waits for them, and re-layouts  41.7 us
    psum x1, blocking collectives, local(): lax.psum((in_gain_part, in_bias_part), ('rows', 'cols'))  40.6 us
    dot_general x16, matrix products, inner_right(): lax.dot_general(former, latter, (((1,), (1,)), ((), ())), preferred_eleme...  33.4 us
    dot_general x16, matrix products, matmul(): return jnp.dot(former, latter, preferred_element_type=jnp.float32)  26.9 us
    all_gather x1, waiting for transfers between devices, local(): lax.all_gather(tower_values, 'cols', axis=0, tiled=True)  22 us
    dot_general x12, matrix products, inner_left(): lax.dot_general(former, latter, (((0,), (0,)), ((), ())), preferred_eleme...  18.4 us
  transfers between devices with their start and end apart: 9, of which 6 were waited for; matrix products, arithmetic and copies ran while one was open for 28% of the time, Pallas kernels for 0%

profile of v1, /device:TPU:0, one launch (start us, length us, event | category | flops | bytes accessed | tf_op | source)
XLA Modules:
  0.0 736.7 jit_solution(11118078193869560509)
XLA Ops:
  16.6 45.9 %all-gather = bf16[96,4,72,9]{2,1,3,0:T(4,128)(2,1)S(1)} all-gather(bf16[3,4,72,9]{2,1,3,0:T(4,128)(2,1)} %param.19), channel_id=2, replica_groups=mesh['rows'=4,'cols'=8] {'rows','cols'}, dimensions={0}, use_global_device_ids=true | all-gather | bytes 513216 | tf_op jit(solution)/shard_map/all_gather | solution.py:221
  69.1 4.0 fusion.289
  74.1 2.1 fusion.127
  94.6 4.2 fusion.55
  98.8 5.7 fusion.5
  104.5 10.5 %multiply_reduce_fusion.4 = (f32[64]{0:T(128)S(1)}, f32[64]{0:T(128)S(1)}, f32[64]{0:T(128)S(1)}, bf16[64,72]{0,1:T(8,128)(2,1)S(1)}, bf16[64,288]{1,0:T(8,128)(2,1)S(1)}, /*index=5*/f32[64]{0:T(128)S(1)}, f32[64]{0:T(128)S(1)}) fusion(f32[72,288]{1,0:T(8,128)S(1)} %add_rsqrt_fusion, f32[72,288]{1,0:T(8,128)S(1)} %get-tuple-element.123, f32[64]{0:T(128)S(1)} %fusion.5, ...), kind=kLoop, calls=%fused_computation.9 | loop fusion | flops 37135552 | bytes 576768 | tf_op jit(solution)/shard_map/reduce_sum | solution.py:148
  122.1 2.8 bitcast_dynamic-update-slice_fusion.4
  125.7 2.2 fusion.308
  129.4 2.8 fusion.130
  132.3 2.7 fusion.124
  135.3 2.2 fusion.133
  137.5 14.5 %all-gather.7.cloned.1.call-done = bf16[512,1024]{1,0:T(8,128)(2,1)} async-done(((bf16[64,1024]{1,0:T(8,128)(2,1)}), bf16[512,1024]{1,0:T(8,128)(2,1)}) %all-gather.7.cloned.1.call-update) | async-done | bytes 1048592 | tf_op jit(solution)/shard_map/all_gather | solution.py:261
  156.0 22.0 %all-gather.5.cloned.1.call-done = bf16[512,1024]{1,0:T(8,128)(2,1)} async-done(((bf16[64,1024]{1,0:T(8,128)(2,1)}), bf16[512,1024]{1,0:T(8,128)(2,1)}) %all-gather.5.cloned.1.call-update) | async-done | bytes 1048592 | tf_op jit(solution)/shard_map/all_gather | solution.py:262
  178.0 3.7 convolution_convert_fusion.4
  181.7 2.3 fusion.310
  185.8 2.9 bitcast_dynamic-update-slice_fusion
  188.7 3.2 fusion.292
  191.9 3.0 multiply_reduce_fusion.15
  198.3 5.9 convolution_convert_fusion.1
  204.2 2.3 copy.623
  206.5 3.8 convolution_convert_fusion
  210.3 2.3 copy.625
  221.1 7.3 concatenate.100
  231.9 6.4 fusion.293
  240.1 2.6 reduce-scatter.16.cloned.1.call-done
  242.7 2.4 fusion.15
  245.1 3.1 fusion.104
  248.2 33.5 %reduce-scatter.18.cloned.1.call-done = bf16[64,1024]{1,0:T(8,128)(2,1)} async-done(((bf16[512,1024]{1,0:T(8,128)(2,1)}), bf16[64,1024]{1,0:T(8,128)(2,1)}) %reduce-scatter.18.cloned.1.call-update) | async-done | bytes 131088
  281.8 3.0 multiply_reduce_fusion.16
  290.5 4.0 fusion.294
  296.2 3.0 multiply_reduce_fusion.17
  303.8 2.9 convert_reduce_fusion.1
  308.5 2.3 fusion.283
  311.5 12.6 %add_reduce_fusion = (f32[72,288]{1,0:T(8,128)}, f32[64,72,288]{2,0,1:T(8,128)S(1)}) fusion(f32[64]{0:T(128)S(1)} %reduce_sum.789, f32[64]{0:T(128)S(1)} %get-tuple-element.165, f32[64]{0:T(128)S(1)} %get-tuple-element.166, f32[64]{0:T(128)S(1)} %get-tuple-element.164, f32[64,72]{0,1:T(8,128)S(1)} %fusion.236, f32[64,288]{1,0:T(8,128)S(1)} %fusion.230, ...), kind=kLoop, calls=%fused_computation.2 | loop fusion | flops 43773696 | bytes 6014208 | tf_op jit(solution)/shard_map/reduce_sum | solution.py:379
  324.0 2.9 copy-done.2
  327.0 5.3 multiply_reduce_fusion
  345.6 4.4 reshape.1158
  350.1 4.3 all-to-all-start.1
  354.5 4.0 concatenate.110
  360.9 2.5 fusion.280
  366.1 14.7 %all_gather.23 = bf16[2,512,261]{2,0,1:T(2,128)(2,1)S(1)} all-gather(bf16[2,64,261]{2,0,1:T(2,128)(2,1)S(1)} %copy.605), channel_id=1, replica_groups=mesh['rows'=4,'cols'=8] {'cols'}, dimensions={1}, use_global_device_ids=true | all-gather | bytes 601344 | tf_op jit(solution)/shard_map/all_gather | solution.py:453
  381.9 1.9 copy.638
  383.8 1.9 copy.639
  385.8 5.5 reshape.1159
  391.8 1.8 fusion.288
  395.7 1.8 copy.607
  399.4 1.8 copy.603
  401.2 1.8 squeeze.158
  403.9 1.8 squeeze.156
  412.3 2.5 fusion.73
  414.8 2.8 fusion.72
  417.5 2.4 fusion.71
  419.9 2.3 fusion.70
  422.2 2.3 fusion.69
  431.7 2.9 fusion.118
  434.8 9.0 %fusion.252 = f32[3,72,288]{2,0,1:T(4,128)S(1)} fusion(f32[64,261]{0,1:T(8,128)} %copy-done.44, f32[64]{0:T(128)S(1)} %broadcast_multiply_fusion.4, f32[64]{0:T(128)S(1)} %copy-done.129, f32[64]{0:T(128)S(1)} %copy-done.126, pred[72,288]{1,0:T(8,128)(4,1)S(1)} %copy-done.60, f32[64]{0:T(128)S(1)} %copy-done.86, f32[72,288]{1,0:T(8,128)S(1)} %copy-done.18, ...), kind=kOutput, calls=%fused_computation.354 | convolution fusion | flops 69009600 | bytes 780544 | tf_op jit(solution)/shard_map/rj,rcy->jcy/dot_general | solution.py:382
  443.9 4.4 fusion.80
  452.1 4.6 all-to-all-start
  456.8 1.8 add_add_fusion.4
  459.8 40.6 %all-reduce.2 = (f32[261]{0:T(512)}, f32[261]{0:T(512)}) all-reduce(f32[261]{0:T(512)S(1)} %get-tuple-element.95, f32[261]{0:T(512)S(1)} %get-tuple-element.94), channel_id=1, replica_groups=mesh['rows'=4,'cols'=8] {'rows','cols'}, use_global_device_ids=true, to_apply=%region_56.57 | all-reduce | flops 522 | bytes 4176 | tf_op jit(solution)/shard_map/psum | solution.py:399
  500.4 19.6 %reduce-scatter.20.cloned.1.call-done = f32[32,18]{1,0:T(8,128)} async-done(((f32[1024,18]{1,0:T(8,128)}), f32[32,18]{1,0:T(8,128)}) %reduce-scatter.20.cloned.1.call-update) | async-done | bytes 2320
  527.4 193.7 %all-reduce.6.cloned.1.call-done = (f32[4,10,32,1024]{3,2,0,1:T(8,128)}, f32[4,2,32,261]{3,2,0,1:T(8,128)}) async-done(((f32[4,10,32,1024]{3,2,0,1:T(8,128)}, f32[4,2,32,261]{3,2,0,1:T(8,128)}), (f32[4,10,32,1024]{3,2,0,1:T(8,128)}, f32[4,2,32,261]{3,2,0,1:T(8,128)})) %all-reduce.6.cloned.1.call-update) | async-done | bytes 5510160
  721.2 2.1 dynamic-slice_bitcast_fusion
  727.2 2.2 bitcast_add_fusion
  (502 shorter events, 131.9 us)
Async XLA Ops:
  7.2 113.4 %copy-start = (bf16[1024,1024]{1,0:T(8,128)(2,1)S(1)}, bf16[1024,1024]{1,0:T(8,128)(2,1)}, u32[]{:S(2)}) copy-start(bf16[1024,1024]{1,0:T(8,128)(2,1)} %param.23) | copy-start | bytes 6291460
  7.2 66.0 %copy-start.5 = (bf16[64,1024]{1,0:T(8,128)(2,1)S(1)}, bf16[64,1024]{1,0:T(8,128)(2,1)}, u32[]{:S(2)}) copy-start(bf16[64,1024]{1,0:T(8,128)(2,1)} %param.18) | copy-start | bytes 393220
  7.2 144.8 %all-gather.7.cloned.1.call-start = ((), (), s32[]{:S(2)}) async-start(), calls=%async_computation.6 | async-start | bytes 1179648 | tf_op jit(solution)/shard_map/all_gather | solution.py:261
  63.0 35.7 %copy-start.11 = (f32[3,8,9,4,72]{4,1,3,2,0:T(8,128)}, f32[3,8,9,4,72]{4,1,3,2,0:T(8,128)S(1)}, u32[]{:S(2)}) copy-start(f32[3,8,9,4,72]{4,1,3,2,0:T(8,128)S(1)} %convert_bitcast_fusion) | copy-start | bytes 746500
  65.4 16.4 %copy-start.82 = (f32[64]{0:T(128)}, f32[64]{0:T(128)S(1)}, u32[]{:S(2)}) copy-start(f32[64]{0:T(128)S(1)} %fusion.263) | copy-start | bytes 772
  74.1 42.5 %copy-start.74 = (bf16[2,1024]{1,0:T(2,128)(2,1)S(1)}, bf16[2,1024]{1,0:T(2,128)(2,1)}, u32[]{:S(2)}) copy-start(bf16[2,1024]{1,0:T(2,128)(2,1)} %param.31) | copy-start | bytes 12292
  74.1 43.1 %copy-start.67 = (bf16[7,1024]{1,0:T(8,128)(2,1)S(1)}, bf16[7,1024]{1,0:T(8,128)(2,1)}, u32[]{:S(2)}) copy-start(bf16[7,1024]{1,0:T(8,128)(2,1)} %param.32) | copy-start | bytes 43012
  77.3 38.7 %copy-start.85 = (f32[64]{0:T(128)}, f32[64]{0:T(128)S(1)}, u32[]{:S(2)}) copy-start(f32[64]{0:T(128)S(1)} %get-tuple-element.170) | copy-start | bytes 772
  83.2 240.8 %copy-start.9 = (f32[72,288]{1,0:T(8,128)}, f32[72,288]{1,0:T(8,128)S(1)}, u32[]{:S(2)}) copy-start(f32[72,288]{1,0:T(8,128)S(1)} %get-tuple-element.123) | copy-start | bytes 248836
  83.3 37.1 %copy-start.17 = (f32[72,288]{1,0:T(8,128)}, f32[72,288]{1,0:T(8,128)S(1)}, u32[]{:S(2)}) copy-start(f32[72,288]{1,0:T(8,128)S(1)} %add_rsqrt_fusion) | copy-start | bytes 248836
  85.8 39.1 %copy-start.19 = (f32[72,288]{1,0:T(8,128)}, f32[72,288]{1,0:T(8,128)S(1)}, u32[]{:S(2)}) copy-start(f32[72,288]{1,0:T(8,128)S(1)} %mul.868) | copy-start | bytes 248836
  88.5 36.5 %copy-start.22 = (f32[72,288]{1,0:T(8,128)}, f32[72,288]{1,0:T(8,128)S(1)}, u32[]{:S(2)}) copy-start(f32[72,288]{1,0:T(8,128)S(1)} %mul.878) | copy-start | bytes 248836
  90.3 34.7 %copy-start.25 = (f32[72,288]{1,0:T(8,128)}, f32[72,288]{1,0:T(8,128)S(1)}, u32[]{:S(2)}) copy-start(f32[72,288]{1,0:T(8,128)S(1)} %mul.873) | copy-start | bytes 248836
  91.1 33.9 %copy-start.98 = (f32[64]{0:T(128)}, f32[64]{0:T(128)S(1)}, u32[]{:S(2)}) copy-start(f32[64]{0:T(128)S(1)} %get-tuple-element.167) | copy-start | bytes 772
  91.1 33.9 %copy-start.100 = (f32[64]{0:T(128)}, f32[64]{0:T(128)S(1)}, u32[]{:S(2)}) copy-start(f32[64]{0:T(128)S(1)} %get-tuple-element.168) | copy-start | bytes 772
  91.1 33.9 %copy-start.102 = (f32[64]{0:T(128)}, f32[64]{0:T(128)S(1)}, u32[]{:S(2)}) copy-start(f32[64]{0:T(128)S(1)} %get-tuple-element.169) | copy-start | bytes 772
  92.0 24.6 %copy-start.95 = (f32[64]{0:T(128)}, f32[64]{0:T(128)S(1)}, u32[]{:S(2)}) copy-start(f32[64]{0:T(128)S(1)} %reduce_sum.657) | copy-start | bytes 772
  92.8 25.0 %copy-start.59 = (pred[72,288]{1,0:T(8,128)(4,1)}, pred[72,288]{1,0:T(8,128)(4,1)S(1)}, u32[]{:S(2)}) copy-start(pred[72,288]{1,0:T(8,128)(4,1)S(1)} %broadcast_and_fusion) | copy-start | bytes 62212
  93.7 24.2 %copy-start.61 = (f32[64,72]{0,1:T(8,128)}, f32[64,72]{0,1:T(8,128)S(1)}, u32[]{:S(2)}) copy-start(f32[64,72]{0,1:T(8,128)S(1)} %fusion.224) | copy-start | bytes 55300
  94.6 23.3 %copy-start.42 = (f32[64,288]{1,0:T(8,128)}, f32[64,288]{1,0:T(8,128)S(1)}, u32[]{:S(2)}) copy-start(f32[64,288]{1,0:T(8,128)S(1)} %fusion.218) | copy-start | bytes 221188
  98.8 27.0 %copy-start.125 = (f32[64]{0:T(128)}, f32[64]{0:T(128)S(1)}, u32[]{:S(2)}) copy-start(f32[64]{0:T(128)S(1)} %fusion.55) | copy-start | bytes 772
  98.8 27.0 %copy-start.106 = (f32[1,1024]{1,0:T(1,128)S(1)}, f32[1,1024]{1,0:T(1,128)}, u32[]{:S(2)}) copy-start(f32[1,1024]{1,0:T(1,128)} %get-tuple-element.220) | copy-start | bytes 12292
  104.5 23.4 %copy-start.128 = (f32[64]{0:T(128)}, f32[64]{0:T(128)S(1)}, u32[]{:S(2)}) copy-start(f32[64]{0:T(128)S(1)} %fusion.5) | copy-start | bytes 772
  115.1 17.1 %copy-start.122 = (f32[64]{0:T(128)}, f32[64]{0:T(128)S(1)}, u32[]{:S(2)}) copy-start(f32[64]{0:T(128)S(1)} %get-tuple-element.82) | copy-start | bytes 772
  115.1 17.1 %copy-start.123 = (f32[64]{0:T(128)}, f32[64]{0:T(128)S(1)}, u32[]{:S(2)}) copy-start(f32[64]{0:T(128)S(1)} %get-tuple-element.83) | copy-start | bytes 772
  121.1 16.4 %copy-start.87 = (f32[64]{0:T(128)}, f32[64]{0:T(128)S(1)}, u32[]{:S(2)}) copy-start(f32[64]{0:T(128)S(1)} %broadcast_multiply_fusion.9) | copy-start | bytes 772
  128.0 53.7 %copy-start.97 = (f32[64]{0:T(128)}, f32[64]{0:T(128)S(1)}, u32[]{:S(2)}) copy-start(f32[64]{0:T(128)S(1)} %broadcast_multiply_fusion.8) | copy-start | bytes 772
  132.2 45.7 %all-gather.5.cloned.1.call-start = ((), (), s32[]{:S(2)}) async-start(), calls=%async_computation.5 | async-start | bytes 1179648 | tf_op jit(solution)/shard_map/all_gather | solution.py:262
  135.0 107.6 %reduce-scatter.16.cloned.1.call-start = ((), (), s32[]{:S(2)}) async-start(), calls=%async_computation.8 | async-start | bytes 1179648
  135.3 46.4 %copy-start.58 = (pred[64,512]{1,0:T(8,128)(4,1)}, pred[64,512]{1,0:T(8,128)(4,1)S(1)}, u32[]{:S(2)}) copy-start(pred[64,512]{1,0:T(8,128)(4,1)S(1)} %broadcast_compare_fusion) | copy-start | bytes 98308
  137.5 44.2 %copy-start.64 = (bf16[8,8,8,128]{3,2,1,0:T(8,128)(2,1)}, bf16[8,8,8,128]{3,2,1,0:T(8,128)(2,1)S(1)}, u32[]{:S(2)}) copy-start(bf16[8,8,8,128]{3,2,1,0:T(8,128)(2,1)S(1)} %fusion.133) | copy-start | bytes 393220
  156.0 25.7 %copy-start.104 = (f32[8,64]{1,0:T(8,128)}, f32[8,64]{1,0:T(8,128)S(1)}, u32[]{:S(2)}) copy-start(f32[8,64]{1,0:T(8,128)S(1)} %get-tuple-element.246) | copy-start | bytes 6148
  206.5 75.3 %reduce-scatter.18.cloned.1.call-start = ((), (), s32[]{:S(2)}) async-start(), calls=%async_computation.9 | async-start | bytes 1179648
  212.6 199.6 %all-gather.9.cloned.1.call-start = ((), (), s32[]{:S(2)}) async-start(), calls=%async_computation.7 | async-start | bytes 9437184 | tf_op jit(solution)/shard_map/all_gather | solution.py:452
  301.4 30.9 %copy-start.14 = (f32[64,1024]{1,0:T(8,128)}, f32[64,1024]{1,0:T(8,128)S(1)}, u32[]{:S(2)}) copy-start(f32[64,1024]{1,0:T(8,128)S(1)} %get-tuple-element.117) | copy-start | bytes 786436
  301.4 25.6 %copy-start.20 = (f32[72,288]{1,0:T(8,128)S(1)}, f32[72,288]{1,0:T(8,128)}, u32[]{:S(2)}) copy-start(f32[72,288]{1,0:T(8,128)} %copy-done.19) | copy-start | bytes 248836
  301.4 25.6 %copy-start.23 = (f32[72,288]{1,0:T(8,128)S(1)}, f32[72,288]{1,0:T(8,128)}, u32[]{:S(2)}) copy-start(f32[72,288]{1,0:T(8,128)} %copy-done.22) | copy-start | bytes 248836
  306.8 20.2 %copy-start.26 = (f32[72,288]{1,0:T(8,128)S(1)}, f32[72,288]{1,0:T(8,128)}, u32[]{:S(2)}) copy-start(f32[72,288]{1,0:T(8,128)} %copy-done.25) | copy-start | bytes 248836
  310.9 16.1 %copy-start.56 = (f32[72,288]{1,0:T(8,128)S(1)}, f32[72,288]{1,0:T(8,128)}, u32[]{:S(2)}) copy-start(f32[72,288]{1,0:T(8,128)} %get-tuple-element.122) | copy-start | bytes 248836
  311.5 24.2 %copy-start.7 = (bf16[1,261,1024]{2,0,1:T(2,128)(2,1)S(1)}, bf16[1,261,1024]{2,0,1:T(2,128)(2,1)}, u32[]{:S(2)}) copy-start(bf16[1,261,1024]{2,0,1:T(2,128)(2,1)} %copy-done.6) | copy-start | bytes 1603588
  324.0 19.1 %copy-start.39 = (bf16[64,1024]{0,1:T(8,128)(2,1)S(1)}, bf16[64,1024]{0,1:T(8,128)(2,1)}, u32[]{:S(2)}) copy-start(bf16[64,1024]{0,1:T(8,128)(2,1)} %copy.587) | copy-start | bytes 393220
  327.0 17.3 %copy-start.41 = (bf16[64,1024]{0,1:T(8,128)(2,1)S(1)}, bf16[64,1024]{0,1:T(8,128)(2,1)}, u32[]{:S(2)}) copy-start(bf16[64,1024]{0,1:T(8,128)(2,1)} %copy.589) | copy-start | bytes 393220
  327.0 17.4 %copy-start.38 = (bf16[64,1024]{0,1:T(8,128)(2,1)S(1)}, bf16[64,1024]{0,1:T(8,128)(2,1)}, u32[]{:S(2)}) copy-start(bf16[64,1024]{0,1:T(8,128)(2,1)} %copy.590) | copy-start | bytes 393220
  327.0 17.5 %copy-start.40 = (bf16[64,1024]{0,1:T(8,128)(2,1)S(1)}, bf16[64,1024]{0,1:T(8,128)(2,1)}, u32[]{:S(2)}) copy-start(bf16[64,1024]{0,1:T(8,128)(2,1)} %copy.591) | copy-start | bytes 393220
  350.1 35.7 %all-to-all-start.1 = ((bf16[8,2,49152]{2,1,0:T(2,128)(2,1)}), bf16[8,2,49152]{2,1,0:T(2,128)(2,1)}, u32[]{:S(2)}, u32[]{:S(2)}) async-start(bf16[8,2,49152]{2,1,0:T(2,128)(2,1)} %reshape.1158), calls=%async_computation.1 | async-start | bytes 3145728 | tf_op jit(solution)/shard_map/all_to_all | solution.py:456
  354.5 165.6 %reduce-scatter.20.cloned.1.call-start = ((), (), s32[]{:S(2)}) async-start(), calls=%async_computation.10 | async-start | bytes 540672
  385.8 335.4 %all-reduce.6.cloned.1.call-start = ((), (), s32[]{:S(2)}) async-start(), calls=%async_computation.11 | async-start | bytes 11272192
  393.7 17.2 %copy-start.34 = (bf16[1,512,261]{1,2,0:T(8,128)(2,1)S(1)}, bf16[1,512,261]{1,2,0:T(8,128)(2,1)}, u32[]{:S(2)}) copy-start(bf16[1,512,261]{1,2,0:T(8,128)(2,1)} %copy.638) | copy-start | bytes 801796
  393.7 17.5 %copy-start.35 = (bf16[1,512,261]{1,2,0:T(8,128)(2,1)S(1)}, bf16[1,512,261]{1,2,0:T(8,128)(2,1)}, u32[]{:S(2)}) copy-start(bf16[1,512,261]{1,2,0:T(8,128)(2,1)} %copy.639) | copy-start | bytes 801796
  409.3 15.3 %copy-start.54 = (bf16[512,128]{0,1:T(8,128)(2,1)S(1)}, bf16[512,128]{0,1:T(8,128)(2,1)}, u32[]{:S(2)}) copy-start(bf16[512,128]{0,1:T(8,128)(2,1)} %squeeze.152) | copy-start | bytes 393220
  410.1 15.6 %copy-start.53 = (bf16[512,128]{0,1:T(8,128)(2,1)S(1)}, bf16[512,128]{0,1:T(8,128)(2,1)}, u32[]{:S(2)}) copy-start(bf16[512,128]{0,1:T(8,128)(2,1)} %squeeze.153) | copy-start | bytes 393220
  410.7 16.2 %copy-start.52 = (bf16[512,128]{0,1:T(8,128)(2,1)S(1)}, bf16[512,128]{0,1:T(8,128)(2,1)}, u32[]{:S(2)}) copy-start(bf16[512,128]{0,1:T(8,128)(2,1)} %squeeze.154) | copy-start | bytes 393220
  411.5 16.5 %copy-start.51 = (bf16[512,128]{0,1:T(8,128)(2,1)S(1)}, bf16[512,128]{0,1:T(8,128)(2,1)}, u32[]{:S(2)}) copy-start(bf16[512,128]{0,1:T(8,128)(2,1)} %squeeze.156) | copy-start | bytes 393220
  443.8 14.9 %copy-start.29 = (f32[64,261]{0,1:T(8,128)S(1)}, f32[64,261]{0,1:T(8,128)}, u32[]{:S(2)}) copy-start(f32[64,261]{0,1:T(8,128)} %copy-done.28) | copy-start | bytes 200452
  443.8 14.9 %copy-start.31 = (f32[64,261]{0,1:T(8,128)S(1)}, f32[64,261]{0,1:T(8,128)}, u32[]{:S(2)}) copy-start(f32[64,261]{0,1:T(8,128)} %copy-done.30) | copy-start | bytes 200452
  443.8 14.8 %copy-start.45 = (f32[64,261]{0,1:T(8,128)S(1)}, f32[64,261]{0,1:T(8,128)}, u32[]{:S(2)}) copy-start(f32[64,261]{0,1:T(8,128)} %get-tuple-element.239) | copy-start | bytes 200452
  443.8 14.8 %copy-start.79 = (f32[64]{0:T(128)S(1)}, f32[64]{0:T(128)}, u32[]{:S(2)}) copy-start(f32[64]{0:T(128)} %copy-done.78) | copy-start | bytes 772
  443.8 14.8 %copy-start.81 = (f32[64]{0:T(128)S(1)}, f32[64]{0:T(128)}, u32[]{:S(2)}) copy-start(f32[64]{0:T(128)} %copy-done.80) | copy-start | bytes 772
  443.8 14.8 %copy-start.92 = (f32[64]{0:T(128)S(1)}, f32[64]{0:T(128)}, u32[]{:S(2)}) copy-start(f32[64]{0:T(128)} %copy-done.91) | copy-start | bytes 772
  443.9 14.8 %copy-start.94 = (f32[64]{0:T(128)S(1)}, f32[64]{0:T(128)}, u32[]{:S(2)}) copy-start(f32[64]{0:T(128)} %copy-done.93) | copy-start | bytes 772
  448.3 281.1 %copy-start.1 = (bf16[1024,1024]{1,0:T(8,128)(2,1)S(1)}, bf16[1024,1024]{1,0:T(8,128)(2,1)}, u32[]{:S(2)}) copy-start(bf16[1024,1024]{1,0:T(8,128)(2,1)} %param.23) | copy-start | bytes 6291460
  452.1 72.3 %all-to-all-start = ((f32[32,1,1944]{2,1,0:T(1,128)}), f32[32,1,1944]{2,1,0:T(1,128)S(1)}, u32[]{:S(2)}, u32[]{:S(2)}) async-start(f32[32,1,1944]{2,1,0:T(1,128)} %reshape.1156), calls=%async_computation | async-start | bytes 524288 | tf_op jit(solution)/shard_map/all_to_all | solution.py:390
  459.8 266.6 %copy-start.57 = (f32[3,1024,32]{1,2,0:T(8,128)S(1)}, f32[3,1024,32]{1,2,0:T(8,128)}, u32[]{:S(2)}) copy-start(f32[3,1024,32]{1,2,0:T(8,128)} %param.33) | copy-start | bytes 1179652
  459.8 267.4 %copy-start.66 = (f32[2,261,32]{1,2,0:T(8,128)S(1)}, f32[2,261,32]{1,2,0:T(8,128)}, u32[]{:S(2)}) copy-start(f32[2,261,32]{1,2,0:T(8,128)} %param.35) | copy-start | bytes 200452
  (86 other events, 736.6 us)
Sparse Core Ops, SparseCore 0:
  132.4 19.5 all-gather.6
  154.5 23.4 all-gather.4
  206.6 36.0 reduce-scatter.15
  245.7 36.0 reduce-scatter.17
  283.5 54.3 all-gather.8
  385.9 134.1 reduce-scatter.19
  523.2 197.9 all-reduce.5

commit v2 on v1

--- a/solution.py
+++ b/solution.py
@@ -1,6 +1,12 @@
+import functools
+
 import jax
 import jax.numpy as jnp
+import ml_dtypes
+import numpy as np
 from jax import lax
+from jax.experimental import pallas as pl
+from jax.experimental.pallas import tpu as pltpu
 from jax.sharding import PartitionSpec as P
 
 HEADS = 8
@@ -12,6 +18,7 @@
 EPS = 1e-05
 NEG = -1e30
 FREQ_TOP = 112.0
+VMEM_BYTES = 63 * 1024 * 1024
 
 
 def narrow(values):
@@ -500,6 +507,1062 @@
     )
 
 
+STEPS_HELD = 8
+LANES = 128
+MESH = pl.DeviceIdType.MESH
+WIDE = 3 * LANES
+
+
+def own_dot(former, latter, former_dim, latter_dim):
+    return lax.dot_general(
+        former,
+        latter,
+        (((former_dim,), (latter_dim,)), ((), ())),
+        preferred_element_type=jnp.float32,
+    )
+
+
+def selections(tile_cols, grid_cols, steps):
+    held = STEPS_HELD
+    blocks = -(-steps // held)
+    place = np.zeros((grid_cols * 32, WIDE), np.float32)
+    back = np.zeros((grid_cols * 32, blocks * LANES), np.float32)
+    for tile in range(grid_cols):
+        for channel in range(3):
+            for offset in range(tile_cols):
+                col = tile * tile_cols + offset
+                line = tile * 32 + channel * tile_cols + offset
+                place[line, channel * LANES + col] = 1
+                half, step = divmod(col, steps)
+                back[line, step * 16 + half * 8 + channel] = 1
+    pick = np.zeros((7 * LANES, blocks * LANES), np.float32)
+    for step in range(steps):
+        for half in range(2):
+            for slot, kind in enumerate((0, 1, 2, 3, 4, 3, 5, 6)):
+                pick[kind * LANES + half * steps + step, step * 16 + half * 8 + slot] = 1
+    spread = np.zeros((LANES, 2 * LANES), np.float32)
+    for group in range(16):
+        for channel in range(3):
+            for slot in (3, 4):
+                spread[group * 8 + slot, group * 8 + channel] = 1
+            for slot in (6, 7):
+                spread[group * 8 + slot, LANES + group * 8 + channel] = 1
+    low = lambda values: np.asarray(values, ml_dtypes.bfloat16)
+    return (low(place), low(pick), low(pick.T), low(spread), low(back))
+
+
+def norm_parts(values):
+    middle = jnp.mean(values, axis=1, keepdims=True)
+    centered = values - middle
+    spread = jnp.mean(centered * centered, axis=1, keepdims=True)
+    factor = lax.rsqrt(spread + EPS)
+    return (centered * factor, factor)
+
+
+def norm_forward(values, gain, offset):
+    return narrow(norm_parts(values)[0] * gain + offset)
+
+
+def norm_gradient(values, gain, gradient):
+    plain, factor = norm_parts(values)
+    inner = gradient * gain
+    first = jnp.mean(inner, axis=1, keepdims=True)
+    second = jnp.mean(inner * plain, axis=1, keepdims=True)
+    return (
+        factor * (inner - first - plain * second),
+        jnp.sum(gradient * plain, axis=0, keepdims=True),
+        jnp.sum(gradient, axis=0, keepdims=True),
+    )
+
+
+GELU_RATE = 0.7978845608028654
+GELU_CUBE = 0.044715
+
+
+def gelu_value(u):
+    return 0.5 * u * (1.0 + jnp.tanh(GELU_RATE * (u + GELU_CUBE * u * u * u)))
+
+
+def gelu_slope(u):
+    bent = jnp.tanh(GELU_RATE * (u + GELU_CUBE * u * u * u))
+    return 0.5 * (1.0 + bent) + 0.5 * u * (1.0 - bent * bent) * GELU_RATE * (
+        1.0 + 3.0 * GELU_CUBE * u * u
+    )
+
+
+def waves(turns):
+    near = turns - 2.0 * jnp.floor(turns * 0.5 + 0.5)
+    return (jnp.sin(jnp.pi * near), jnp.cos(jnp.pi * near))
+
+
+def axis_lines(place, slot):
+    lane = lax.broadcasted_iota(jnp.int32, (place.shape[0], LANES), 1)
+    band = lax.rem(lane, NBANDS)
+    frequency = 1.0 + to_float(band) * ((FREQ_TOP - 1.0) / (NBANDS - 1))
+    sine, cosine = waves(place * frequency)
+    return jnp.concatenate(
+        [jnp.where(lane < NBANDS, sine, cosine), jnp.where(lane == slot, place, 0.0)], axis=1
+    )
+
+
+def layer_kernel(
+    sizes,
+    boxes, latents, cotangent, color_tiles, input_gains, cross_gains, cross_biases, self_gains,
+    self_biases, place, pick, pick_t, spread, back, prior_cross, prior_out,
+    w_cross, w_out, w_self, w_self_out, w_input,
+    new_latents, latent_grad, color_out, cross_total, out_total, self_total, self_out_total,
+    input_parts, vector_out, input_vector_out,
+    wts, win, xbuf, xsmall, gsrc, gbuf, staged, arrived, staged_small, arrived_small,
+    colbuf, img, img7, fa, ft, sl, ycoef, xcoef, yfeat, xfeat, mixrow,
+    cgright, rowsum, colsum, cgacc, cgsend, cgbuf,
+    act, lnvec, lnbuf, biasvec, vecsend, vecbuf, ivec, ivbuf,
+    heads, probs, prob_grad, mix_s, mix_b, dmix_b, dqkv_s, dqkv_b,
+    weight_sem, x_send, x_recv, y_send, y_recv, g_send, g_recv, a_send, a_recv, r_send, r_recv,
+    misc_send, misc_recv,
+):
+    grid_rows, grid_cols, rows, steps, tile_rows, tile_cols = sizes
+    n_dev = grid_rows * grid_cols
+    width = latents.shape[1]
+    quads = grid_cols // 2
+    chunk = width // grid_cols
+    own = chunk // grid_rows
+    tall = grid_rows * tile_rows
+    z = lax.axis_index("rows")
+    j = lax.axis_index("cols")
+    core = lax.rem(j, 2)
+    quad = j // 2
+    me = z * grid_cols + j
+    f32, bf16 = jnp.float32, jnp.bfloat16
+    score_scale = width ** (-0.5)
+    head_scale = HEAD_DIM ** (-0.5)
+
+    def at_device(d):
+        return {"rows": d // grid_cols, "cols": lax.rem(d, grid_cols)}
+
+    def lanes_of(index):
+        return pl.ds(pl.multiple_of(index * chunk, chunk), chunk)
+
+    def push(src, dst, send, recv, where):
+        pltpu.make_async_remote_copy(
+            src_ref=src, dst_ref=dst, send_sem=send, recv_sem=recv, device_id=where,
+            device_id_type=MESH,
+        ).start()
+
+    def wait_for(ref, sem):
+        pltpu.make_async_copy(ref, ref, sem).wait()
+
+    barrier = pltpu.get_barrier_semaphore()
+
+    def greet(step, carry):
+        pl.semaphore_signal(
+            barrier, inc=1, device_id=at_device(lax.rem(me + step, n_dev)), device_id_type=MESH
+        )
+        return carry
+
+    lax.fori_loop(1, n_dev, greet, 0)
+
+    sources = (
+        [w_cross.at[0], w_out, w_cross.at[1], w_cross.at[2]]
+        + [w_self.at[0], w_self.at[1], w_self.at[2], w_self_out, w_self.at[3], w_self.at[4]]
+    )
+    CQ, CO, C1, C2, SQ, SK, SV, SO, S1, S2 = range(10)
+    loads = [pltpu.make_async_copy(s, wts.at[k], weight_sem.at[k]) for k, s in enumerate(sources)]
+    loads.append(pltpu.make_async_copy(w_input, win, weight_sem.at[10]))
+    loads[CQ].start()
+    loads[10].start()
+
+    gc, bc = to_float(cross_gains[...]), to_float(cross_biases[...])
+    gs, bs = to_float(self_gains[...]), to_float(self_biases[...])
+    gin, bin_ = input_gains[0:1], input_gains[1:2]
+    lat = to_float(latents[...])
+    nq = norm_forward(lat, gc[0:1], bc[0:1])
+    xbuf[0, core, quad] = nq
+
+    pl.semaphore_wait(barrier, n_dev - 1)
+
+    def send_color(step, carry):
+        d = lax.rem(me + step, n_dev)
+        push(color_tiles.at[d // grid_cols], colbuf.at[me], misc_send.at[0], misc_recv.at[0], at_device(d))
+        return carry
+
+    lax.fori_loop(1, n_dev, send_color, 0)
+    colbuf[me] = color_tiles[z]
+
+    def x_spread(block, sem):
+        def one(step, carry):
+            peer = 2 * lax.rem(quad + step, quads) + core
+            push(block, block, x_send.at[sem], x_recv.at[sem], {"cols": peer})
+            return carry
+
+        lax.fori_loop(1, quads, one, 0)
+
+    def x_relay(half, sem):
+        wait_for(half.at[pl.ds(0, quads - 1)], x_recv.at[sem])
+        push(half, half, y_send.at[sem], y_recv.at[sem], {"cols": j + 1 - 2 * core})
+
+    def x_arrived(half, sem):
+        wait_for(half, y_recv.at[sem])
+
+    def spread_x(k):
+        x_spread(xbuf.at[k, core, quad], k)
+
+    def relay_x(k):
+        x_relay(xbuf.at[k, core], k)
+
+    def have_x(k):
+        x_arrived(xbuf.at[k, 1 - core], k)
+
+    def to_plane(step):
+        peer = lax.rem(j + step, grid_cols)
+        return peer, {"cols": peer}
+
+    def spread_g(k, values):
+        gsrc[k] = values
+
+        def one(step, carry):
+            peer, where = to_plane(step)
+            push(gsrc.at[k, :, lanes_of(peer)], gbuf.at[k, core, quad], g_send.at[k], g_recv.at[k], where)
+            return carry
+
+        lax.fori_loop(1, grid_cols, one, 0)
+        gbuf[k, core, quad] = gsrc[k, :, lanes_of(j)]
+
+    def have_g(k):
+        wait_for(gsrc.at[k, :, pl.ds(0, chunk * (grid_cols - 1))], g_recv.at[k])
+        return gbuf[k].reshape(grid_cols * rows, chunk)
+
+    def send_parts(src, dst, sem):
+        for part in range(grid_rows):
+            d = grid_rows * j + part
+            block = src.at[pl.ds(part * own, own)]
+
+            @pl.when(d != me)
+            def _():
+                push(block, dst.at[z], r_send.at[sem], r_recv.at[sem], at_device(d))
+
+            @pl.when(d == me)
+            def _():
+                pltpu.make_async_copy(block, dst.at[z], r_recv.at[sem]).start()
+
+    def weight_part(m, right, left):
+        def one(n, carry):
+            at = pl.ds(pl.multiple_of(n * 256, 256), 256)
+            block = left[:, :, :, at].reshape(grid_cols * rows, 256)
+            staged[m, :, at] = narrow(own_dot(right, block, 0, 0))
+            return carry
+
+        lax.fori_loop(0, width // 256, one, 0)
+        send_parts(staged.at[m], arrived.at[m], m)
+
+    def small_part(m, right, left):
+        staged_small[m] = narrow(own_dot(right, left[...].reshape(grid_cols * rows, WIDE), 0, 0))
+        send_parts(staged_small.at[m], arrived_small.at[m], 10 + m)
+
+    def times(x, k, out):
+        def one(n, carry):
+            at = pl.ds(pl.multiple_of(n * 256, 256), 256)
+            out[:, at] = own_dot(x, wts[k, :, at], 1, 0)
+            return carry
+
+        lax.fori_loop(0, width // 256, one, 0)
+
+    def times_t(x, k, out, add=False):
+        def one(n, carry):
+            at = pl.ds(pl.multiple_of(n * 256, 256), 256)
+            result = own_dot(x, wts[k, at, :], 1, 1)
+            out[:, at] = out[:, at] + result if add else result
+            return carry
+
+        lax.fori_loop(0, width // 256, one, 0)
+
+    FIRST, SECOND, THIRD, PRE_C, PRE_S, TMP, ATT, GRAD = range(8)
+    tmp = act.at[TMP]
+
+    spread_x(0)
+    loads[CQ].wait()
+    for k in range(1, 10):
+        loads[k].start()
+    times(nq, CQ, tmp)
+    query_low = narrow(tmp[...] + bc[2:3])
+    spread_g(7, query_low)
+    loads[10].wait()
+    query_inputs = own_dot(query_low, win[0], 1, 1)
+
+    box = [boxes[z, k] for k in range(4)]
+
+    def filled(value, shape):
+        return to_float(jnp.full(shape, value, jnp.int32))
+
+    row_at = lax.broadcasted_iota(jnp.int32, (tall, 1), 0)
+    y_place = -1.0 + 2.0 * to_float(row_at - box[0]) / filled(box[2] - 1, (tall, 1))
+    y_lines = axis_lines(y_place, 3)
+    y_sum = jnp.sum(y_lines, axis=1, keepdims=True)
+    row_out = jnp.where((row_at >= box[0]) & (row_at < box[0] + box[2]), 0.0, NEG)
+    yfeat[...] = narrow(y_lines)
+    held_rows = xfeat.shape[1]
+    col_lane = lax.broadcasted_iota(jnp.int32, (held_rows, LANES), 1)
+    col_row = lax.broadcasted_iota(jnp.int32, (held_rows, LANES), 0)
+    x_sum = jnp.zeros((1, LANES), f32)
+    col_out = []
+    for half in range(2):
+        col_at = lax.broadcasted_iota(jnp.int32, (held_rows, 1), 0) + half * steps
+        x_place = -1.0 + 2.0 * to_float(col_at - box[1]) / filled(box[3] - 1, (held_rows, 1))
+        x_lines = axis_lines(x_place, 4)
+        xfeat[half] = narrow(x_lines)
+        here = (col_lane == col_row + half * steps) & (col_row < steps)
+        x_sum = x_sum + jnp.sum(
+            jnp.where(here, jnp.sum(x_lines, axis=1, keepdims=True), 0.0), axis=0, keepdims=True
+        )
+        col_out.append(jnp.where((col_at >= box[1]) & (col_at < box[1] + box[3]), 0.0, NEG))
+    x_lane = lax.broadcasted_iota(jnp.int32, (1, LANES), 1)
+    x_here = -1.0 + 2.0 * to_float(x_lane - box[1]) / filled(box[3] - 1, (1, LANES))
+    count = 3 + 2 + 4 * NBANDS
+
+    wait_for(colbuf.at[pl.ds(0, n_dev - 1)], misc_recv.at[0])
+    for part in range(grid_rows):
+        at = pl.ds(part * tile_rows, tile_rows)
+        tiles = colbuf[part * grid_cols : (part + 1) * grid_cols].reshape(grid_cols * 32, LANES)
+        img[at, :] = own_dot(tiles, place[...], 0, 0)[:tile_rows]
+    c0, c1, c2 = img[:, :LANES], img[:, LANES : 2 * LANES], img[:, 2 * LANES :]
+    mean = (c0 + c1 + c2 + y_sum + x_sum) * (1.0 / count)
+    square = (c0 * c0 + c1 * c1 + c2 * c2 + y_place * y_place + x_here * x_here + 2.0 * NBANDS) * (
+        1.0 / count
+    )
+    dev = lax.rsqrt(square - mean * mean + EPS)
+    mean_low, dev_low = narrow(mean), narrow(dev)
+    img7[...] = jnp.concatenate(
+        [
+            narrow(c0), narrow(c1), narrow(c2),
+            mean_low, narrow(mean - to_float(mean_low)),
+            dev_low, narrow(dev - to_float(dev_low)),
+        ],
+        axis=1,
+    )
+    blocks = fa.shape[0]
+    for block in range(blocks):
+        at = pl.ds(block * LANES, LANES)
+        fa[block] = narrow(own_dot(img7[...], pick[:, at], 1, 0))
+        turned = own_dot(pick_t[at, :], img7[...], 1, 1)
+        line = lax.broadcasted_iota(jnp.int32, turned.shape, 0)
+        ft[at, :] = narrow(jnp.where(lax.rem(line, 8) == 5, 1.0, turned))
+
+    lane1 = lax.broadcasted_iota(jnp.int32, (rows, LANES), 1)
+    lane_half = lax.broadcasted_iota(jnp.int32, (8, LANES), 1) // rows
+    sub8 = lax.broadcasted_iota(jnp.int32, (8, LANES), 0)
+
+    def twice(values):
+        return jnp.concatenate([values, values], axis=0)
+
+    def turn(values):
+        return jnp.transpose(twice(values))[:8]
+
+    def coefficients(scaled, extra):
+        tail = scaled[:, 2 * LANES :]
+        total = jnp.sum(scaled, axis=1, keepdims=True)
+        turned = turn(jnp.where(lane1 == 5, total, jnp.where(lane1 == 6, extra, tail)))
+        total_high = to_float(narrow(turned[5:6]))
+        body = jnp.where(
+            sub8 < 3, turned, jnp.where(sub8 < 5, -total_high, jnp.where(sub8 == 5, total_high - turned[5:6], 0.0))
+        )
+        body = narrow(jnp.concatenate(
+            [jnp.where(lane_half == 0, body, 0.0), jnp.where(lane_half == 1, body, 0.0)], axis=0
+        ))
+        ones = jnp.where(sub8 >= 6, 1.0, 0.0)
+        ones = narrow(jnp.concatenate(
+            [jnp.where(lane_half == 0, ones, 0.0), jnp.where(lane_half == 1, ones, 0.0)], axis=0
+        ))
+        mixrow[...] = jnp.zeros(mixrow.shape, bf16)
+        for held in range(STEPS_HELD):
+            mixrow[held, held * 16 : held * 16 + 16, :] = jnp.concatenate([body, ones], axis=1)
+        scaled_low = narrow(jnp.concatenate([scaled[:, :LANES], tail], axis=1))
+        ycoef[...] = own_dot(yfeat[...], twice(scaled_low), 1, 1)
+        scaled_low = narrow(jnp.concatenate([scaled[:, LANES : 2 * LANES], tail], axis=1))
+        nothing = jnp.zeros_like(scaled_low)
+        xcoef[...] = own_dot(xfeat[0], jnp.concatenate([scaled_low, nothing], axis=0), 1, 1) + own_dot(
+            xfeat[1], jnp.concatenate([nothing, scaled_low], axis=0), 1, 1
+        )
+        return turned
+
+    def step_lines(s):
+        block, held = s // STEPS_HELD, lax.rem(s, STEPS_HELD)
+        result = own_dot(fa[block], mixrow[held], 1, 0)
+        deviation = result[:, LANES:]
+        lines = (ycoef[...] + xcoef[pl.ds(s, 1), :] + result[:, :LANES]) * deviation
+        return lines, deviation
+
+    def step_sums(s, weighted):
+        rowsum[...] += weighted
+        at = pl.ds(pl.multiple_of(s * 16, 16), 16)
+        found = own_dot(ft[at, :], narrow(weighted), 1, 0)
+        found = jnp.where(lane_half == 0, found[:8], found[8:])
+        colsum[pl.ds(s, 1), :] = found[5:6]
+        return found
+
+    def fold(values):
+        return values[:rows] + values[rows:]
+
+    def pixel_sums(found, factor):
+        by_row = fold(own_dot(narrow(rowsum[...] * factor), yfeat[...], 0, 0))
+        cols = narrow(colsum[...] * factor)
+        by_col = own_dot(cols, xfeat[0], 0, 0)[:rows] + own_dot(cols, xfeat[1], 0, 0)[rows:]
+        padded = jnp.concatenate([found * factor, jnp.zeros((LANES - 8, LANES), f32)], axis=0)
+        sums = fold(jnp.transpose(padded))
+        middle = sums[:, 3:4] + sums[:, 4:5]
+        tail = jnp.where(lane1 < 3, sums, 0.0) + by_row[:, LANES:] + by_col[:, LANES:]
+        return jnp.concatenate([by_row[:, :LANES], by_col[:, :LANES], tail], axis=1) - middle
+
+    def other_half(line):
+        return pltpu.roll(jnp.broadcast_to(line, (8, LANES)), rows, 1)[:1]
+
+    query_scaled = query_inputs * gin * score_scale
+    coefficients(query_scaled, 0.0)
+    ycoef[...] += row_out
+    half_lane = lax.broadcasted_iota(jnp.int32, (held_rows, LANES), 1) // rows
+    xcoef[...] += jnp.where(half_lane == 0, col_out[0], col_out[1])
+
+    def first_pass(s, best):
+        lines, deviation = step_lines(s)
+        sl[s] = lines
+        return jnp.maximum(best, jnp.max(lines, axis=0, keepdims=True))
+
+    best = lax.fori_loop(0, steps, first_pass, jnp.full((1, LANES), -3e38, f32))
+    best = jnp.maximum(best, other_half(best))
+    rowsum[...] = jnp.zeros(rowsum.shape, f32)
+    colsum[...] = jnp.zeros(colsum.shape, f32)
+
+    def second_pass(s, carry):
+        total, found = carry
+        block, held = s // STEPS_HELD, lax.rem(s, STEPS_HELD)
+        deviation = own_dot(fa[block], mixrow[held][:, LANES:], 1, 0)
+        weights = jnp.exp(sl[s] - best)
+        total = total + jnp.sum(weights, axis=0, keepdims=True)
+        return total, found + step_sums(s, weights * deviation)
+
+    total, found = lax.fori_loop(
+        0, steps, second_pass, (jnp.zeros((1, LANES), f32), jnp.zeros((8, LANES), f32))
+    )
+    total = total + other_half(total)
+    log_total = best + jnp.log(total)
+    plain_mixed = pixel_sums(found, 1.0 / total)
+    mixed_low = narrow(plain_mixed * gin + bin_)
+    xsmall[0, core, quad] = mixed_low
+    relay_x(0)
+    attended = own_dot(mixed_low, win[1], 1, 0) + bc[3:4]
+    act[ATT] = attended
+    attended_low = narrow(attended)
+    xbuf[3, core, quad] = attended_low
+    loads[CO].wait()
+    times(attended_low, CO, tmp)
+    first = lat + tmp[...] + bc[4:5]
+    act[FIRST] = first
+    normed_c = norm_forward(first, gc[1:2], bc[1:2])
+    xbuf[1, core, quad] = normed_c
+    loads[C1].wait()
+    times(normed_c, C1, tmp)
+    pre = tmp[...] + bc[5:6]
+    act[PRE_C] = pre
+    hidden_c = narrow(gelu_value(pre))
+    xbuf[2, core, quad] = hidden_c
+    loads[C2].wait()
+    times(hidden_c, C2, tmp)
+    second = act[FIRST] + tmp[...] + bc[6:7]
+    act[SECOND] = second
+    normed_t = norm_forward(second, gs[0:1], bs[0:1])
+    xbuf[4, core, quad] = normed_t
+    spread_x(4)
+    relay_x(4)
+    x_spread(xsmall.at[0, core, quad], 8)
+    spread_x(3)
+    spread_x(1)
+    spread_x(2)
+    have_x(4)
+
+    for k in (SQ, SK, SV):
+        loads[k].wait()
+    head_rows = grid_cols * rows
+    biasvec[...] = jnp.concatenate([bs, jnp.zeros((1, width), f32)], axis=0)
+
+    def head_in(n, carry):
+        x = xbuf[4, n].reshape(quads * rows, width)
+        at = pl.ds(pl.multiple_of(n * (quads * rows), quads * rows), quads * rows)
+        heads[0, at, :] = narrow(own_dot(x, wts[SQ, :, lanes_of(j)], 1, 0) + biasvec[2:3, lanes_of(j)])
+        heads[1, at, :] = narrow(own_dot(x, wts[SK, :, lanes_of(j)], 1, 0))
+        heads[2, at, :] = narrow(own_dot(x, wts[SV, :, lanes_of(j)], 1, 0) + biasvec[3:4, lanes_of(j)])
+        return carry
+
+    lax.fori_loop(0, 2, head_in, 0)
+    per = 128
+
+    def head_forward(n, carry):
+        at = pl.ds(pl.multiple_of(n * per, per), per)
+        scores = own_dot(heads[0, at, :], heads[1], 1, 1) * head_scale
+        weights = jnp.exp(scores - jnp.max(scores, axis=1, keepdims=True))
+        found_probs = weights / jnp.sum(weights, axis=1, keepdims=True)
+        probs[at, :] = found_probs
+        mixed = narrow(own_dot(narrow(found_probs), heads[2], 1, 0))
+        for part in range(per // rows):
+            mix_s[n * (per // rows) + part] = mixed[part * rows : (part + 1) * rows]
+        return carry
+
+    lax.fori_loop(0, head_rows // per, head_forward, 0)
+
+    def block_of(peer):
+        return lax.rem(peer, 2) * quads + peer // 2
+
+    mine = core * quads + quad
+
+    def send_mixed(step, carry):
+        peer, where = to_plane(step)
+        push(mix_s.at[block_of(peer)], mix_b.at[:, lanes_of(j)], a_send.at[0], a_recv.at[0], where)
+        return carry
+
+    lax.fori_loop(1, grid_cols, send_mixed, 0)
+    mix_b[:, lanes_of(j)] = mix_s[mine]
+    relay_x(3)
+    relay_x(1)
+    relay_x(2)
+    x_relay(xsmall.at[0, core], 8)
+    loads[SO].wait()
+    wait_for(mix_b.at[:, pl.ds(0, chunk * (grid_cols - 1))], a_recv.at[0])
+    mixed_rows = mix_b[...]
+    xbuf[7, core, quad] = mixed_rows
+    times(mixed_rows, SO, tmp)
+    third = act[SECOND] + tmp[...] + bs[4:5]
+    act[THIRD] = third
+    normed_s = norm_forward(third, gs[1:2], bs[1:2])
+    xbuf[5, core, quad] = normed_s
+    spread_x(7)
+    loads[S1].wait()
+    times(normed_s, S1, tmp)
+    spread_x(5)
+    pre = tmp[...] + bs[5:6]
+    act[PRE_S] = pre
+    hidden_s = narrow(gelu_value(pre))
+    xbuf[6, core, quad] = hidden_s
+    spread_x(6)
+    loads[S2].wait()
+    times(hidden_s, S2, tmp)
+    new_latents[...] = narrow(act[THIRD] + tmp[...] + bs[6:7])
+
+    cot_low = cotangent[...]
+    spread_g(5, cot_low)
+    times_t(cot_low, S2, tmp)
+    d_pre = tmp[...] * gelu_slope(act[PRE_S])
+    pre_low = narrow(d_pre)
+    spread_g(4, pre_low)
+    times_t(pre_low, S1, tmp)
+    d_rows, lnvec[6:7, :], lnvec[7:8, :] = norm_gradient(act[THIRD], gs[1:2], tmp[...])
+    gradient = to_float(cot_low) + d_rows
+    act[GRAD] = gradient
+    out_low = narrow(gradient)
+    times_t(out_low, SO, tmp)
+    mix_b2 = narrow(tmp[...])
+    gsrc[9] = mix_b2
+
+    def send_dmixed(step, carry):
+        peer, where = to_plane(step)
+        push(gsrc.at[9, :, lanes_of(peer)], dmix_b.at[mine], a_send.at[1], a_recv.at[1], where)
+        return carry
+
+    lax.fori_loop(1, grid_cols, send_dmixed, 0)
+    dmix_b[mine] = gsrc[9, :, lanes_of(j)]
+    spread_g(6, out_low)
+    relay_x(7)
+    relay_x(5)
+    relay_x(6)
+    wait_for(dmix_b.at[pl.ds(0, grid_cols - 1)], a_recv.at[1])
+
+    def head_backward(n, carry):
+        at = pl.ds(pl.multiple_of(n * per, per), per)
+        parts = [dmix_b[n * (per // rows) + part] for part in range(per // rows)]
+        d_mixed = jnp.concatenate(parts, axis=0)
+        d_probs = own_dot(d_mixed, heads[2], 1, 1)
+        found_probs = probs[at, :]
+        d_scores = found_probs * (d_probs - jnp.sum(found_probs * d_probs, axis=1, keepdims=True))
+        d_low = narrow(d_scores * head_scale)
+        prob_grad[0, at, :] = d_low
+        prob_grad[1, at, :] = narrow(found_probs)
+        d_query = own_dot(d_low, heads[1], 1, 0)
+        for part in range(per // rows):
+            dqkv_s[n * (per // rows) + part, 0] = narrow(d_query[part * rows : (part + 1) * rows])
+        return carry + jnp.sum(d_query, axis=0, keepdims=True)
+
+    query_bias = lax.fori_loop(0, head_rows // per, head_backward, jnp.zeros((1, chunk), f32))
+    d_mixed_all = dmix_b[...].reshape(head_rows, chunk)
+
+    def head_keys(n, carry):
+        at = pl.ds(pl.multiple_of(n * per, per), per)
+        d_key = own_dot(prob_grad[0, :, at], heads[0], 0, 0)
+        d_value = own_dot(prob_grad[1, :, at], d_mixed_all, 0, 0)
+        for part in range(per // rows):
+            cut = slice(part * rows, (part + 1) * rows)
+            dqkv_s[n * (per // rows) + part, 1] = narrow(d_key[cut])
+            dqkv_s[n * (per // rows) + part, 2] = narrow(d_value[cut])
+        return carry + jnp.sum(d_value, axis=0, keepdims=True)
+
+    value_bias = lax.fori_loop(0, head_rows // per, head_keys, jnp.zeros((1, chunk), f32))
+
+    def send_dqkv(step, carry):
+        peer, where = to_plane(step)
+        push(dqkv_s.at[block_of(peer)], dqkv_b.at[:, :, lanes_of(j)], a_send.at[2], a_recv.at[2], where)
+        return carry
+
+    lax.fori_loop(1, grid_cols, send_dqkv, 0)
+    dqkv_b[:, :, lanes_of(j)] = dqkv_s[mine]
+
+    def column_sum(values):
+        return jnp.sum(to_float(values), axis=0, keepdims=True)
+
+    have_x(6)
+    right = have_g(5)
+    bias_s6 = column_sum(right)
+    weight_part(8, right, xbuf.at[6])
+    have_x(5)
+    right = have_g(4)
+    bias_s5 = column_sum(right)
+    weight_part(7, right, xbuf.at[5])
+
+    wait_for(dqkv_b.at[:, :, pl.ds(0, chunk * (grid_cols - 1))], a_recv.at[2])
+    times_t(dqkv_b[0], SQ, tmp)
+    times_t(dqkv_b[1], SK, tmp, True)
+    times_t(dqkv_b[2], SV, tmp, True)
+    d_rows, lnvec[4:5, :], lnvec[5:6, :] = norm_gradient(act[SECOND], gs[0:1], tmp[...])
+    gradient = act[GRAD] + d_rows
+    act[GRAD] = gradient
+    second_low = narrow(gradient)
+    spread_g(2, second_low)
+    times_t(second_low, C2, tmp)
+    d_pre = tmp[...] * gelu_slope(act[PRE_C])
+    pre_low = narrow(d_pre)
+    spread_g(1, pre_low)
+    times_t(pre_low, C1, tmp)
+    d_rows, lnvec[2:3, :], lnvec[3:4, :] = norm_gradient(act[FIRST], gc[1:2], tmp[...])
+    gradient = act[GRAD] + d_rows
+    act[GRAD] = gradient
+    out_low = narrow(gradient)
+    spread_g(3, out_low)
+    times_t(out_low, CO, tmp)
+    d_attended = narrow(tmp[...])
+    spread_g(8, d_attended)
+
+    have_x(7)
+    right = have_g(6)
+    bias_s4 = column_sum(right)
+    weight_part(9, right, xbuf.at[7])
+    for k in range(3):
+        weight_part(4 + k, dqkv_s[:, k].reshape(head_rows, chunk), xbuf.at[4])
+
+    grad_inputs = own_dot(d_attended, win[1], 1, 1)
+    d_attended = to_float(d_attended)
+    shift = jnp.sum(d_attended * bc[3:4], axis=1, keepdims=True)
+    row_delta = jnp.sum(d_attended * act[ATT], axis=1, keepdims=True) - shift
+    grad_shift = jnp.sum(grad_inputs * bin_, axis=1, keepdims=True)
+    grad_scaled = grad_inputs * gin
+    turned = coefficients(grad_scaled, grad_shift - row_delta)
+    constant = turned[6:7]
+
+    def away(scaled):
+        values = scaled[:, 2 * LANES :] - jnp.sum(scaled, axis=1, keepdims=True) * (1.0 / count)
+        values = jnp.where(lane1 < 3, values, 0.0)
+        return jnp.concatenate([values, pltpu.roll(values, 8, 1)], axis=0)
+
+    query_away, grad_away = away(query_scaled), away(grad_scaled)
+    wide_lane = lax.broadcasted_iota(jnp.int32, (LANES, LANES), 1)
+    wide_half = lax.broadcasted_iota(jnp.int32, (LANES, LANES), 0) // rows
+    blank = jnp.zeros((LANES, LANES), bf16)
+    for held in range(STEPS_HELD):
+        group = wide_lane - held * 16 - wide_half * 8
+        along = narrow(jnp.where((group >= 0) & (group < 3), 1.0, 0.0))
+        colors_here = [query_away, grad_away]
+        if held:
+            colors_here = [pltpu.roll(v, held * 16, 1) for v in colors_here]
+        cgright[held] = jnp.concatenate(
+            [
+                jnp.concatenate([narrow(colors_here[0]), blank], axis=1),
+                jnp.concatenate([narrow(colors_here[1]), blank], axis=1),
+                jnp.concatenate([blank, along], axis=1),
+            ],
+            axis=0,
+        )
+    rowsum[...] = jnp.zeros(rowsum.shape, f32)
+    colsum[...] = jnp.zeros(colsum.shape, f32)
+    cgacc[...] = jnp.zeros(cgacc.shape, f32)
+
+    def back_pass(s, carry):
+        total, found = carry
+        lines, deviation = step_lines(s)
+        scores = sl[s]
+        found_probs = jnp.exp(scores - log_total)
+        d_scores = found_probs * (lines + constant)
+        left = jnp.concatenate(
+            [narrow(d_scores), narrow(found_probs), narrow(d_scores * scores + found_probs * lines)], axis=1
+        )
+        block, held = s // STEPS_HELD, lax.rem(s, STEPS_HELD)
+        cgacc[block] += own_dot(left, cgright[held], 1, 0)
+        total = total + jnp.sum(d_scores, axis=0, keepdims=True)
+        return total, found + step_sums(s, d_scores * deviation)
+
+    total, found = lax.fori_loop(
+        0, steps, back_pass, (jnp.zeros((1, LANES), f32), jnp.zeros((8, LANES), f32))
+    )
+    plain_scores = pixel_sums(found, 1.0) * score_scale
+    total = total * score_scale
+    score_total = fold(jnp.transpose(jnp.concatenate([total, jnp.zeros((LANES - 1, LANES), f32)], axis=0)))[:, 0:1]
+    score_low = narrow(plain_scores * gin + score_total * bin_)
+    xsmall[1, core, quad] = score_low
+    x_spread(xsmall.at[1, core, quad], 9)
+
+    def d_query_part(n, carry):
+        at = pl.ds(pl.multiple_of(n * 256, 256), 256)
+        tmp[:, at] = own_dot(score_low, win[0, :, at], 1, 0)
+        return carry
+
+    lax.fori_loop(0, width // 256, d_query_part, 0)
+    query_grad_low = narrow(tmp[...])
+    spread_g(0, query_grad_low)
+    gain_part = jnp.sum(query_inputs * plain_scores + grad_inputs * plain_mixed, axis=0, keepdims=True)
+    bias_part = jnp.sum(query_inputs * score_total + grad_inputs, axis=0, keepdims=True)
+    ivec[...] = jnp.concatenate([gain_part, bias_part, jnp.zeros((6, WIDE), f32)], axis=0)
+    ivbuf[me] = ivec[...]
+
+    def send_ivec(step, carry):
+        push(ivec, ivbuf.at[me], misc_send.at[1], misc_recv.at[1], at_device(lax.rem(me + step, n_dev)))
+        return carry
+
+    lax.fori_loop(1, n_dev, send_ivec, 0)
+
+    times_t(query_grad_low, CQ, tmp)
+    d_rows, lnvec[0:1, :], lnvec[1:2, :] = norm_gradient(to_float(latents[...]), gc[0:1], tmp[...])
+    latent_grad[...] = act[GRAD] + d_rows
+
+    def send_ln(step, carry):
+        peer, where = to_plane(step)
+        push(lnvec.at[:, lanes_of(peer)], lnbuf.at[j], misc_send.at[2], misc_recv.at[2], where)
+        return carry
+
+    lax.fori_loop(1, grid_cols, send_ln, 0)
+    lnbuf[j] = lnvec[:, lanes_of(j)]
+
+    for block in range(blocks):
+        both = own_dot(fa[block], spread[...], 1, 0)
+        center, factor = both[:, :LANES], both[:, LANES:]
+        here = cgacc[block]
+        cgacc[block, :, :LANES] = factor * (
+            here[:, :LANES] - (to_float(fa[block]) - center) * factor * here[:, LANES:] * (1.0 / count)
+        )
+    for part in range(grid_rows):
+        at = pl.ds(part * tile_rows, tile_rows)
+        lines = jnp.concatenate([narrow(cgacc[block, at, :LANES]) for block in range(blocks)], axis=1)
+        tiles = narrow(own_dot(back[...], lines, 1, 1))
+        for tile in range(grid_cols):
+            cgsend[part * grid_cols + tile, :, :tile_rows] = tiles[tile * 32 : tile * 32 + 32]
+    cgbuf[me] = cgsend[me]
+
+    def send_cg(step, carry):
+        d = lax.rem(me + step, n_dev)
+        push(cgsend.at[d], cgbuf.at[me], misc_send.at[3], misc_recv.at[3], at_device(d))
+        return carry
+
+    lax.fori_loop(1, n_dev, send_cg, 0)
+
+    x_relay(xsmall.at[1, core], 9)
+    for m, (left, g) in ((2, (2, 2)), (1, (1, 1)), (3, (3, 3))):
+        have_x(left)
+        right = have_g(g)
+        if m == 2:
+            bias_c6 = column_sum(right)
+        elif m == 1:
+            bias_c5 = column_sum(right)
+        else:
+            bias_c4 = column_sum(right)
+        weight_part(m, right, xbuf.at[left])
+    x_arrived(xsmall.at[0, 1 - core], 8)
+    right = have_g(8)
+    bias_c3 = column_sum(right)
+    small_part(1, right, xsmall.at[0])
+    have_x(0)
+    right = have_g(0)
+    bias_c2 = column_sum(right)
+    weight_part(0, right, xbuf.at[0])
+    x_arrived(xsmall.at[1, 1 - core], 9)
+    small_part(0, have_g(7), xsmall.at[1])
+
+    wait_for(lnbuf.at[pl.ds(0, grid_cols - 1)], misc_recv.at[2])
+    norms = lnbuf[0]
+    for peer in range(1, grid_cols):
+        norms = norms + lnbuf[peer]
+    vecsend[...] = jnp.concatenate(
+        [
+            norms, bias_c2, bias_c3, bias_c4, bias_c5, bias_c6, query_bias, value_bias,
+            bias_s4, bias_s5, bias_s6, jnp.zeros((6, chunk), f32),
+        ],
+        axis=0,
+    )
+    for part in range(grid_rows):
+        d = grid_rows * j + part
+
+        @pl.when(d != me)
+        def _():
+            push(vecsend, vecbuf.at[z], misc_send.at[4], misc_recv.at[4], at_device(d))
+
+        @pl.when(d == me)
+        def _():
+            pltpu.make_async_copy(vecsend, vecbuf.at[z], misc_recv.at[4]).start()
+
+    wait_for(cgbuf.at[pl.ds(0, n_dev - 1)], misc_recv.at[3])
+    for part in range(grid_rows):
+        tile = to_float(cgbuf[part * grid_cols])
+        for peer in range(1, grid_cols):
+            tile = tile + to_float(cgbuf[part * grid_cols + peer])
+        color_out[part] = tile
+    wait_for(ivbuf.at[pl.ds(0, n_dev - 1)], misc_recv.at[1])
+    sums = ivbuf[0]
+    for d in range(1, n_dev):
+        sums = sums + ivbuf[d]
+    input_vector_out[...] = sums
+
+    def gathered(ref):
+        result = to_float(ref[0])
+        for part in range(1, grid_rows):
+            result = result + to_float(ref[part])
+        return result
+
+    order = (8, 7, 9, 4, 5, 6, 2, 1, 3, 0)
+    for m in order:
+        wait_for(arrived.at[m], r_recv.at[m])
+        result = gathered(arrived.at[m])
+        if m < 3:
+            cross_total[m] = prior_cross[m] + result
+        elif m == 3:
+            out_total[...] = prior_out[...] + result
+        elif m < 9:
+            self_total[m - 4] = result
+        else:
+            self_out_total[...] = result
+    for m in (1, 0):
+        wait_for(arrived_small.at[m], r_recv.at[10 + m])
+        input_parts[m] = gathered(arrived_small.at[m])
+    wait_for(vecbuf, misc_recv.at[4])
+    vector_out[...] = gathered(vecbuf)
+
+    for k in range(8):
+        wait_for(xbuf.at[k, 0, pl.ds(0, quads - 1)], x_send.at[k])
+        wait_for(xbuf.at[k, 0], y_send.at[k])
+    for k in range(2):
+        wait_for(xsmall.at[k, 0, pl.ds(0, quads - 1)], x_send.at[8 + k])
+        wait_for(xsmall.at[k, 0], y_send.at[8 + k])
+    for k in range(9):
+        wait_for(gsrc.at[k, :, pl.ds(0, chunk * (grid_cols - 1))], g_send.at[k])
+    wait_for(mix_s.at[pl.ds(0, grid_cols - 1)], a_send.at[0])
+    wait_for(dmix_b.at[pl.ds(0, grid_cols - 1)], a_send.at[1])
+    wait_for(dqkv_s.at[pl.ds(0, grid_cols - 1)], a_send.at[2])
+    wait_for(colbuf.at[pl.ds(0, n_dev - 1)], misc_send.at[0])
+    wait_for(ivbuf.at[pl.ds(0, n_dev - 1)], misc_send.at[1])
+    wait_for(lnbuf.at[pl.ds(0, grid_cols - 1)], misc_send.at[2])
+    wait_for(cgbuf.at[pl.ds(0, n_dev - 1)], misc_send.at[3])
+    away_from_me = me // grid_rows != j
+
+    @pl.when(away_from_me)
+    def _():
+        for m in range(10):
+            wait_for(staged.at[m], r_send.at[m])
+        for m in range(2):
+            wait_for(staged_small.at[m], r_send.at[10 + m])
+        wait_for(vecbuf, misc_send.at[4])
+
+    @pl.when(jnp.logical_not(away_from_me))
+    def _():
+        for m in range(10):
+            wait_for(staged.at[m, pl.ds(0, chunk - own)], r_send.at[m])
+        for m in range(2):
+            wait_for(staged_small.at[m, pl.ds(0, chunk - own)], r_send.at[10 + m])
+        wait_for(vecbuf.at[pl.ds(0, grid_rows - 1)], misc_send.at[4])
+
+
+def by_kind(rows):
+    n = NBANDS
+    parts = [rows[:, 5 : 5 + n], rows[:, 5 + 2 * n : 5 + 3 * n], rows[:, 5 + n : 5 + 2 * n]]
+    parts += [rows[:, 5 + 3 * n :], rows[:, :5]]
+    spare = WIDE - rows.shape[1]
+    return jnp.pad(jnp.concatenate(parts, axis=1), ((0, 0), (0, spare)) + ((0, 0),) * (rows.ndim - 2))
+
+
+def by_channel(lines):
+    n = NBANDS
+    parts = [lines[..., 4 * n : 4 * n + 5], lines[..., :n], lines[..., 2 * n : 3 * n]]
+    parts += [lines[..., n : 2 * n], lines[..., 3 * n : 4 * n]]
+    return jnp.concatenate(parts, axis=-1)
+
+
+def local_kernel(
+    latents,
+    pixel_colors,
+    image_boxes,
+    cotangent,
+    cross_matrices,
+    cross_out,
+    input_matrices,
+    in_gain,
+    in_bias,
+    cross_gains,
+    cross_biases,
+    self_matrices,
+    self_out,
+    self_gains,
+    self_biases,
+    prior_cross_matrices,
+    prior_cross_out,
+    prior_input_matrices,
+):
+    rows, width = latents.shape
+    channels, image_count, tile_rows, tile_cols = pixel_colors.shape
+    grid_rows = lax.axis_size("rows")
+    grid_cols = lax.axis_size("cols")
+    n_dev = grid_rows * grid_cols
+    tall, wide = grid_rows * tile_rows, grid_cols * tile_cols
+    steps = wide // 2
+    chunk = width // grid_cols
+    own = chunk // grid_rows
+    quads = grid_cols // 2
+    place, pick, pick_t, spread, back = selections(tile_cols, grid_cols, steps)
+    blocks = back.shape[1] // LANES
+    held_rows = -(-steps // 8) * 8
+    color_tiles = jnp.transpose(pixel_colors, (1, 0, 3, 2)).reshape(
+        image_count, channels * tile_cols, tile_rows
+    )
+    color_tiles = jnp.pad(
+        color_tiles, ((0, 0), (0, 32 - channels * tile_cols), (0, LANES - tile_rows))
+    )
+    w_input = by_kind(input_matrices)
+    input_gains = by_kind(to_float(jnp.stack([in_gain, in_bias])))
+    input_gains = jnp.pad(input_gains, ((0, 6), (0, 0)))
+    f32, bf16 = jnp.float32, jnp.bfloat16
+    vmem = pl.BlockSpec(memory_space=pltpu.VMEM)
+    away = pl.BlockSpec(memory_space=pl.ANY)
+    shape = jax.ShapeDtypeStruct
+    sizes = (grid_rows, grid_cols, rows, steps, tile_rows, tile_cols)
+    dma = pltpu.SemaphoreType.DMA
+    scratch = [
+        ((10, width, width), bf16),
+        ((2, WIDE, width), bf16),
+        ((8, 2, quads, rows, width), bf16),
+        ((2, 2, quads, rows, WIDE), bf16),
+        ((10, rows, width), bf16),
+        ((9, 2, quads, rows, chunk), bf16),
+        ((10, chunk, width), bf16),
+        ((10, grid_rows, own, width), bf16),
+        ((2, chunk, WIDE), bf16),
+        ((2, grid_rows, own, WIDE), bf16),
+        ((n_dev, 32, LANES), bf16),
+        ((tall, WIDE), f32),
+        ((tall, 7 * LANES), bf16),
+        ((blocks, tall, LANES), bf16),
+        ((blocks * LANES, tall), bf16),
+        ((steps, tall, LANES), f32),
+        ((tall, LANES), f32),
+        ((held_rows, LANES), f32),
+        ((tall, 2 * LANES), bf16),
+        ((2, held_rows, 2 * LANES), bf16),
+        ((STEPS_HELD, LANES, 2 * LANES), bf16),
+        ((STEPS_HELD, WIDE, 2 * LANES), bf16),
+        ((tall, LANES), f32),
+        ((held_rows, LANES), f32),
+        ((blocks, tall, 2 * LANES), f32),
+        ((n_dev, 32, LANES), bf16),
+        ((n_dev, 32, LANES), bf16),
+        ((8, rows, width), f32),
+        ((8, width), f32),
+        ((grid_cols, 8, chunk), f32),
+        ((8, width), f32),
+        ((24, chunk), f32),
+        ((grid_rows, 24, chunk), f32),
+        ((8, WIDE), f32),
+        ((n_dev, 8, WIDE), f32),
+        ((3, grid_cols * rows, chunk), bf16),
+        ((grid_cols * rows, grid_cols * rows), f32),
+        ((2, grid_cols * rows, grid_cols * rows), bf16),
+        ((grid_cols, rows, chunk), bf16),
+        ((rows, width), bf16),
+        ((grid_cols, rows, chunk), bf16),
+        ((grid_cols, 3, rows, chunk), bf16),
+        ((3, rows, width), bf16),
+    ]
+    scratch = [pltpu.VMEM(dims, kind) for dims, kind in scratch]
+    scratch += [dma((count,)) for count in (11, 10, 10, 10, 10, 9, 9, 3, 3, 12, 12, 5, 5)]
+    outs = [
+        ((rows, width), bf16),
+        ((rows, width), f32),
+        ((image_count, 32, LANES), f32),
+        ((3, own, width), f32),
+        ((own, width), f32),
+        ((5, own, width), f32),
+        ((own, width), f32),
+        ((2, own, WIDE), f32),
+        ((24, chunk), f32),
+        ((8, WIDE), f32),
+    ]
+    results = pl.pallas_call(
+        functools.partial(layer_kernel, sizes),
+        out_shape=[shape(dims, kind) for dims, kind in outs],
+        in_specs=[pl.BlockSpec(memory_space=pltpu.SMEM)] + [vmem] * 15 + [away] * 5,
+        out_specs=[vmem] * len(outs),
+        scratch_shapes=scratch,
+        compiler_params=pltpu.CompilerParams(
+            collective_id=0, has_side_effects=True, vmem_limit_bytes=VMEM_BYTES
+        ),
+        cost_estimate=pl.CostEstimate(
+            flops=20_000_000_000, bytes_accessed=40_000_000, transcendentals=4_000_000
+        ),
+    )(
+        image_boxes,
+        latents,
+        cotangent,
+        color_tiles,
+        input_gains,
+        cross_gains,
+        cross_biases,
+        self_gains,
+        self_biases,
+        place,
+        pick,
+        pick_t,
+        spread,
+        back,
+        jnp.transpose(prior_cross_matrices, (0, 2, 1)),
+        jnp.transpose(prior_cross_out),
+        cross_matrices,
+        cross_out,
+        self_matrices,
+        self_out,
+        w_input,
+    )
+    new_latents, latent_grad, colors, cross_total, out_total = results[:5]
+    self_total, self_out_total, input_parts, vectors, input_vectors = results[5:]
+    me = lax.axis_index("rows") * grid_cols + lax.axis_index("cols")
+    vectors = lax.dynamic_slice_in_dim(vectors, lax.rem(me, grid_rows) * own, own, axis=1)
+    colors = colors[:, : channels * tile_cols, :tile_rows].reshape(
+        image_count, channels, tile_cols, tile_rows
+    )
+    input_total = prior_input_matrices + jnp.transpose(by_channel(input_parts), (0, 2, 1))
+    input_vectors = by_channel(input_vectors[:2])
+    return (
+        new_latents,
+        latent_grad,
+        jnp.transpose(colors, (1, 0, 3, 2)),
+        jnp.transpose(cross_total, (0, 2, 1)),
+        jnp.transpose(out_total),
+        input_total,
+        input_vectors[0],
+        input_vectors[1],
+        jnp.stack([vectors[0], vectors[2]]),
+        jnp.concatenate([vectors[1:2], vectors[3:4], vectors[8:13]]),
+        jnp.transpose(self_total, (0, 2, 1)),
+        jnp.transpose(self_out_total),
+        jnp.stack([vectors[4], vectors[6]]),
+        jnp.concatenate([vectors[5:6], vectors[7:8], vectors[13:18]]),
+    )
+
+
 def solution(mesh):
     placed = (
         P(("rows", "cols"), None),
@@ -521,8 +1584,9 @@
         P(None, ("rows", "cols")),
         P(None, None, ("rows", "cols")),
     )
+    one_head_each = mesh.shape["cols"] == HEADS
     return jax.shard_map(
-        local,
+        local_kernel if one_head_each else local,
         mesh=mesh,
         in_specs=placed,
         out_specs=(

time: 749 us -> 317 us (0.42); the launches traced: 737 us -> 317 us
  Pallas kernels: 0 us -> 296 us
  waiting for transfers between devices: 286 us -> 0 us
  matrix products: 115 us -> 0 us
  local copies, waits for them, and re-layouts: 125 us -> 17.6 us
  blocking collectives: 101 us -> 0 us
  other arithmetic: 79.3 us -> 1.85 us
  between operations: 20.8 us -> 0.77 us
  starting transfers between devices: 9.23 us -> 0 us
    pallas_call x0 -> x1, Pallas kernels: none -> 296 us  [local_kernel(): pl.pallas_call(functools.partial(layer_kernel, sizes), out_shape=[shape(d...]
    unnamed x11 -> x0, waiting for transfers between devices: 250 us -> none
    dot_general x52 -> x0, matrix products: 115 us -> none  [the longest x16 33.4 us: inner_right(): lax.dot_general(former, latter, (((1,), (1,)), ((), ())), preferred_eleme...]
    all_gather x2 -> x0, blocking collectives: 60.6 us -> none  [the longest x1 45.9 us: local(): lax.all_gather(pixel_colors, ('rows', 'cols'), axis=0, tiled=False)]
    reduce_sum x27 -> x0, other arithmetic: 48.8 us -> none  [the longest x2 15.8 us: over_pixels(): middle = jnp.sum(scaled * mean[None], axis=(1, 2))]
    psum x1 -> x0, blocking collectives: 40.6 us -> none  [local(): lax.psum((in_gain_part, in_bias_part), ('rows', 'cols'))]
    unnamed x313 -> x26, local copies, waits for them, and re-layouts: 41.7 us -> 4.48 us
    all_gather x3 -> x0, waiting for transfers between devices: 36.5 us -> none  [the longest x1 22 us: local(): lax.all_gather(tower_values, 'cols', axis=0, tiled=True)]
  transfers between devices with their start and end apart: 9 -> 0, of which waited for: 6 -> 0; matrix products, arithmetic and copies ran while one was open for 28% -> 0% of each run, Pallas kernels for 0% -> 0%
where the time goes in v2:
time: 317 us
  Pallas kernels  296 us (93%)
  local copies, waits for them, and re-layouts  17.6 us (6%)
    pallas_call x1, Pallas kernels, local_kernel(): pl.pallas_call(functools.partial(layer_kernel, sizes), out_shape=[shape(d...  296 us

profile of v2, /device:TPU:0, one launch (start us, length us, event | category | flops | bytes accessed | tf_op | source)
XLA Modules:
  0.0 316.6 jit_solution(17897517227787747813)
XLA Ops:
  0.6 0.8 copy.44
  1.4 0.6 pad.16.color_tiles
  2.0 0.7 stack.16
  2.7 0.7 stack.15
  3.4 0.1 fusion.5
  3.5 0.1 concatenate.18
  3.6 0.6 pad.32.input_gains
  4.2 1.9 fusion
  6.1 0.0 slice-start
  6.2 0.1 copy_dynamic-update-slice_fusion.2
  6.2 0.1 copy_dynamic-update-slice_fusion.1
  6.3 0.1 copy_dynamic-update-slice_fusion
  6.3 0.5 slice-done
  6.8 1.4 pad.19.w_input
  8.2 0.0 copy-start.6
  8.2 296.4 %shard_map.326 = (bf16[64,1024]{1,0:T(8,128)(2,1)}, f32[64,1024]{1,0:T(8,128)}, f32[4,32,128]{2,1,0:T(8,128)}, f32[3,32,1024]{2,1,0:T(8,128)}, f32[32,1024]{1,0:...) custom-call(s32[4,4]{1,0:T(4,128)} %boxes.1, ...), custom_call_target="tpu_custom_call" | custom-call | flops 20000000000 | bytes 40000000 | tf_op jit(solution)/shard_map/pallas_call | solution.py:1504
  304.6 0.0 copy-start.7
  304.7 0.0 copy-start.5
  304.7 0.0 copy-start.2
  304.7 0.0 copy-start.1
  304.7 1.6 copy.50
  306.3 0.8 slice.116
  307.0 0.9 fusion.1
  307.9 0.1 concatenate.20
  308.1 0.0 copy-done.6
  308.1 0.0 copy-start.4
  308.1 0.7 bitcast_add_fusion
  308.7 0.0 copy-start
  308.7 0.7 slice.121
  309.5 0.8 fusion.4
  310.3 0.1 concatenate.21
  310.4 0.6 slice_reduce_fusion
  311.0 0.0 copy-done.7
  311.0 0.1 fusion.2
  311.1 0.6 pad_maximum_fusion.2
  311.7 0.1 fusion.3
  311.8 0.6 pad_maximum_fusion
  312.4 0.0 copy-done.5
  312.4 0.7 copy.71
  313.0 0.0 copy-done.2
  313.0 0.7 copy.72
  313.7 0.0 copy-done.1
  313.7 0.0 copy-start.3
  313.7 0.7 copy.73
  314.5 0.0 copy-done.4
  314.5 0.7 copy.74
  315.1 0.0 copy-done
  315.1 0.8 copy.75
  316.0 0.0 copy-done.3
  316.0 0.7 copy.76
  (4 shorter events, 0.1 us)
Async XLA Ops:
  6.1 0.7 slice-start
  8.2 299.8 %copy-start.6 = (f32[2,261,32]{1,2,0:T(8,128)S(1)}, f32[2,261,32]{1,2,0:T(8,128)}, u32[]{:S(2)}) copy-start(f32[2,261,32]{1,2,0:T(8,128)} %param.40) | copy-start | bytes 200452
  304.6 6.4 %copy-start.7 = (f32[24,128]{1,0:T(8,128)S(1)}, f32[24,128]{1,0:T(8,128)}, u32[]{:S(2)}) copy-start(f32[24,128]{1,0:T(8,128)} %get-tuple-element.31) | copy-start | bytes 36868
  304.7 7.7 %copy-start.5 = (bf16[64,1024]{1,0:T(8,128)(2,1)S(1)}, bf16[64,1024]{1,0:T(8,128)(2,1)}, u32[]{:S(2)}) copy-start(bf16[64,1024]{1,0:T(8,128)(2,1)} %get-tuple-element.80) | copy-start | bytes 393220
  304.7 8.4 %copy-start.2 = (f32[64,1024]{1,0:T(8,128)S(1)}, f32[64,1024]{1,0:T(8,128)}, u32[]{:S(2)}) copy-start(f32[64,1024]{1,0:T(8,128)} %get-tuple-element.81) | copy-start | bytes 786436
  304.7 9.1 %copy-start.1 = (f32[3,32,1024]{2,1,0:T(8,128)S(1)}, f32[3,32,1024]{2,1,0:T(8,128)}, u32[]{:S(2)}) copy-start(f32[3,32,1024]{2,1,0:T(8,128)} %get-tuple-element.27) | copy-start | bytes 1179652
  308.1 6.4 %copy-start.4 = (f32[32,1024]{1,0:T(8,128)S(1)}, f32[32,1024]{1,0:T(8,128)}, u32[]{:S(2)}) copy-start(f32[32,1024]{1,0:T(8,128)} %get-tuple-element.28) | copy-start | bytes 393220
  308.7 6.4 %copy-start = (f32[5,32,1024]{2,1,0:T(8,128)S(1)}, f32[5,32,1024]{2,1,0:T(8,128)}, u32[]{:S(2)}) copy-start(f32[5,32,1024]{2,1,0:T(8,128)} %get-tuple-element.32) | copy-start | bytes 1966084
  313.7 2.2 copy-start.3

commit v3 on v2

--- a/solution.py
+++ b/solution.py
@@ -19,6 +19,7 @@
 NEG = -1e30
 FREQ_TOP = 112.0
 VMEM_BYTES = 63 * 1024 * 1024
+SEND = (4, 2, 0, 4, 4, 4, 4)
 
 
 def narrow(values):
@@ -548,7 +549,7 @@
             for slot in (6, 7):
                 spread[group * 8 + slot, LANES + group * 8 + channel] = 1
     low = lambda values: np.asarray(values, ml_dtypes.bfloat16)
-    return (low(place), low(pick), low(pick.T), low(spread), low(back))
+    return (low(place), low(pick), low(spread), low(back))
 
 
 def norm_parts(values):
@@ -607,17 +608,17 @@
 
 def layer_kernel(
     sizes,
-    boxes, latents, cotangent, color_tiles, input_gains, cross_gains, cross_biases, self_gains,
-    self_biases, place, pick, pick_t, spread, back, prior_cross, prior_out,
+    boxes, latents, cotangent, colors, in_gain, in_bias, order, cross_gains, cross_biases, self_gains,
+    self_biases, place, pick, spread, back,
     w_cross, w_out, w_self, w_self_out, w_input,
     new_latents, latent_grad, color_out, cross_total, out_total, self_total, self_out_total,
     input_parts, vector_out, input_vector_out,
-    wts, win, xbuf, xsmall, gsrc, gbuf, staged, arrived, staged_small, arrived_small,
-    colbuf, img, img7, fa, ft, sl, ycoef, xcoef, yfeat, xfeat, mixrow,
-    cgright, rowsum, colsum, cgacc, cgsend, cgbuf,
-    act, lnvec, lnbuf, biasvec, vecsend, vecbuf, ivec, ivbuf,
+    wts, win, win_raw, xbuf, xsmall, gsrc, gbuf, staged, paired, handed, crossed, staged_small, paired_small, handed_small, crossed_small, kept_small,
+    color_lines, color_tiles, colstage, colbuf, img, img7, fa, ft, sl, ycoef, xcoef, yfeat, xfeat, mixrow,
+    cgright, rowsum, colsum, cgacc, cgsend, cgbuf, cgsum, cgfin,
+    act, lnvec, lnsend, lnbuf, biasvec, vecsend, vecbuf, ivec, ivbuf,
     heads, probs, prob_grad, mix_s, mix_b, dmix_b, dqkv_s, dqkv_b,
-    weight_sem, x_send, x_recv, y_send, y_recv, g_send, g_recv, a_send, a_recv, r_send, r_recv,
+    weight_sem, x_send, x_recv, y_send, y_recv, g_send, g_recv, a_send, a_recv, r_send, r_recv, f_send, f_recv,
     misc_send, misc_recv,
 ):
     grid_rows, grid_cols, rows, steps, tile_rows, tile_cols = sizes
@@ -667,26 +668,38 @@
     )
     CQ, CO, C1, C2, SQ, SK, SV, SO, S1, S2 = range(10)
     loads = [pltpu.make_async_copy(s, wts.at[k], weight_sem.at[k]) for k, s in enumerate(sources)]
-    loads.append(pltpu.make_async_copy(w_input, win, weight_sem.at[10]))
+    loads.append(pltpu.make_async_copy(w_input, win_raw, weight_sem.at[10]))
     loads[CQ].start()
     loads[10].start()
 
+    color_lines[...] = jnp.zeros(color_lines.shape, f32)
+    for channel in range(3):
+        for col in range(tile_cols):
+            line = channel * tile_cols + col
+            shown = to_float(colors[channel, col])
+            for image in range(grid_rows):
+                color_lines[image, line : line + 1, :tile_rows] = shown[image : image + 1]
+    color_tiles[...] = narrow(color_lines[...])
     gc, bc = to_float(cross_gains[...]), to_float(cross_biases[...])
     gs, bs = to_float(self_gains[...]), to_float(self_biases[...])
-    gin, bin_ = input_gains[0:1], input_gains[1:2]
+    gains_here = [to_float(in_gain[...]), to_float(in_bias[...])]
+    gains_here = jnp.concatenate(gains_here + [jnp.zeros((6, in_gain.shape[1]), f32)], axis=0)
+    gains_here = own_dot(narrow(gains_here), order[...], 1, 1)
+    gin, bin_ = gains_here[0:1], gains_here[1:2]
     lat = to_float(latents[...])
     nq = norm_forward(lat, gc[0:1], bc[0:1])
     xbuf[0, core, quad] = nq
 
+    cot_low = cotangent[...]
     pl.semaphore_wait(barrier, n_dev - 1)
 
     def send_color(step, carry):
-        d = lax.rem(me + step, n_dev)
-        push(color_tiles.at[d // grid_cols], colbuf.at[me], misc_send.at[0], misc_recv.at[0], at_device(d))
+        image = lax.rem(z + step, grid_rows)
+        push(color_tiles.at[image], colstage.at[z], misc_send.at[5], misc_recv.at[5], {"rows": image})
         return carry
 
-    lax.fori_loop(1, n_dev, send_color, 0)
-    colbuf[me] = color_tiles[z]
+    lax.fori_loop(1, grid_rows, send_color, 0)
+    colstage[z] = color_tiles[z]
 
     def x_spread(block, sem):
         def one(step, carry):
@@ -703,8 +716,19 @@
     def x_arrived(half, sem):
         wait_for(half, y_recv.at[sem])
 
+    waiting = []
+    pieces = rows // 16
+
     def spread_x(k):
         x_spread(xbuf.at[k, core, quad], k)
+
+    def later_x(k):
+        waiting.extend((k, piece) for piece in range(pieces))
+
+    def background(count):
+        for k, piece in waiting[:count]:
+            x_spread(xbuf.at[k, core, quad, pl.ds(piece * 16, 16)], k)
+        del waiting[:count]
 
     def relay_x(k):
         x_relay(xbuf.at[k, core], k)
@@ -716,8 +740,22 @@
         peer = lax.rem(j + step, grid_cols)
         return peer, {"cols": peer}
 
+    def regroup(values):
+        tiles = [values[:, t * LANES : (t + 1) * LANES] for t in range(width // LANES)]
+        piece = lax.broadcasted_iota(jnp.int32, tiles[0].shape, 1) // own
+        result = []
+        for peer in range(grid_cols):
+            chunk_now = None
+            for part in range(grid_rows):
+                tile, offset = divmod((part * grid_cols + peer) * own, LANES)
+                shift = (part * own - offset) % LANES
+                moved = pltpu.roll(tiles[tile], shift, 1) if shift else tiles[tile]
+                chunk_now = moved if part == 0 else jnp.where(piece == part, moved, chunk_now)
+            result.append(chunk_now)
+        return jnp.concatenate(result, axis=1)
+
     def spread_g(k, values):
-        gsrc[k] = values
+        gsrc[k] = narrow(regroup(to_float(values)))
 
         def one(step, carry):
             peer, where = to_plane(step)
@@ -731,32 +769,57 @@
         wait_for(gsrc.at[k, :, pl.ds(0, chunk * (grid_cols - 1))], g_recv.at[k])
         return gbuf[k].reshape(grid_cols * rows, chunk)
 
-    def send_parts(src, dst, sem):
-        for part in range(grid_rows):
-            d = grid_rows * j + part
-            block = src.at[pl.ds(part * own, own)]
-
-            @pl.when(d != me)
-            def _():
-                push(block, dst.at[z], r_send.at[sem], r_recv.at[sem], at_device(d))
-
-            @pl.when(d == me)
-            def _():
-                pltpu.make_async_copy(block, dst.at[z], r_recv.at[sem]).start()
+    partner = z + 1 - 2 * lax.rem(z, 2)
+    across = lax.rem(z + 2, grid_rows)
+
+    def block_at(part):
+        return pl.ds(pl.multiple_of(part * own, own), own)
+
+    def send_parts(src, pair, sem):
+        for slot, part in enumerate((partner, lax.rem(partner + 2, grid_rows))):
+            push(src.at[block_at(part)], pair.at[slot], r_send.at[sem], r_recv.at[sem], {"rows": partner})
+
+    def join_parts(src, pair, hand, far, kept, sem):
+        wait_for(pair, r_recv.at[sem])
+        hand[...] = narrow(to_float(src[block_at(across)]) + to_float(pair[1]))
+        push(hand, far, f_send.at[sem], f_recv.at[sem], {"rows": across})
+        kept[...] = to_float(src[block_at(z)]) + to_float(pair[0])
+
+    def kept_of(m):
+        if m < 3:
+            return cross_total.at[m]
+        if m < 9:
+            return self_total.at[m - 4]
+        return self_out_total
+
+    def slot_of(m):
+        return m if m < 3 else m - 1
+
+    def join(m):
+        k = slot_of(m)
+        join_parts(staged.at[k], paired.at[k], handed.at[k], crossed.at[k], kept_of(m), m)
+
+    def join_small(m):
+        join_parts(
+            staged_small.at[m], paired_small.at[m], handed_small.at[m], crossed_small.at[m],
+            kept_small.at[m], 10 + m,
+        )
 
     def weight_part(m, right, left):
+        turned = jnp.transpose(right)
+
         def one(n, carry):
             at = pl.ds(pl.multiple_of(n * 256, 256), 256)
             block = left[:, :, :, at].reshape(grid_cols * rows, 256)
-            staged[m, :, at] = narrow(own_dot(right, block, 0, 0))
+            staged[slot_of(m), :, at] = narrow(own_dot(turned, block, 1, 0))
             return carry
 
-        lax.fori_loop(0, width // 256, one, 0)
-        send_parts(staged.at[m], arrived.at[m], m)
+        lax.fori_loop(0, width // 256, one, 0, unroll=4)
+        send_parts(staged.at[slot_of(m)], paired.at[slot_of(m)], m)
 
     def small_part(m, right, left):
         staged_small[m] = narrow(own_dot(right, left[...].reshape(grid_cols * rows, WIDE), 0, 0))
-        send_parts(staged_small.at[m], arrived_small.at[m], 10 + m)
+        send_parts(staged_small.at[m], paired_small.at[m], 10 + m)
 
     def times(x, k, out):
         def one(n, carry):
@@ -764,7 +827,7 @@
             out[:, at] = own_dot(x, wts[k, :, at], 1, 0)
             return carry
 
-        lax.fori_loop(0, width // 256, one, 0)
+        lax.fori_loop(0, width // 256, one, 0, unroll=4)
 
     def times_t(x, k, out, add=False):
         def one(n, carry):
@@ -773,20 +836,35 @@
             out[:, at] = out[:, at] + result if add else result
             return carry
 
-        lax.fori_loop(0, width // 256, one, 0)
-
-    FIRST, SECOND, THIRD, PRE_C, PRE_S, TMP, ATT, GRAD = range(8)
+        lax.fori_loop(0, width // 256, one, 0, unroll=4)
+
+    FIRST, SECOND, THIRD, PRE_C, PRE_S, TMP, ATT, GRAD, COT_BACK = range(9)
     tmp = act.at[TMP]
 
-    spread_x(0)
     loads[CQ].wait()
     for k in range(1, 10):
         loads[k].start()
     times(nq, CQ, tmp)
     query_low = narrow(tmp[...] + bc[2:3])
+    wait_for(colstage.at[pl.ds(0, grid_rows - 1)], misc_recv.at[5])
+
+    def send_strip(step, carry):
+        peer, where = to_plane(step)
+        push(colstage, colbuf.at[j], misc_send.at[0], misc_recv.at[0], where)
+        return carry
+
+    lax.fori_loop(1, grid_cols, send_strip, 0)
+    colbuf[j] = colstage[...]
+    spread_x(0)
     spread_g(7, query_low)
+    spread_g(5, cot_low)
     loads[10].wait()
+    for k in range(2):
+        win[k] = narrow(own_dot(order[...], win_raw[k], 1, 0))
     query_inputs = own_dot(query_low, win[0], 1, 1)
+    spare = pl.ds(2 * LANES, 16)
+    spare_row = lax.broadcasted_iota(jnp.int32, (16, width), 0)
+    win[1, spare, :] = narrow(jnp.where(spare_row == 5, bc[3:4], to_float(win[1, spare, :])))
 
     box = [boxes[z, k] for k in range(4)]
 
@@ -818,10 +896,10 @@
     x_here = -1.0 + 2.0 * to_float(x_lane - box[1]) / filled(box[3] - 1, (1, LANES))
     count = 3 + 2 + 4 * NBANDS
 
-    wait_for(colbuf.at[pl.ds(0, n_dev - 1)], misc_recv.at[0])
+    wait_for(colbuf.at[pl.ds(0, grid_cols - 1)], misc_recv.at[0])
     for part in range(grid_rows):
         at = pl.ds(part * tile_rows, tile_rows)
-        tiles = colbuf[part * grid_cols : (part + 1) * grid_cols].reshape(grid_cols * 32, LANES)
+        tiles = colbuf[:, part].reshape(grid_cols * 32, LANES)
         img[at, :] = own_dot(tiles, place[...], 0, 0)[:tile_rows]
     c0, c1, c2 = img[:, :LANES], img[:, LANES : 2 * LANES], img[:, 2 * LANES :]
     mean = (c0 + c1 + c2 + y_sum + x_sum) * (1.0 / count)
@@ -842,7 +920,7 @@
     for block in range(blocks):
         at = pl.ds(block * LANES, LANES)
         fa[block] = narrow(own_dot(img7[...], pick[:, at], 1, 0))
-        turned = own_dot(pick_t[at, :], img7[...], 1, 1)
+        turned = own_dot(pick[:, at], img7[...], 0, 1)
         line = lax.broadcasted_iota(jnp.int32, turned.shape, 0)
         ft[at, :] = narrow(jnp.where(lax.rem(line, 8) == 5, 1.0, turned))
 
@@ -925,7 +1003,7 @@
         sl[s] = lines
         return jnp.maximum(best, jnp.max(lines, axis=0, keepdims=True))
 
-    best = lax.fori_loop(0, steps, first_pass, jnp.full((1, LANES), -3e38, f32))
+    best = lax.fori_loop(0, steps, first_pass, jnp.full((1, LANES), -3e38, f32), unroll=4)
     best = jnp.maximum(best, other_half(best))
     rowsum[...] = jnp.zeros(rowsum.shape, f32)
     colsum[...] = jnp.zeros(colsum.shape, f32)
@@ -939,18 +1017,19 @@
         return total, found + step_sums(s, weights * deviation)
 
     total, found = lax.fori_loop(
-        0, steps, second_pass, (jnp.zeros((1, LANES), f32), jnp.zeros((8, LANES), f32))
+        0, steps, second_pass, (jnp.zeros((1, LANES), f32), jnp.zeros((8, LANES), f32)), unroll=4
     )
     total = total + other_half(total)
     log_total = best + jnp.log(total)
     plain_mixed = pixel_sums(found, 1.0 / total)
-    mixed_low = narrow(plain_mixed * gin + bin_)
+    wide1 = lax.broadcasted_iota(jnp.int32, (rows, WIDE), 1)
+    mixed_low = narrow(jnp.where(wide1 == 2 * LANES + 5, 1.0, plain_mixed * gin + bin_))
     xsmall[0, core, quad] = mixed_low
+    x_spread(xsmall.at[0, core, quad], 8)
     relay_x(0)
-    attended = own_dot(mixed_low, win[1], 1, 0) + bc[3:4]
+    attended = own_dot(mixed_low, win[1], 1, 0)
     act[ATT] = attended
     attended_low = narrow(attended)
-    xbuf[3, core, quad] = attended_low
     loads[CO].wait()
     times(attended_low, CO, tmp)
     first = lat + tmp[...] + bc[4:5]
@@ -970,11 +1049,13 @@
     normed_t = norm_forward(second, gs[0:1], bs[0:1])
     xbuf[4, core, quad] = normed_t
     spread_x(4)
+    later_x(1)
+    later_x(2)
+    background(SEND[0])
+    loads[S2].wait()
+    times_t(cot_low, S2, act.at[COT_BACK])
     relay_x(4)
-    x_spread(xsmall.at[0, core, quad], 8)
-    spread_x(3)
-    spread_x(1)
-    spread_x(2)
+    x_relay(xsmall.at[0, core], 8)
     have_x(4)
 
     for k in (SQ, SK, SV):
@@ -1017,39 +1098,34 @@
         return carry
 
     lax.fori_loop(1, grid_cols, send_mixed, 0)
+    background(SEND[1])
     mix_b[:, lanes_of(j)] = mix_s[mine]
-    relay_x(3)
-    relay_x(1)
-    relay_x(2)
-    x_relay(xsmall.at[0, core], 8)
     loads[SO].wait()
     wait_for(mix_b.at[:, pl.ds(0, chunk * (grid_cols - 1))], a_recv.at[0])
     mixed_rows = mix_b[...]
-    xbuf[7, core, quad] = mixed_rows
+    xbuf[3, core, quad] = mixed_rows
     times(mixed_rows, SO, tmp)
     third = act[SECOND] + tmp[...] + bs[4:5]
     act[THIRD] = third
     normed_s = norm_forward(third, gs[1:2], bs[1:2])
     xbuf[5, core, quad] = normed_s
-    spread_x(7)
+    later_x(5)
+    background(SEND[2])
     loads[S1].wait()
     times(normed_s, S1, tmp)
-    spread_x(5)
     pre = tmp[...] + bs[5:6]
     act[PRE_S] = pre
     hidden_s = narrow(gelu_value(pre))
     xbuf[6, core, quad] = hidden_s
-    spread_x(6)
-    loads[S2].wait()
+    waiting[:0] = [(6, piece) for piece in range(pieces)]
+    later_x(3)
+    background(SEND[3])
+    relay_x(1)
     times(hidden_s, S2, tmp)
     new_latents[...] = narrow(act[THIRD] + tmp[...] + bs[6:7])
 
-    cot_low = cotangent[...]
-    spread_g(5, cot_low)
-    times_t(cot_low, S2, tmp)
-    d_pre = tmp[...] * gelu_slope(act[PRE_S])
+    d_pre = act[COT_BACK] * gelu_slope(act[PRE_S])
     pre_low = narrow(d_pre)
-    spread_g(4, pre_low)
     times_t(pre_low, S1, tmp)
     d_rows, lnvec[6:7, :], lnvec[7:8, :] = norm_gradient(act[THIRD], gs[1:2], tmp[...])
     gradient = to_float(cot_low) + d_rows
@@ -1057,19 +1133,18 @@
     out_low = narrow(gradient)
     times_t(out_low, SO, tmp)
     mix_b2 = narrow(tmp[...])
-    gsrc[9] = mix_b2
+    gsrc[12] = mix_b2
 
     def send_dmixed(step, carry):
         peer, where = to_plane(step)
-        push(gsrc.at[9, :, lanes_of(peer)], dmix_b.at[mine], a_send.at[1], a_recv.at[1], where)
+        push(gsrc.at[12, :, lanes_of(peer)], dmix_b.at[mine], a_send.at[1], a_recv.at[1], where)
         return carry
 
     lax.fori_loop(1, grid_cols, send_dmixed, 0)
-    dmix_b[mine] = gsrc[9, :, lanes_of(j)]
+    dmix_b[mine] = gsrc[12, :, lanes_of(j)]
+    spread_g(4, pre_low)
     spread_g(6, out_low)
-    relay_x(7)
-    relay_x(5)
-    relay_x(6)
+    background(SEND[4])
     wait_for(dmix_b.at[pl.ds(0, grid_cols - 1)], a_recv.at[1])
 
     def head_backward(n, carry):
@@ -1085,9 +1160,9 @@
         d_query = own_dot(d_low, heads[1], 1, 0)
         for part in range(per // rows):
             dqkv_s[n * (per // rows) + part, 0] = narrow(d_query[part * rows : (part + 1) * rows])
-        return carry + jnp.sum(d_query, axis=0, keepdims=True)
-
-    query_bias = lax.fori_loop(0, head_rows // per, head_backward, jnp.zeros((1, chunk), f32))
+        return carry
+
+    lax.fori_loop(0, head_rows // per, head_backward, 0)
     d_mixed_all = dmix_b[...].reshape(head_rows, chunk)
 
     def head_keys(n, carry):
@@ -1098,9 +1173,9 @@
             cut = slice(part * rows, (part + 1) * rows)
             dqkv_s[n * (per // rows) + part, 1] = narrow(d_key[cut])
             dqkv_s[n * (per // rows) + part, 2] = narrow(d_value[cut])
-        return carry + jnp.sum(d_value, axis=0, keepdims=True)
-
-    value_bias = lax.fori_loop(0, head_rows // per, head_keys, jnp.zeros((1, chunk), f32))
+        return carry
+
+    lax.fori_loop(0, head_rows // per, head_keys, 0)
 
     def send_dqkv(step, carry):
         peer, where = to_plane(step)
@@ -1108,24 +1183,31 @@
         return carry
 
     lax.fori_loop(1, grid_cols, send_dqkv, 0)
+    background(SEND[5])
     dqkv_b[:, :, lanes_of(j)] = dqkv_s[mine]
 
     def column_sum(values):
         return jnp.sum(to_float(values), axis=0, keepdims=True)
 
+    relay_x(6)
     have_x(6)
     right = have_g(5)
     bias_s6 = column_sum(right)
     weight_part(8, right, xbuf.at[6])
+    wait_for(dqkv_b.at[:, :, pl.ds(0, chunk * (grid_cols - 1))], a_recv.at[2])
+    for k in range(3):
+        spread_g(9 + k, dqkv_b[k])
+    times_t(dqkv_b[0], SQ, tmp)
+    times_t(dqkv_b[1], SK, tmp, True)
+    times_t(dqkv_b[2], SV, tmp, True)
+    background(SEND[6])
+    relay_x(5)
+    relay_x(2)
     have_x(5)
     right = have_g(4)
     bias_s5 = column_sum(right)
     weight_part(7, right, xbuf.at[5])
-
-    wait_for(dqkv_b.at[:, :, pl.ds(0, chunk * (grid_cols - 1))], a_recv.at[2])
-    times_t(dqkv_b[0], SQ, tmp)
-    times_t(dqkv_b[1], SK, tmp, True)
-    times_t(dqkv_b[2], SV, tmp, True)
+    join(8)
     d_rows, lnvec[4:5, :], lnvec[5:6, :] = norm_gradient(act[SECOND], gs[0:1], tmp[...])
     gradient = act[GRAD] + d_rows
     act[GRAD] = gradient
@@ -1145,16 +1227,19 @@
     d_attended = narrow(tmp[...])
     spread_g(8, d_attended)
 
-    have_x(7)
-    right = have_g(6)
-    bias_s4 = column_sum(right)
-    weight_part(9, right, xbuf.at[7])
+    background(len(waiting))
     for k in range(3):
-        weight_part(4 + k, dqkv_s[:, k].reshape(head_rows, chunk), xbuf.at[4])
+        right = have_g(9 + k)
+        if k == 0:
+            bias_s2 = column_sum(right)
+        elif k == 2:
+            bias_s3 = column_sum(right)
+        weight_part(4 + k, right, xbuf.at[4])
+    join(7)
 
     grad_inputs = own_dot(d_attended, win[1], 1, 1)
     d_attended = to_float(d_attended)
-    shift = jnp.sum(d_attended * bc[3:4], axis=1, keepdims=True)
+    shift = grad_inputs[:, 2 * LANES + 5 : 2 * LANES + 6]
     row_delta = jnp.sum(d_attended * act[ATT], axis=1, keepdims=True) - shift
     grad_shift = jnp.sum(grad_inputs * bin_, axis=1, keepdims=True)
     grad_scaled = grad_inputs * gin
@@ -1202,9 +1287,34 @@
         total = total + jnp.sum(d_scores, axis=0, keepdims=True)
         return total, found + step_sums(s, d_scores * deviation)
 
-    total, found = lax.fori_loop(
-        0, steps, back_pass, (jnp.zeros((1, LANES), f32), jnp.zeros((8, LANES), f32))
-    )
+    carry = (jnp.zeros((1, LANES), f32), jnp.zeros((8, LANES), f32))
+    third_of = steps // 3
+    carry = lax.fori_loop(0, third_of, back_pass, carry, unroll=4)
+    relay_x(3)
+    for k in range(3):
+        join(4 + k)
+    have_x(3)
+    right = have_g(6)
+    bias_s4 = column_sum(right)
+    weight_part(9, right, xbuf.at[3])
+    carry = lax.fori_loop(third_of, 2 * third_of, back_pass, carry, unroll=4)
+    have_x(2)
+    right = have_g(2)
+    bias_c6 = column_sum(right)
+    weight_part(2, right, xbuf.at[2])
+    have_x(1)
+    right = have_g(1)
+    bias_c5 = column_sum(right)
+    weight_part(1, right, xbuf.at[1])
+    join(9)
+    x_arrived(xsmall.at[0, 1 - core], 8)
+    right = have_g(3)
+    bias_c4 = column_sum(right)
+    small_part(2, right, xsmall.at[0])
+    right = have_g(8)
+    bias_c3 = column_sum(right)
+    small_part(1, right, xsmall.at[0])
+    total, found = lax.fori_loop(2 * third_of, steps, back_pass, carry, unroll=4)
     plain_scores = pixel_sums(found, 1.0) * score_scale
     total = total * score_scale
     score_total = fold(jnp.transpose(jnp.concatenate([total, jnp.zeros((LANES - 1, LANES), f32)], axis=0)))[:, 0:1]
@@ -1222,7 +1332,8 @@
     spread_g(0, query_grad_low)
     gain_part = jnp.sum(query_inputs * plain_scores + grad_inputs * plain_mixed, axis=0, keepdims=True)
     bias_part = jnp.sum(query_inputs * score_total + grad_inputs, axis=0, keepdims=True)
-    ivec[...] = jnp.concatenate([gain_part, bias_part, jnp.zeros((6, WIDE), f32)], axis=0)
+    cuts = [part[:, k * LANES : (k + 1) * LANES] for part in (gain_part, bias_part) for k in range(3)]
+    ivec[...] = jnp.concatenate(cuts + [jnp.zeros((2, LANES), f32)], axis=0)
     ivbuf[me] = ivec[...]
 
     def send_ivec(step, carry):
@@ -1235,13 +1346,15 @@
     d_rows, lnvec[0:1, :], lnvec[1:2, :] = norm_gradient(to_float(latents[...]), gc[0:1], tmp[...])
     latent_grad[...] = act[GRAD] + d_rows
 
+    lnsend[...] = regroup(lnvec[...])
+
     def send_ln(step, carry):
         peer, where = to_plane(step)
-        push(lnvec.at[:, lanes_of(peer)], lnbuf.at[j], misc_send.at[2], misc_recv.at[2], where)
+        push(lnsend.at[:, lanes_of(peer)], lnbuf.at[j], misc_send.at[2], misc_recv.at[2], where)
         return carry
 
     lax.fori_loop(1, grid_cols, send_ln, 0)
-    lnbuf[j] = lnvec[:, lanes_of(j)]
+    lnbuf[j] = lnsend[:, lanes_of(j)]
 
     for block in range(blocks):
         both = own_dot(fa[block], spread[...], 1, 0)
@@ -1255,31 +1368,21 @@
         lines = jnp.concatenate([narrow(cgacc[block, at, :LANES]) for block in range(blocks)], axis=1)
         tiles = narrow(own_dot(back[...], lines, 1, 1))
         for tile in range(grid_cols):
-            cgsend[part * grid_cols + tile, :, :tile_rows] = tiles[tile * 32 : tile * 32 + 32]
-    cgbuf[me] = cgsend[me]
+            cgsend[tile, part, :, :tile_rows] = tiles[tile * 32 : tile * 32 + 32]
+    cgbuf[j] = cgsend[j]
 
     def send_cg(step, carry):
-        d = lax.rem(me + step, n_dev)
-        push(cgsend.at[d], cgbuf.at[me], misc_send.at[3], misc_recv.at[3], at_device(d))
+        peer, where = to_plane(step)
+        push(cgsend.at[peer], cgbuf.at[j], misc_send.at[3], misc_recv.at[3], where)
         return carry
 
-    lax.fori_loop(1, n_dev, send_cg, 0)
+    lax.fori_loop(1, grid_cols, send_cg, 0)
 
     x_relay(xsmall.at[1, core], 9)
-    for m, (left, g) in ((2, (2, 2)), (1, (1, 1)), (3, (3, 3))):
-        have_x(left)
-        right = have_g(g)
-        if m == 2:
-            bias_c6 = column_sum(right)
-        elif m == 1:
-            bias_c5 = column_sum(right)
-        else:
-            bias_c4 = column_sum(right)
-        weight_part(m, right, xbuf.at[left])
-    x_arrived(xsmall.at[0, 1 - core], 8)
-    right = have_g(8)
-    bias_c3 = column_sum(right)
-    small_part(1, right, xsmall.at[0])
+    for m in (2, 1):
+        join(m)
+    for m in (2, 1):
+        join_small(m)
     have_x(0)
     right = have_g(0)
     bias_c2 = column_sum(right)
@@ -1287,104 +1390,99 @@
     x_arrived(xsmall.at[1, 1 - core], 9)
     small_part(0, have_g(7), xsmall.at[1])
 
+    wait_for(cgbuf.at[pl.ds(0, grid_cols - 1)], misc_recv.at[3])
+    tiles = to_float(cgbuf[0])
+    for peer in range(1, grid_cols):
+        tiles = tiles + to_float(cgbuf[peer])
+    cgsum[...] = tiles
+
+    def send_tile(step, carry):
+        part = lax.rem(z + step, grid_rows)
+        push(cgsum.at[part], cgfin.at[z], misc_send.at[6], misc_recv.at[6], {"rows": part})
+        return carry
+
+    lax.fori_loop(1, grid_rows, send_tile, 0)
+    cgfin[z] = cgsum[z]
     wait_for(lnbuf.at[pl.ds(0, grid_cols - 1)], misc_recv.at[2])
     norms = lnbuf[0]
     for peer in range(1, grid_cols):
         norms = norms + lnbuf[peer]
     vecsend[...] = jnp.concatenate(
         [
-            norms, bias_c2, bias_c3, bias_c4, bias_c5, bias_c6, query_bias, value_bias,
+            norms, bias_c2, bias_c3, bias_c4, bias_c5, bias_c6, bias_s2, bias_s3,
             bias_s4, bias_s5, bias_s6, jnp.zeros((6, chunk), f32),
         ],
         axis=0,
     )
-    for part in range(grid_rows):
-        d = grid_rows * j + part
-
-        @pl.when(d != me)
-        def _():
-            push(vecsend, vecbuf.at[z], misc_send.at[4], misc_recv.at[4], at_device(d))
-
-        @pl.when(d == me)
-        def _():
-            pltpu.make_async_copy(vecsend, vecbuf.at[z], misc_recv.at[4]).start()
-
-    wait_for(cgbuf.at[pl.ds(0, n_dev - 1)], misc_recv.at[3])
-    for part in range(grid_rows):
-        tile = to_float(cgbuf[part * grid_cols])
-        for peer in range(1, grid_cols):
-            tile = tile + to_float(cgbuf[part * grid_cols + peer])
-        color_out[part] = tile
+
+    def send_vec(step, carry):
+        where = {"rows": lax.rem(z + step, grid_rows)}
+        push(vecsend, vecbuf.at[z], misc_send.at[4], misc_recv.at[4], where)
+        return carry
+
+    lax.fori_loop(1, grid_rows, send_vec, 0)
+    vecbuf[z] = vecsend[...]
+
+    wait_for(cgfin.at[pl.ds(0, grid_rows - 1)], misc_recv.at[6])
+    color_out[...] = cgfin[...]
     wait_for(ivbuf.at[pl.ds(0, n_dev - 1)], misc_recv.at[1])
     sums = ivbuf[0]
     for d in range(1, n_dev):
         sums = sums + ivbuf[d]
     input_vector_out[...] = sums
 
-    def gathered(ref):
-        result = to_float(ref[0])
-        for part in range(1, grid_rows):
-            result = result + to_float(ref[part])
-        return result
-
-    order = (8, 7, 9, 4, 5, 6, 2, 1, 3, 0)
-    for m in order:
-        wait_for(arrived.at[m], r_recv.at[m])
-        result = gathered(arrived.at[m])
-        if m < 3:
-            cross_total[m] = prior_cross[m] + result
-        elif m == 3:
-            out_total[...] = prior_out[...] + result
-        elif m < 9:
-            self_total[m - 4] = result
-        else:
-            self_out_total[...] = result
-    for m in (1, 0):
-        wait_for(arrived_small.at[m], r_recv.at[10 + m])
-        input_parts[m] = gathered(arrived_small.at[m])
-    wait_for(vecbuf, misc_recv.at[4])
-    vector_out[...] = gathered(vecbuf)
-
-    for k in range(8):
+    join(0)
+    join_small(0)
+    wait_for(vecbuf.at[pl.ds(0, grid_rows - 1)], misc_recv.at[4])
+    vectors = vecbuf[0]
+    for part in range(1, grid_rows):
+        vectors = vectors + vecbuf[part]
+    vector_out[...] = vectors
+    for m in (8, 7, 4, 5, 6, 9, 2, 1, 0):
+        wait_for(crossed.at[slot_of(m)], f_recv.at[m])
+        result = kept_of(m)[...] + to_float(crossed[slot_of(m)])
+        kept_of(m)[...] = result
+    sums = []
+    for m in (2, 1, 0):
+        wait_for(crossed_small.at[m], f_recv.at[10 + m])
+        sums.append(kept_small[m] + to_float(crossed_small[m]))
+    out_total[...] = own_dot(narrow(sums[0]), win[1], 1, 0)
+    input_parts[1] = sums[1]
+    input_parts[0] = sums[2]
+
+    for k in range(7):
         wait_for(xbuf.at[k, 0, pl.ds(0, quads - 1)], x_send.at[k])
         wait_for(xbuf.at[k, 0], y_send.at[k])
     for k in range(2):
         wait_for(xsmall.at[k, 0, pl.ds(0, quads - 1)], x_send.at[8 + k])
         wait_for(xsmall.at[k, 0], y_send.at[8 + k])
-    for k in range(9):
+    for k in range(12):
         wait_for(gsrc.at[k, :, pl.ds(0, chunk * (grid_cols - 1))], g_send.at[k])
     wait_for(mix_s.at[pl.ds(0, grid_cols - 1)], a_send.at[0])
     wait_for(dmix_b.at[pl.ds(0, grid_cols - 1)], a_send.at[1])
     wait_for(dqkv_s.at[pl.ds(0, grid_cols - 1)], a_send.at[2])
-    wait_for(colbuf.at[pl.ds(0, n_dev - 1)], misc_send.at[0])
+    wait_for(colbuf.at[pl.ds(0, grid_cols - 1)], misc_send.at[0])
     wait_for(ivbuf.at[pl.ds(0, n_dev - 1)], misc_send.at[1])
     wait_for(lnbuf.at[pl.ds(0, grid_cols - 1)], misc_send.at[2])
-    wait_for(cgbuf.at[pl.ds(0, n_dev - 1)], misc_send.at[3])
-    away_from_me = me // grid_rows != j
-
-    @pl.when(away_from_me)
-    def _():
-        for m in range(10):
-            wait_for(staged.at[m], r_send.at[m])
-        for m in range(2):
-            wait_for(staged_small.at[m], r_send.at[10 + m])
-        wait_for(vecbuf, misc_send.at[4])
-
-    @pl.when(jnp.logical_not(away_from_me))
-    def _():
-        for m in range(10):
-            wait_for(staged.at[m, pl.ds(0, chunk - own)], r_send.at[m])
-        for m in range(2):
-            wait_for(staged_small.at[m, pl.ds(0, chunk - own)], r_send.at[10 + m])
-        wait_for(vecbuf.at[pl.ds(0, grid_rows - 1)], misc_send.at[4])
-
-
-def by_kind(rows):
+    wait_for(cgbuf.at[pl.ds(0, grid_cols - 1)], misc_send.at[3])
+    wait_for(colstage.at[pl.ds(0, grid_rows - 1)], misc_send.at[5])
+    wait_for(cgfin.at[pl.ds(0, grid_rows - 1)], misc_send.at[6])
+    for m in (0, 1, 2, 4, 5, 6, 7, 8, 9):
+        wait_for(paired.at[slot_of(m)], r_send.at[m])
+        wait_for(handed.at[slot_of(m)], f_send.at[m])
+    for m in range(3):
+        wait_for(paired_small.at[m], r_send.at[10 + m])
+        wait_for(handed_small.at[m], f_send.at[10 + m])
+    wait_for(vecbuf.at[pl.ds(0, grid_rows - 1)], misc_send.at[4])
+
+
+def channel_order(count):
     n = NBANDS
-    parts = [rows[:, 5 : 5 + n], rows[:, 5 + 2 * n : 5 + 3 * n], rows[:, 5 + n : 5 + 2 * n]]
-    parts += [rows[:, 5 + 3 * n :], rows[:, :5]]
-    spare = WIDE - rows.shape[1]
-    return jnp.pad(jnp.concatenate(parts, axis=1), ((0, 0), (0, spare)) + ((0, 0),) * (rows.ndim - 2))
+    starts = ((5, n), (5 + 2 * n, n), (5 + n, n), (5 + 3 * n, n), (0, 5))
+    order = np.concatenate([np.arange(start, start + size) for start, size in starts])
+    result = np.zeros((WIDE, count), np.float32)
+    result[np.arange(count), order] = 1
+    return np.asarray(result, ml_dtypes.bfloat16)
 
 
 def by_channel(lines):
@@ -1392,6 +1490,43 @@
     parts = [lines[..., 4 * n : 4 * n + 5], lines[..., :n], lines[..., 2 * n : 3 * n]]
     parts += [lines[..., n : 2 * n], lines[..., 3 * n : 4 * n]]
     return jnp.concatenate(parts, axis=-1)
+
+
+def finish_kernel(
+    own, tile_rows, tile_cols,
+    latents, latent_grad, colors, cross, out, self_parts, self_out, inputs, vectors, input_vectors,
+    prior_cross, prior_out, prior_input,
+    o_latents, o_latent_grad, o_colors, o_cross, o_out, o_input, o_gain, o_bias,
+    o_cross_gains, o_cross_biases, o_self, o_self_out, o_self_gains, o_self_biases,
+):
+    o_latents[...] = latents[...]
+    o_latent_grad[...] = latent_grad[...]
+    for channel in range(3):
+        for col in range(tile_cols):
+            line = channel * tile_cols + col
+            for image in range(colors.shape[0]):
+                o_colors[channel, col, image : image + 1, :] = colors[image, line : line + 1, :tile_rows]
+    o_cross[...] = prior_cross[...] + cross[...]
+    o_out[...] = prior_out[...] + out[...]
+    o_self[...] = self_parts[...]
+    o_self_out[...] = self_out[...]
+    for k in range(2):
+        o_input[k] = prior_input[k] + by_channel(inputs[k])
+    lines = input_vectors[...]
+    for k, target in enumerate((o_gain, o_bias)):
+        wide = jnp.concatenate([lines[3 * k + t : 3 * k + t + 1] for t in range(3)], axis=1)
+        target[...] = by_channel(wide)
+    place = lax.axis_index("rows")
+    width = vectors.shape[1]
+    mine = pltpu.roll(vectors[...], lax.rem(width - place * own, width), 1)[:, :own]
+    for target, rows in (
+        (o_cross_gains, (0, 2)),
+        (o_cross_biases, (1, 3, 8, 9, 10, 11, 12)),
+        (o_self_gains, (4, 6)),
+        (o_self_biases, (5, 7, 13, 14, 15, 16, 17)),
+    ):
+        for k, row in enumerate(rows):
+            target[k : k + 1, :] = mine[row : row + 1]
 
 
 def local_kernel(
@@ -1424,18 +1559,10 @@
     chunk = width // grid_cols
     own = chunk // grid_rows
     quads = grid_cols // 2
-    place, pick, pick_t, spread, back = selections(tile_cols, grid_cols, steps)
+    place, pick, spread, back = selections(tile_cols, grid_cols, steps)
     blocks = back.shape[1] // LANES
     held_rows = -(-steps // 8) * 8
-    color_tiles = jnp.transpose(pixel_colors, (1, 0, 3, 2)).reshape(
-        image_count, channels * tile_cols, tile_rows
-    )
-    color_tiles = jnp.pad(
-        color_tiles, ((0, 0), (0, 32 - channels * tile_cols), (0, LANES - tile_rows))
-    )
-    w_input = by_kind(input_matrices)
-    input_gains = by_kind(to_float(jnp.stack([in_gain, in_bias])))
-    input_gains = jnp.pad(input_gains, ((0, 6), (0, 0)))
+    order = channel_order(input_matrices.shape[1])
     f32, bf16 = jnp.float32, jnp.bfloat16
     vmem = pl.BlockSpec(memory_space=pltpu.VMEM)
     away = pl.BlockSpec(memory_space=pl.ANY)
@@ -1445,15 +1572,24 @@
     scratch = [
         ((10, width, width), bf16),
         ((2, WIDE, width), bf16),
-        ((8, 2, quads, rows, width), bf16),
+        (input_matrices.shape, bf16),
+        ((7, 2, quads, rows, width), bf16),
         ((2, 2, quads, rows, WIDE), bf16),
-        ((10, rows, width), bf16),
-        ((9, 2, quads, rows, chunk), bf16),
-        ((10, chunk, width), bf16),
-        ((10, grid_rows, own, width), bf16),
-        ((2, chunk, WIDE), bf16),
-        ((2, grid_rows, own, WIDE), bf16),
-        ((n_dev, 32, LANES), bf16),
+        ((13, rows, width), bf16),
+        ((12, 2, quads, rows, chunk), bf16),
+        ((9, chunk, width), bf16),
+        ((9, 2, own, width), bf16),
+        ((9, own, width), bf16),
+        ((9, own, width), bf16),
+        ((3, chunk, WIDE), bf16),
+        ((3, 2, own, WIDE), bf16),
+        ((3, own, WIDE), bf16),
+        ((3, own, WIDE), bf16),
+        ((3, own, WIDE), f32),
+        ((grid_rows, 32, LANES), f32),
+        ((grid_rows, 32, LANES), bf16),
+        ((grid_rows, 32, LANES), bf16),
+        ((grid_cols, grid_rows, 32, LANES), bf16),
         ((tall, WIDE), f32),
         ((tall, 7 * LANES), bf16),
         ((blocks, tall, LANES), bf16),
@@ -1468,16 +1604,19 @@
         ((tall, LANES), f32),
         ((held_rows, LANES), f32),
         ((blocks, tall, 2 * LANES), f32),
-        ((n_dev, 32, LANES), bf16),
-        ((n_dev, 32, LANES), bf16),
-        ((8, rows, width), f32),
+        ((grid_cols, grid_rows, 32, LANES), bf16),
+        ((grid_cols, grid_rows, 32, LANES), bf16),
+        ((grid_rows, 32, LANES), f32),
+        ((grid_rows, 32, LANES), f32),
+        ((9, rows, width), f32),
+        ((8, width), f32),
         ((8, width), f32),
         ((grid_cols, 8, chunk), f32),
         ((8, width), f32),
         ((24, chunk), f32),
         ((grid_rows, 24, chunk), f32),
-        ((8, WIDE), f32),
-        ((n_dev, 8, WIDE), f32),
+        ((8, LANES), f32),
+        ((n_dev, 8, LANES), f32),
         ((3, grid_cols * rows, chunk), bf16),
         ((grid_cols * rows, grid_cols * rows), f32),
         ((2, grid_cols * rows, grid_cols * rows), bf16),
@@ -1488,7 +1627,7 @@
         ((3, rows, width), bf16),
     ]
     scratch = [pltpu.VMEM(dims, kind) for dims, kind in scratch]
-    scratch += [dma((count,)) for count in (11, 10, 10, 10, 10, 9, 9, 3, 3, 12, 12, 5, 5)]
+    scratch += [dma((count,)) for count in (11, 10, 10, 10, 10, 12, 12, 3, 3, 13, 13, 13, 13, 7, 7)]
     outs = [
         ((rows, width), bf16),
         ((rows, width), f32),
@@ -1499,12 +1638,12 @@
         ((own, width), f32),
         ((2, own, WIDE), f32),
         ((24, chunk), f32),
-        ((8, WIDE), f32),
+        ((8, LANES), f32),
     ]
     results = pl.pallas_call(
         functools.partial(layer_kernel, sizes),
         out_shape=[shape(dims, kind) for dims, kind in outs],
-        in_specs=[pl.BlockSpec(memory_space=pltpu.SMEM)] + [vmem] * 15 + [away] * 5,
+        in_specs=[pl.BlockSpec(memory_space=pltpu.SMEM)] + [vmem] * 14 + [away] * 5,
         out_specs=[vmem] * len(outs),
         scratch_shapes=scratch,
         compiler_params=pltpu.CompilerParams(
@@ -1517,49 +1656,70 @@
         image_boxes,
         latents,
         cotangent,
-        color_tiles,
-        input_gains,
+        jnp.transpose(pixel_colors, (0, 3, 1, 2)),
+        in_gain.reshape(1, -1),
+        in_bias.reshape(1, -1),
+        order,
         cross_gains,
         cross_biases,
         self_gains,
         self_biases,
         place,
         pick,
-        pick_t,
         spread,
         back,
-        jnp.transpose(prior_cross_matrices, (0, 2, 1)),
-        jnp.transpose(prior_cross_out),
         cross_matrices,
         cross_out,
         self_matrices,
         self_out,
-        w_input,
-    )
-    new_latents, latent_grad, colors, cross_total, out_total = results[:5]
-    self_total, self_out_total, input_parts, vectors, input_vectors = results[5:]
-    me = lax.axis_index("rows") * grid_cols + lax.axis_index("cols")
-    vectors = lax.dynamic_slice_in_dim(vectors, lax.rem(me, grid_rows) * own, own, axis=1)
-    colors = colors[:, : channels * tile_cols, :tile_rows].reshape(
-        image_count, channels, tile_cols, tile_rows
-    )
-    input_total = prior_input_matrices + jnp.transpose(by_channel(input_parts), (0, 2, 1))
-    input_vectors = by_channel(input_vectors[:2])
+        input_matrices,
+    )
+    count = input_matrices.shape[1]
+    last = [
+        ((rows, width), bf16),
+        ((rows, width), f32),
+        ((channels, tile_cols, image_count, tile_rows), f32),
+        ((3, own, width), f32),
+        ((own, width), f32),
+        ((2, own, count), f32),
+        ((1, count), f32),
+        ((1, count), f32),
+        ((2, own), f32),
+        ((7, own), f32),
+        ((5, own, width), f32),
+        ((own, width), f32),
+        ((2, own), f32),
+        ((7, own), f32),
+    ]
+    done = pl.pallas_call(
+        functools.partial(finish_kernel, own, tile_rows, tile_cols),
+        out_shape=[shape(dims, kind) for dims, kind in last],
+        in_specs=[vmem] * (len(outs) + 3),
+        out_specs=[vmem] * len(last),
+        compiler_params=pltpu.CompilerParams(vmem_limit_bytes=VMEM_BYTES),
+    )(
+        *results,
+        jnp.transpose(prior_cross_matrices, (0, 2, 1)),
+        jnp.transpose(prior_cross_out),
+        jnp.transpose(prior_input_matrices, (0, 2, 1)),
+    )
+    (new_latents, latent_grad, colors, cross_total, out_total, input_total, gain, bias) = done[:8]
+    cross_gain, cross_bias, self_total, self_out_total, self_gain, self_bias = done[8:]
     return (
         new_latents,
         latent_grad,
-        jnp.transpose(colors, (1, 0, 3, 2)),
+        jnp.transpose(colors, (0, 2, 3, 1)),
         jnp.transpose(cross_total, (0, 2, 1)),
         jnp.transpose(out_total),
-        input_total,
-        input_vectors[0],
-        input_vectors[1],
-        jnp.stack([vectors[0], vectors[2]]),
-        jnp.concatenate([vectors[1:2], vectors[3:4], vectors[8:13]]),
+        jnp.transpose(input_total, (0, 2, 1)),
+        gain[0],
+        bias[0],
+        cross_gain,
+        cross_bias,
         jnp.transpose(self_total, (0, 2, 1)),
         jnp.transpose(self_out_total),
-        jnp.stack([vectors[4], vectors[6]]),
-        jnp.concatenate([vectors[5:6], vectors[7:8], vectors[13:18]]),
+        self_gain,
+        self_bias,
     )
 
 

time: 317 us -> 143 us (0.45)
  Pallas kernels: 296 us -> 135 us
  local copies, waits for them, and re-layouts: 17.6 us -> 5 us
    pallas_call x1, Pallas kernels: 296 us -> 132 us  [local_kernel(): pl.pallas_call(functools.partial(layer_kernel, sizes), out_shape=[shape(d...]
    slice x13 -> x0, local copies, waits for them, and re-layouts: 8.07 us -> none  [the longest x5 2.48 us: by_kind(): parts += [rows[:, 5 + 3 * n:], rows[:, :5]]]
where the time goes in v3:
time: 143 us
  Pallas kernels  135 us (94%)
  local copies, waits for them, and re-layouts  5 us (3%)
  other arithmetic  2.55 us (2%)
    pallas_call x1, Pallas kernels, local_kernel(): pl.pallas_call(functools.partial(layer_kernel, sizes), out_shape=[shape(d...  132 us
    pallas_call x1, Pallas kernels, local_kernel(): pl.pallas_call(functools.partial(finish_kernel, own, tile_rows, tile_cols...  2.94 us

profile of v3, /device:TPU:0, one launch (start us, length us, event | category | flops | bytes accessed | tf_op | source)
XLA Modules:
  0.0 143.0 jit_solution(7741318074482448963)
XLA Ops:
  0.6 1.2 reshape.34.in_gain
  1.9 1.2 reshape.35.in_bias
  3.1 2.5 %copy.37.w_input = bf16[2,261,1024]{2,1,0:T(8,128)(2,1)} copy(bf16[2,261,1024]{2,0,1:T(2,128)(2,1)} %param.29) | data formatting | bytes 2138112 | tf_op args[6]
  5.6 131.9 %shard_map.326 = (bf16[64,1024]{1,0:T(8,128)(2,1)}, f32[64,1024]{1,0:T(8,128)}, f32[4,32,128]{2,1,0:T(8,128)}, f32[3,32,1024]{2,1,0:T(8,128)}, f32[32,1024]{1,0:...) custom-call(s32[4,4]{1,0:T(4,128)} %boxes.1, ...), custom_call_target="tpu_custom_call" | custom-call | flops 20000000000 | bytes 40000000 | tf_op jit(solution)/shard_map/pallas_call | solution.py:1643
  137.5 2.9 %shard_map.327 = (bf16[64,1024]{1,0:T(8,128)(2,1)}, f32[64,1024]{1,0:T(8,128)}, f32[3,9,4,72]{3,2,1,0:T(4,128)}, f32[3,32,1024]{2,1,0:T(8,128)}, f32[32,1024]{1,...) custom-call(bf16[64,1024]{1,0:T(8,128)(2,1)} %get-tuple-element.38.l, ...), custom_call_target="tpu_custom_call" | custom-call | tf_op jit(solution)/shard_map/pallas_call | solution.py:1694
  140.5 1.3 reduce
  141.7 1.3 reduce.1

commit v4 on v3

--- a/solution.py
+++ b/solution.py
@@ -19,7 +19,7 @@
 NEG = -1e30
 FREQ_TOP = 112.0
 VMEM_BYTES = 63 * 1024 * 1024
-SEND = (4, 2, 0, 4, 4, 4, 4)
+PLAN = {0: ((4, 4),), 1: ((1, 2),), 3: ((5, 2),), 4: ((5, 2),), 5: ((1, 2),), 8: ((3, 4),)}
 
 
 def narrow(values):
@@ -509,6 +509,7 @@
 
 
 STEPS_HELD = 8
+GROUP = 4
 LANES = 128
 MESH = pl.DeviceIdType.MESH
 WIDE = 3 * LANES
@@ -614,9 +615,10 @@
     new_latents, latent_grad, color_out, cross_total, out_total, self_total, self_out_total,
     input_parts, vector_out, input_vector_out,
     wts, win, win_raw, xbuf, xsmall, gsrc, gbuf, staged, paired, handed, crossed, staged_small, paired_small, handed_small, crossed_small, kept_small,
+    row_pair, row_hand, row_cross, row_kept, row_turned, row_done, biases,
     color_lines, color_tiles, colstage, colbuf, img, img7, fa, ft, sl, ycoef, xcoef, yfeat, xfeat, mixrow,
     cgright, rowsum, colsum, cgacc, cgsend, cgbuf, cgsum, cgfin,
-    act, lnvec, lnsend, lnbuf, biasvec, vecsend, vecbuf, ivec, ivbuf,
+    act, lnvec, lnsend, lnbuf, biasvec, vecsend, vecbuf,
     heads, probs, prob_grad, mix_s, mix_b, dmix_b, dqkv_s, dqkv_b,
     weight_sem, x_send, x_recv, y_send, y_recv, g_send, g_recv, a_send, a_recv, r_send, r_recv, f_send, f_recv,
     misc_send, misc_recv,
@@ -654,13 +656,18 @@
 
     barrier = pltpu.get_barrier_semaphore()
 
-    def greet(step, carry):
-        pl.semaphore_signal(
-            barrier, inc=1, device_id=at_device(lax.rem(me + step, n_dev)), device_id_type=MESH
-        )
+    def greet_plane(step, carry):
+        where = {"cols": lax.rem(j + step, grid_cols)}
+        pl.semaphore_signal(barrier, inc=1, device_id=where, device_id_type=MESH)
         return carry
 
-    lax.fori_loop(1, n_dev, greet, 0)
+    def greet_line(step, carry):
+        where = {"rows": lax.rem(z + step, grid_rows)}
+        pl.semaphore_signal(barrier, inc=1, device_id=where, device_id_type=MESH)
+        return carry
+
+    lax.fori_loop(1, grid_rows, greet_line, 0)
+    lax.fori_loop(1, grid_cols, greet_plane, 0)
 
     sources = (
         [w_cross.at[0], w_out, w_cross.at[1], w_cross.at[2]]
@@ -682,16 +689,17 @@
     color_tiles[...] = narrow(color_lines[...])
     gc, bc = to_float(cross_gains[...]), to_float(cross_biases[...])
     gs, bs = to_float(self_gains[...]), to_float(self_biases[...])
-    gains_here = [to_float(in_gain[...]), to_float(in_bias[...])]
-    gains_here = jnp.concatenate(gains_here + [jnp.zeros((6, in_gain.shape[1]), f32)], axis=0)
+    gains_here = [to_float(ref[...]).reshape(1, -1) for ref in (in_gain, in_bias)]
+    gains_here = jnp.concatenate(gains_here + [jnp.zeros((6, in_gain.shape[0]), f32)], axis=0)
     gains_here = own_dot(narrow(gains_here), order[...], 1, 1)
     gin, bin_ = gains_here[0:1], gains_here[1:2]
     lat = to_float(latents[...])
     nq = norm_forward(lat, gc[0:1], bc[0:1])
     xbuf[0, core, quad] = nq
-
     cot_low = cotangent[...]
-    pl.semaphore_wait(barrier, n_dev - 1)
+    xbuf[6, core, quad] = cot_low
+    biases[...] = jnp.concatenate([bc, jnp.zeros((1, width), f32)], axis=0)
+    pl.semaphore_wait(barrier, grid_cols + grid_rows - 2)
 
     def send_color(step, carry):
         image = lax.rem(z + step, grid_rows)
@@ -716,19 +724,17 @@
     def x_arrived(half, sem):
         wait_for(half, y_recv.at[sem])
 
-    waiting = []
     pieces = rows // 16
+    sent = {}
 
     def spread_x(k):
         x_spread(xbuf.at[k, core, quad], k)
 
-    def later_x(k):
-        waiting.extend((k, piece) for piece in range(pieces))
-
-    def background(count):
-        for k, piece in waiting[:count]:
-            x_spread(xbuf.at[k, core, quad, pl.ds(piece * 16, 16)], k)
-        del waiting[:count]
+    def background(point):
+        for k, count in PLAN.get(point, ()):
+            for piece in range(sent.get(k, 0), sent.get(k, 0) + count):
+                x_spread(xbuf.at[k, core, quad, pl.ds(piece * 16, 16)], k)
+            sent[k] = sent.get(k, 0) + count
 
     def relay_x(k):
         x_relay(xbuf.at[k, core], k)
@@ -755,7 +761,10 @@
         return jnp.concatenate(result, axis=1)
 
     def spread_g(k, values):
-        gsrc[k] = narrow(regroup(to_float(values)))
+        spread_plain(k, narrow(regroup(to_float(values))))
+
+    def spread_plain(k, values):
+        gsrc[k] = values
 
         def one(step, carry):
             peer, where = to_plane(step)
@@ -799,6 +808,44 @@
         k = slot_of(m)
         join_parts(staged.at[k], paired.at[k], handed.at[k], crossed.at[k], kept_of(m), m)
 
+    def columns_of(part):
+        size = width // grid_rows
+        return pl.ds(pl.multiple_of(part * size, size), size)
+
+    def send_rows(src, sem):
+        for slot, part in enumerate((partner, lax.rem(partner + 2, grid_rows))):
+            push(src.at[:, columns_of(part)], row_pair.at[slot], r_send.at[sem], r_recv.at[sem], {"rows": partner})
+
+    def join_rows(src, sem):
+        wait_for(row_pair, r_recv.at[sem])
+        row_hand[...] = narrow(to_float(src[:, columns_of(across)]) + to_float(row_pair[1]))
+        push(row_hand, row_cross, f_send.at[sem], f_recv.at[sem], {"rows": across})
+        row_kept[...] = to_float(src[:, columns_of(z)]) + to_float(row_pair[0])
+
+    def finish_rows(sem):
+        wait_for(row_cross, f_recv.at[sem])
+        row_turned[...] = jnp.transpose(row_kept[...] + to_float(row_cross[...]))
+
+        def one(step, carry):
+            peer, where = to_plane(step)
+            push(row_turned.at[block_at(peer)], row_done.at[:, lanes_of(j)], a_send.at[3], a_recv.at[3], where)
+            return carry
+
+        lax.fori_loop(1, grid_cols, one, 0)
+        row_done[:, lanes_of(j)] = row_turned[block_at(j)]
+
+    def recompute(source, target, k, bias):
+        half = grid_cols * rows // 2
+
+        def one(n, carry):
+            at = pl.ds(pl.multiple_of(lax.rem(n, 4) * 256, 256), 256)
+            x = xbuf[source, n // 4].reshape(half, width)
+            pre = own_dot(x, wts[k, :, at], 1, 0) + bias[:, at]
+            xbuf[target, n // 4, :, :, at] = narrow(gelu_value(pre)).reshape(quads, rows, 256)
+            return carry
+
+        lax.fori_loop(0, 8, one, 0, unroll=2)
+
     def join_small(m):
         join_parts(
             staged_small.at[m], paired_small.at[m], handed_small.at[m], crossed_small.at[m],
@@ -815,7 +862,10 @@
             return carry
 
         lax.fori_loop(0, width // 256, one, 0, unroll=4)
-        send_parts(staged.at[slot_of(m)], paired.at[slot_of(m)], m)
+        if m == 8:
+            send_rows(staged.at[slot_of(m)], m)
+        else:
+            send_parts(staged.at[slot_of(m)], paired.at[slot_of(m)], m)
 
     def small_part(m, right, left):
         staged_small[m] = narrow(own_dot(right, left[...].reshape(grid_cols * rows, WIDE), 0, 0))
@@ -841,23 +891,23 @@
     FIRST, SECOND, THIRD, PRE_C, PRE_S, TMP, ATT, GRAD, COT_BACK = range(9)
     tmp = act.at[TMP]
 
+    wait_for(colstage.at[pl.ds(0, grid_rows - 1)], misc_recv.at[5])
+
+    def send_strip(step, carry):
+        peer, where = to_plane(step)
+        push(colstage, colbuf.at[j], misc_send.at[0], misc_recv.at[0], where)
+        return carry
+
+    lax.fori_loop(1, grid_cols, send_strip, 0)
+    colbuf[j] = colstage[...]
     loads[CQ].wait()
     for k in range(1, 10):
         loads[k].start()
     times(nq, CQ, tmp)
     query_low = narrow(tmp[...] + bc[2:3])
-    wait_for(colstage.at[pl.ds(0, grid_rows - 1)], misc_recv.at[5])
-
-    def send_strip(step, carry):
-        peer, where = to_plane(step)
-        push(colstage, colbuf.at[j], misc_send.at[0], misc_recv.at[0], where)
-        return carry
-
-    lax.fori_loop(1, grid_cols, send_strip, 0)
-    colbuf[j] = colstage[...]
     spread_x(0)
     spread_g(7, query_low)
-    spread_g(5, cot_low)
+    spread_x(6)
     loads[10].wait()
     for k in range(2):
         win[k] = narrow(own_dot(order[...], win_raw[k], 1, 0))
@@ -895,34 +945,6 @@
     x_lane = lax.broadcasted_iota(jnp.int32, (1, LANES), 1)
     x_here = -1.0 + 2.0 * to_float(x_lane - box[1]) / filled(box[3] - 1, (1, LANES))
     count = 3 + 2 + 4 * NBANDS
-
-    wait_for(colbuf.at[pl.ds(0, grid_cols - 1)], misc_recv.at[0])
-    for part in range(grid_rows):
-        at = pl.ds(part * tile_rows, tile_rows)
-        tiles = colbuf[:, part].reshape(grid_cols * 32, LANES)
-        img[at, :] = own_dot(tiles, place[...], 0, 0)[:tile_rows]
-    c0, c1, c2 = img[:, :LANES], img[:, LANES : 2 * LANES], img[:, 2 * LANES :]
-    mean = (c0 + c1 + c2 + y_sum + x_sum) * (1.0 / count)
-    square = (c0 * c0 + c1 * c1 + c2 * c2 + y_place * y_place + x_here * x_here + 2.0 * NBANDS) * (
-        1.0 / count
-    )
-    dev = lax.rsqrt(square - mean * mean + EPS)
-    mean_low, dev_low = narrow(mean), narrow(dev)
-    img7[...] = jnp.concatenate(
-        [
-            narrow(c0), narrow(c1), narrow(c2),
-            mean_low, narrow(mean - to_float(mean_low)),
-            dev_low, narrow(dev - to_float(dev_low)),
-        ],
-        axis=1,
-    )
-    blocks = fa.shape[0]
-    for block in range(blocks):
-        at = pl.ds(block * LANES, LANES)
-        fa[block] = narrow(own_dot(img7[...], pick[:, at], 1, 0))
-        turned = own_dot(pick[:, at], img7[...], 0, 1)
-        line = lax.broadcasted_iota(jnp.int32, turned.shape, 0)
-        ft[at, :] = narrow(jnp.where(lax.rem(line, 8) == 5, 1.0, turned))
 
     lane1 = lax.broadcasted_iota(jnp.int32, (rows, LANES), 1)
     lane_half = lax.broadcasted_iota(jnp.int32, (8, LANES), 1) // rows
@@ -961,6 +983,40 @@
         )
         return turned
 
+    query_scaled = query_inputs * gin * score_scale
+    coefficients(query_scaled, 0.0)
+    ycoef[...] += row_out
+    half_lane = lax.broadcasted_iota(jnp.int32, (held_rows, LANES), 1) // rows
+    xcoef[...] += jnp.where(half_lane == 0, col_out[0], col_out[1])
+
+    wait_for(colbuf.at[pl.ds(0, grid_cols - 1)], misc_recv.at[0])
+    for part in range(grid_rows):
+        at = pl.ds(part * tile_rows, tile_rows)
+        tiles = colbuf[:, part].reshape(grid_cols * 32, LANES)
+        img[at, :] = own_dot(tiles, place[...], 0, 0)[:tile_rows]
+    c0, c1, c2 = img[:, :LANES], img[:, LANES : 2 * LANES], img[:, 2 * LANES :]
+    mean = (c0 + c1 + c2 + y_sum + x_sum) * (1.0 / count)
+    square = (c0 * c0 + c1 * c1 + c2 * c2 + y_place * y_place + x_here * x_here + 2.0 * NBANDS) * (
+        1.0 / count
+    )
+    dev = lax.rsqrt(square - mean * mean + EPS)
+    mean_low, dev_low = narrow(mean), narrow(dev)
+    img7[...] = jnp.concatenate(
+        [
+            narrow(c0), narrow(c1), narrow(c2),
+            mean_low, narrow(mean - to_float(mean_low)),
+            dev_low, narrow(dev - to_float(dev_low)),
+        ],
+        axis=1,
+    )
+    blocks = fa.shape[0]
+    for block in range(blocks):
+        at = pl.ds(block * LANES, LANES)
+        fa[block] = narrow(own_dot(img7[...], pick[:, at], 1, 0))
+        turned = own_dot(pick[:, at], img7[...], 0, 1)
+        line = lax.broadcasted_iota(jnp.int32, turned.shape, 0)
+        ft[at, :] = narrow(jnp.where(lax.rem(line, 8) == 5, 1.0, turned))
+
     def step_lines(s):
         block, held = s // STEPS_HELD, lax.rem(s, STEPS_HELD)
         result = own_dot(fa[block], mixrow[held], 1, 0)
@@ -968,13 +1024,33 @@
         lines = (ycoef[...] + xcoef[pl.ds(s, 1), :] + result[:, :LANES]) * deviation
         return lines, deviation
 
-    def step_sums(s, weighted):
-        rowsum[...] += weighted
-        at = pl.ds(pl.multiple_of(s * 16, 16), 16)
-        found = own_dot(ft[at, :], narrow(weighted), 1, 0)
-        found = jnp.where(lane_half == 0, found[:8], found[8:])
-        colsum[pl.ds(s, 1), :] = found[5:6]
-        return found
+    def pair_sums(s, weighted):
+        at = pl.ds(pl.multiple_of(s * 16, 32), 32)
+        both = own_dot(ft[at, :], jnp.concatenate([narrow(w) for w in weighted], axis=1), 1, 0)
+        result = None
+        for k in range(2):
+            found = both[k * 16 : k * 16 + 16, k * LANES : (k + 1) * LANES]
+            found = jnp.where(lane_half == 0, found[:8], found[8:])
+            colsum[pl.ds(s + k, 1), :] = found[5:6]
+            result = found if result is None else result + found
+        return result
+
+    def in_groups(one, first, last, start):
+        def group(n, carry):
+            rows_here = None
+            for pair in range(GROUP // 2):
+                weighted = []
+                for k in range(2):
+                    s = n * GROUP + pair * 2 + k
+                    total, found, here = one(s, carry)
+                    carry = (total, found)
+                    weighted.append(here)
+                    rows_here = here if rows_here is None else rows_here + here
+                carry = (carry[0], carry[1] + pair_sums(n * GROUP + pair * 2, weighted))
+            rowsum[...] += rows_here
+            return carry
+
+        return lax.fori_loop(first // GROUP, last // GROUP, group, start)
 
     def fold(values):
         return values[:rows] + values[rows:]
@@ -992,12 +1068,6 @@
     def other_half(line):
         return pltpu.roll(jnp.broadcast_to(line, (8, LANES)), rows, 1)[:1]
 
-    query_scaled = query_inputs * gin * score_scale
-    coefficients(query_scaled, 0.0)
-    ycoef[...] += row_out
-    half_lane = lax.broadcasted_iota(jnp.int32, (held_rows, LANES), 1) // rows
-    xcoef[...] += jnp.where(half_lane == 0, col_out[0], col_out[1])
-
     def first_pass(s, best):
         lines, deviation = step_lines(s)
         sl[s] = lines
@@ -1014,10 +1084,10 @@
         deviation = own_dot(fa[block], mixrow[held][:, LANES:], 1, 0)
         weights = jnp.exp(sl[s] - best)
         total = total + jnp.sum(weights, axis=0, keepdims=True)
-        return total, found + step_sums(s, weights * deviation)
-
-    total, found = lax.fori_loop(
-        0, steps, second_pass, (jnp.zeros((1, LANES), f32), jnp.zeros((8, LANES), f32)), unroll=4
+        return total, found, weights * deviation
+
+    total, found = in_groups(
+        second_pass, 0, steps, (jnp.zeros((1, LANES), f32), jnp.zeros((8, LANES), f32))
     )
     total = total + other_half(total)
     log_total = best + jnp.log(total)
@@ -1027,6 +1097,7 @@
     xsmall[0, core, quad] = mixed_low
     x_spread(xsmall.at[0, core, quad], 8)
     relay_x(0)
+    relay_x(6)
     attended = own_dot(mixed_low, win[1], 1, 0)
     act[ATT] = attended
     attended_low = narrow(attended)
@@ -1041,56 +1112,69 @@
     pre = tmp[...] + bc[5:6]
     act[PRE_C] = pre
     hidden_c = narrow(gelu_value(pre))
-    xbuf[2, core, quad] = hidden_c
     loads[C2].wait()
     times(hidden_c, C2, tmp)
     second = act[FIRST] + tmp[...] + bc[6:7]
     act[SECOND] = second
     normed_t = norm_forward(second, gs[0:1], bs[0:1])
     xbuf[4, core, quad] = normed_t
-    spread_x(4)
-    later_x(1)
-    later_x(2)
-    background(SEND[0])
+    mine = core * quads + quad
+
+    def block_of(peer):
+        return lax.rem(peer, 2) * quads + peer // 2
+
+    def to_heads(kind, values):
+        gsrc[9 + kind] = values
+
+        def one(step, carry):
+            peer, where = to_plane(step)
+            push(
+                gsrc.at[9 + kind, :, lanes_of(peer)], heads.at[kind, mine],
+                a_send.at[4 + kind], a_recv.at[4 + kind], where,
+            )
+            return carry
+
+        lax.fori_loop(1, grid_cols, one, 0)
+        heads[kind, mine] = gsrc[9 + kind, :, lanes_of(j)]
+
+    loads[SQ].wait()
+    times(normed_t, SQ, tmp)
+    to_heads(0, narrow(tmp[...] + bs[2:3]))
+    loads[SK].wait()
+    times(normed_t, SK, tmp)
+    to_heads(1, narrow(tmp[...]))
+    loads[SV].wait()
+    times(normed_t, SV, tmp)
+    to_heads(2, narrow(tmp[...] + bs[3:4]))
+    background(0)
     loads[S2].wait()
     times_t(cot_low, S2, act.at[COT_BACK])
-    relay_x(4)
     x_relay(xsmall.at[0, core], 8)
-    have_x(4)
-
-    for k in (SQ, SK, SV):
-        loads[k].wait()
     head_rows = grid_cols * rows
-    biasvec[...] = jnp.concatenate([bs, jnp.zeros((1, width), f32)], axis=0)
-
-    def head_in(n, carry):
-        x = xbuf[4, n].reshape(quads * rows, width)
-        at = pl.ds(pl.multiple_of(n * (quads * rows), quads * rows), quads * rows)
-        heads[0, at, :] = narrow(own_dot(x, wts[SQ, :, lanes_of(j)], 1, 0) + biasvec[2:3, lanes_of(j)])
-        heads[1, at, :] = narrow(own_dot(x, wts[SK, :, lanes_of(j)], 1, 0))
-        heads[2, at, :] = narrow(own_dot(x, wts[SV, :, lanes_of(j)], 1, 0) + biasvec[3:4, lanes_of(j)])
-        return carry
-
-    lax.fori_loop(0, 2, head_in, 0)
     per = 128
+    each = per // rows
+
+    for kind in range(3):
+        wait_for(heads.at[kind, pl.ds(0, grid_cols - 1)], a_recv.at[4 + kind])
+
+    def head_of(kind):
+        return heads[kind].reshape(head_rows, chunk)
+
+    def head_part(kind, n):
+        return heads[kind, pl.ds(n * each, each)].reshape(per, chunk)
 
     def head_forward(n, carry):
         at = pl.ds(pl.multiple_of(n * per, per), per)
-        scores = own_dot(heads[0, at, :], heads[1], 1, 1) * head_scale
+        scores = own_dot(head_part(0, n), head_of(1), 1, 1) * head_scale
         weights = jnp.exp(scores - jnp.max(scores, axis=1, keepdims=True))
         found_probs = weights / jnp.sum(weights, axis=1, keepdims=True)
         probs[at, :] = found_probs
-        mixed = narrow(own_dot(narrow(found_probs), heads[2], 1, 0))
-        for part in range(per // rows):
-            mix_s[n * (per // rows) + part] = mixed[part * rows : (part + 1) * rows]
+        probs_low = narrow(found_probs)
+        prob_grad[1, at, :] = probs_low
+        mix_s[pl.ds(n * each, each)] = narrow(own_dot(probs_low, head_of(2), 1, 0)).reshape(each, rows, chunk)
         return carry
 
-    lax.fori_loop(0, head_rows // per, head_forward, 0)
-
-    def block_of(peer):
-        return lax.rem(peer, 2) * quads + peer // 2
-
-    mine = core * quads + quad
+    lax.fori_loop(0, head_rows // per, head_forward, 0, unroll=2)
 
     def send_mixed(step, carry):
         peer, where = to_plane(step)
@@ -1098,29 +1182,26 @@
         return carry
 
     lax.fori_loop(1, grid_cols, send_mixed, 0)
-    background(SEND[1])
+    background(1)
     mix_b[:, lanes_of(j)] = mix_s[mine]
     loads[SO].wait()
     wait_for(mix_b.at[:, pl.ds(0, chunk * (grid_cols - 1))], a_recv.at[0])
     mixed_rows = mix_b[...]
     xbuf[3, core, quad] = mixed_rows
     times(mixed_rows, SO, tmp)
+    relay_x(4)
     third = act[SECOND] + tmp[...] + bs[4:5]
     act[THIRD] = third
     normed_s = norm_forward(third, gs[1:2], bs[1:2])
     xbuf[5, core, quad] = normed_s
-    later_x(5)
-    background(SEND[2])
+    background(2)
     loads[S1].wait()
     times(normed_s, S1, tmp)
     pre = tmp[...] + bs[5:6]
     act[PRE_S] = pre
     hidden_s = narrow(gelu_value(pre))
-    xbuf[6, core, quad] = hidden_s
-    waiting[:0] = [(6, piece) for piece in range(pieces)]
-    later_x(3)
-    background(SEND[3])
-    relay_x(1)
+    spread_plain(5, hidden_s)
+    background(3)
     times(hidden_s, S2, tmp)
     new_latents[...] = narrow(act[THIRD] + tmp[...] + bs[6:7])
 
@@ -1142,81 +1223,99 @@
 
     lax.fori_loop(1, grid_cols, send_dmixed, 0)
     dmix_b[mine] = gsrc[12, :, lanes_of(j)]
+    background(4)
     spread_g(4, pre_low)
+    have_x(6)
+    weight_part(8, have_g(5), xbuf.at[6])
     spread_g(6, out_low)
-    background(SEND[4])
+    background(5)
     wait_for(dmix_b.at[pl.ds(0, grid_cols - 1)], a_recv.at[1])
 
-    def head_backward(n, carry):
+    def from_heads(kind):
+        def one(step, carry):
+            peer, where = to_plane(step)
+            push(
+                dqkv_s.at[kind, block_of(peer)], dqkv_b.at[kind, :, lanes_of(j)],
+                a_send.at[7 + kind], a_recv.at[7 + kind], where,
+            )
+            return carry
+
+        lax.fori_loop(1, grid_cols, one, 0)
+        dqkv_b[kind, :, lanes_of(j)] = dqkv_s[kind, mine]
+
+    def rows_back(kind):
+        wait_for(dqkv_b.at[kind, :, pl.ds(0, chunk * (grid_cols - 1))], a_recv.at[7 + kind])
+        wait_for(heads.at[kind, pl.ds(0, grid_cols - 1)], a_send.at[4 + kind])
+        spread_g(9 + kind, dqkv_b[kind])
+
+    def put_head(kind, n, values):
+        dqkv_s[kind, pl.ds(n * each, each)] = narrow(values).reshape(each, rows, chunk)
+
+    d_mixed_all = dmix_b[...].reshape(head_rows, chunk)
+
+    def head_values(n, carry):
         at = pl.ds(pl.multiple_of(n * per, per), per)
-        parts = [dmix_b[n * (per // rows) + part] for part in range(per // rows)]
-        d_mixed = jnp.concatenate(parts, axis=0)
-        d_probs = own_dot(d_mixed, heads[2], 1, 1)
+        put_head(2, n, own_dot(prob_grad[1, :, at], d_mixed_all, 0, 0))
+        return carry
+
+    def head_queries(n, carry):
+        at = pl.ds(pl.multiple_of(n * per, per), per)
+        d_mixed = dmix_b[pl.ds(n * each, each)].reshape(per, chunk)
+        d_probs = own_dot(d_mixed, head_of(2), 1, 1)
         found_probs = probs[at, :]
         d_scores = found_probs * (d_probs - jnp.sum(found_probs * d_probs, axis=1, keepdims=True))
         d_low = narrow(d_scores * head_scale)
         prob_grad[0, at, :] = d_low
-        prob_grad[1, at, :] = narrow(found_probs)
-        d_query = own_dot(d_low, heads[1], 1, 0)
-        for part in range(per // rows):
-            dqkv_s[n * (per // rows) + part, 0] = narrow(d_query[part * rows : (part + 1) * rows])
+        put_head(0, n, own_dot(d_low, head_of(1), 1, 0))
         return carry
-
-    lax.fori_loop(0, head_rows // per, head_backward, 0)
-    d_mixed_all = dmix_b[...].reshape(head_rows, chunk)
 
     def head_keys(n, carry):
         at = pl.ds(pl.multiple_of(n * per, per), per)
-        d_key = own_dot(prob_grad[0, :, at], heads[0], 0, 0)
-        d_value = own_dot(prob_grad[1, :, at], d_mixed_all, 0, 0)
-        for part in range(per // rows):
-            cut = slice(part * rows, (part + 1) * rows)
-            dqkv_s[n * (per // rows) + part, 1] = narrow(d_key[cut])
-            dqkv_s[n * (per // rows) + part, 2] = narrow(d_value[cut])
+        put_head(1, n, own_dot(prob_grad[0, :, at], head_of(0), 0, 0))
         return carry
 
-    lax.fori_loop(0, head_rows // per, head_keys, 0)
-
-    def send_dqkv(step, carry):
-        peer, where = to_plane(step)
-        push(dqkv_s.at[block_of(peer)], dqkv_b.at[:, :, lanes_of(j)], a_send.at[2], a_recv.at[2], where)
-        return carry
-
-    lax.fori_loop(1, grid_cols, send_dqkv, 0)
-    background(SEND[5])
-    dqkv_b[:, :, lanes_of(j)] = dqkv_s[mine]
+    lax.fori_loop(0, head_rows // per, head_values, 0, unroll=2)
+    from_heads(2)
+    background(6)
+    join_rows(staged.at[slot_of(8)], 8)
+    lax.fori_loop(0, head_rows // per, head_queries, 0, unroll=2)
+    from_heads(0)
+    background(7)
+    relay_x(5)
+    lax.fori_loop(0, head_rows // per, head_keys, 0, unroll=2)
+    from_heads(1)
+    background(8)
+    relay_x(1)
 
     def column_sum(values):
         return jnp.sum(to_float(values), axis=0, keepdims=True)
 
-    relay_x(6)
-    have_x(6)
-    right = have_g(5)
-    bias_s6 = column_sum(right)
-    weight_part(8, right, xbuf.at[6])
-    wait_for(dqkv_b.at[:, :, pl.ds(0, chunk * (grid_cols - 1))], a_recv.at[2])
-    for k in range(3):
-        spread_g(9 + k, dqkv_b[k])
-    times_t(dqkv_b[0], SQ, tmp)
-    times_t(dqkv_b[1], SK, tmp, True)
-    times_t(dqkv_b[2], SV, tmp, True)
-    background(SEND[6])
-    relay_x(5)
-    relay_x(2)
     have_x(5)
     right = have_g(4)
     bias_s5 = column_sum(right)
     weight_part(7, right, xbuf.at[5])
-    join(8)
+    rows_back(2)
+    times_t(dqkv_b[2], SV, tmp)
+    rows_back(0)
+    times_t(dqkv_b[0], SQ, tmp, True)
+    have_x(1)
+    recompute(1, 2, C1, biases.at[5:6])
+    rows_back(1)
+    times_t(dqkv_b[1], SK, tmp, True)
+    background(9)
     d_rows, lnvec[4:5, :], lnvec[5:6, :] = norm_gradient(act[SECOND], gs[0:1], tmp[...])
     gradient = act[GRAD] + d_rows
     act[GRAD] = gradient
     second_low = narrow(gradient)
     spread_g(2, second_low)
+    background(10)
     times_t(second_low, C2, tmp)
     d_pre = tmp[...] * gelu_slope(act[PRE_C])
     pre_low = narrow(d_pre)
     spread_g(1, pre_low)
+    background(11)
+    join(7)
+    relay_x(3)
     times_t(pre_low, C1, tmp)
     d_rows, lnvec[2:3, :], lnvec[3:4, :] = norm_gradient(act[FIRST], gc[1:2], tmp[...])
     gradient = act[GRAD] + d_rows
@@ -1227,15 +1326,18 @@
     d_attended = narrow(tmp[...])
     spread_g(8, d_attended)
 
-    background(len(waiting))
-    for k in range(3):
+    have_x(3)
+    right = have_g(6)
+    bias_s4 = column_sum(right)
+    weight_part(9, right, xbuf.at[3])
+    have_x(4)
+    for k in (2, 0, 1):
         right = have_g(9 + k)
         if k == 0:
             bias_s2 = column_sum(right)
         elif k == 2:
             bias_s3 = column_sum(right)
         weight_part(4 + k, right, xbuf.at[4])
-    join(7)
 
     grad_inputs = own_dot(d_attended, win[1], 1, 1)
     d_attended = to_float(d_attended)
@@ -1261,7 +1363,7 @@
         colors_here = [query_away, grad_away]
         if held:
             colors_here = [pltpu.roll(v, held * 16, 1) for v in colors_here]
-        cgright[held] = jnp.concatenate(
+        cgright[held // 2, (held % 2) * WIDE : (held % 2 + 1) * WIDE, :] = jnp.concatenate(
             [
                 jnp.concatenate([narrow(colors_here[0]), blank], axis=1),
                 jnp.concatenate([narrow(colors_here[1]), blank], axis=1),
@@ -1271,7 +1373,12 @@
         )
     rowsum[...] = jnp.zeros(rowsum.shape, f32)
     colsum[...] = jnp.zeros(colsum.shape, f32)
-    cgacc[...] = jnp.zeros(cgacc.shape, f32)
+
+    def kept_at(s):
+        place_now = lax.rem(s, 6)
+        line = pl.ds(pl.multiple_of((place_now // 2) * tall, 32), tall)
+        lane = pl.ds(pl.multiple_of(lax.rem(place_now, 2) * WIDE, LANES), WIDE)
+        return wts.at[1 + s // 6, line, lane]
 
     def back_pass(s, carry):
         total, found = carry
@@ -1279,34 +1386,35 @@
         scores = sl[s]
         found_probs = jnp.exp(scores - log_total)
         d_scores = found_probs * (lines + constant)
-        left = jnp.concatenate(
+        kept_at(s)[...] = jnp.concatenate(
             [narrow(d_scores), narrow(found_probs), narrow(d_scores * scores + found_probs * lines)], axis=1
         )
-        block, held = s // STEPS_HELD, lax.rem(s, STEPS_HELD)
-        cgacc[block] += own_dot(left, cgright[held], 1, 0)
         total = total + jnp.sum(d_scores, axis=0, keepdims=True)
-        return total, found + step_sums(s, d_scores * deviation)
+        return total, found, d_scores * deviation
+
+    def color_block(block):
+        result = None
+        for pair in range(block * STEPS_HELD // 2, min((block + 1) * STEPS_HELD, steps) // 2):
+            line = pl.ds((pair % 3) * tall, tall)
+            left = wts[1 + pair // 3, line, pl.ds(0, 2 * WIDE)]
+            part = own_dot(left, cgright[pair % (STEPS_HELD // 2)], 1, 0)
+            result = part if result is None else result + part
+        cgacc[block] = result
 
     carry = (jnp.zeros((1, LANES), f32), jnp.zeros((8, LANES), f32))
     third_of = steps // 3
-    carry = lax.fori_loop(0, third_of, back_pass, carry, unroll=4)
-    relay_x(3)
-    for k in range(3):
-        join(4 + k)
-    have_x(3)
-    right = have_g(6)
-    bias_s4 = column_sum(right)
-    weight_part(9, right, xbuf.at[3])
-    carry = lax.fori_loop(third_of, 2 * third_of, back_pass, carry, unroll=4)
-    have_x(2)
+    carry = in_groups(back_pass, 0, third_of, carry)
+    finish_rows(8)
+    join(9)
     right = have_g(2)
     bias_c6 = column_sum(right)
     weight_part(2, right, xbuf.at[2])
-    have_x(1)
     right = have_g(1)
     bias_c5 = column_sum(right)
     weight_part(1, right, xbuf.at[1])
-    join(9)
+    carry = in_groups(back_pass, third_of, 2 * third_of, carry)
+    join(6)
+    join(4)
     x_arrived(xsmall.at[0, 1 - core], 8)
     right = have_g(3)
     bias_c4 = column_sum(right)
@@ -1314,7 +1422,7 @@
     right = have_g(8)
     bias_c3 = column_sum(right)
     small_part(1, right, xsmall.at[0])
-    total, found = lax.fori_loop(2 * third_of, steps, back_pass, carry, unroll=4)
+    total, found = in_groups(back_pass, 2 * third_of, steps, carry)
     plain_scores = pixel_sums(found, 1.0) * score_scale
     total = total * score_scale
     score_total = fold(jnp.transpose(jnp.concatenate([total, jnp.zeros((LANES - 1, LANES), f32)], axis=0)))[:, 0:1]
@@ -1333,28 +1441,39 @@
     gain_part = jnp.sum(query_inputs * plain_scores + grad_inputs * plain_mixed, axis=0, keepdims=True)
     bias_part = jnp.sum(query_inputs * score_total + grad_inputs, axis=0, keepdims=True)
     cuts = [part[:, k * LANES : (k + 1) * LANES] for part in (gain_part, bias_part) for k in range(3)]
-    ivec[...] = jnp.concatenate(cuts + [jnp.zeros((2, LANES), f32)], axis=0)
-    ivbuf[me] = ivec[...]
-
-    def send_ivec(step, carry):
-        push(ivec, ivbuf.at[me], misc_send.at[1], misc_recv.at[1], at_device(lax.rem(me + step, n_dev)))
-        return carry
-
-    lax.fori_loop(1, n_dev, send_ivec, 0)
-
+    shared = jnp.concatenate(cuts + [jnp.zeros((1, LANES), f32)], axis=0)
     times_t(query_grad_low, CQ, tmp)
     d_rows, lnvec[0:1, :], lnvec[1:2, :] = norm_gradient(to_float(latents[...]), gc[0:1], tmp[...])
     latent_grad[...] = act[GRAD] + d_rows
-
-    lnsend[...] = regroup(lnvec[...])
+    lnvec[8:9, :] = jnp.sum(to_float(cotangent[...]), axis=0, keepdims=True)
+    lines = regroup(lnvec[...])
+    for peer in range(grid_cols):
+        lnsend[peer] = jnp.concatenate([lines[:9, peer * chunk : (peer + 1) * chunk], shared], axis=0)
 
     def send_ln(step, carry):
         peer, where = to_plane(step)
-        push(lnsend.at[:, lanes_of(peer)], lnbuf.at[j], misc_send.at[2], misc_recv.at[2], where)
+        push(lnsend.at[peer], lnbuf.at[j], misc_send.at[2], misc_recv.at[2], where)
         return carry
 
     lax.fori_loop(1, grid_cols, send_ln, 0)
-    lnbuf[j] = lnsend[:, lanes_of(j)]
+    lnbuf[j] = lnsend[j]
+    join(5)
+    for block in range(0, blocks // 2):
+        color_block(block)
+    x_relay(xsmall.at[1, core], 9)
+    have_x(0)
+    right = have_g(0)
+    bias_c2 = column_sum(right)
+    weight_part(0, right, xbuf.at[0])
+    for block in range(blocks // 2, blocks - 1):
+        color_block(block)
+    x_arrived(xsmall.at[1, 1 - core], 9)
+    small_part(0, have_g(7), xsmall.at[1])
+    join(2)
+    color_block(blocks - 1)
+    join(1)
+    for m in (2, 1):
+        join_small(m)
 
     for block in range(blocks):
         both = own_dot(fa[block], spread[...], 1, 0)
@@ -1378,39 +1497,14 @@
 
     lax.fori_loop(1, grid_cols, send_cg, 0)
 
-    x_relay(xsmall.at[1, core], 9)
-    for m in (2, 1):
-        join(m)
-    for m in (2, 1):
-        join_small(m)
-    have_x(0)
-    right = have_g(0)
-    bias_c2 = column_sum(right)
-    weight_part(0, right, xbuf.at[0])
-    x_arrived(xsmall.at[1, 1 - core], 9)
-    small_part(0, have_g(7), xsmall.at[1])
-
-    wait_for(cgbuf.at[pl.ds(0, grid_cols - 1)], misc_recv.at[3])
-    tiles = to_float(cgbuf[0])
-    for peer in range(1, grid_cols):
-        tiles = tiles + to_float(cgbuf[peer])
-    cgsum[...] = tiles
-
-    def send_tile(step, carry):
-        part = lax.rem(z + step, grid_rows)
-        push(cgsum.at[part], cgfin.at[z], misc_send.at[6], misc_recv.at[6], {"rows": part})
-        return carry
-
-    lax.fori_loop(1, grid_rows, send_tile, 0)
-    cgfin[z] = cgsum[z]
     wait_for(lnbuf.at[pl.ds(0, grid_cols - 1)], misc_recv.at[2])
     norms = lnbuf[0]
     for peer in range(1, grid_cols):
         norms = norms + lnbuf[peer]
     vecsend[...] = jnp.concatenate(
         [
-            norms, bias_c2, bias_c3, bias_c4, bias_c5, bias_c6, bias_s2, bias_s3,
-            bias_s4, bias_s5, bias_s6, jnp.zeros((6, chunk), f32),
+            norms[:8], bias_c2, bias_c3, bias_c4, bias_c5, bias_c6, bias_s2, bias_s3,
+            bias_s4, bias_s5, norms[8:9], jnp.zeros((6, chunk), f32), norms[9:], jnp.zeros((1, chunk), f32),
         ],
         axis=0,
     )
@@ -1422,26 +1516,34 @@
 
     lax.fori_loop(1, grid_rows, send_vec, 0)
     vecbuf[z] = vecsend[...]
-
-    wait_for(cgfin.at[pl.ds(0, grid_rows - 1)], misc_recv.at[6])
-    color_out[...] = cgfin[...]
-    wait_for(ivbuf.at[pl.ds(0, n_dev - 1)], misc_recv.at[1])
-    sums = ivbuf[0]
-    for d in range(1, n_dev):
-        sums = sums + ivbuf[d]
-    input_vector_out[...] = sums
-
     join(0)
     join_small(0)
+    wait_for(cgbuf.at[pl.ds(0, grid_cols - 1)], misc_recv.at[3])
+    tiles = to_float(cgbuf[0])
+    for peer in range(1, grid_cols):
+        tiles = tiles + to_float(cgbuf[peer])
+    cgsum[...] = tiles
+
+    def send_tile(step, carry):
+        part = lax.rem(z + step, grid_rows)
+        push(cgsum.at[part], cgfin.at[z], misc_send.at[6], misc_recv.at[6], {"rows": part})
+        return carry
+
+    lax.fori_loop(1, grid_rows, send_tile, 0)
+    cgfin[z] = cgsum[z]
+
     wait_for(vecbuf.at[pl.ds(0, grid_rows - 1)], misc_recv.at[4])
     vectors = vecbuf[0]
     for part in range(1, grid_rows):
         vectors = vectors + vecbuf[part]
-    vector_out[...] = vectors
-    for m in (8, 7, 4, 5, 6, 9, 2, 1, 0):
+    vector_out[...] = vectors[:24]
+    input_vector_out[...] = vectors[24:]
+    for m in (7, 4, 5, 6, 9, 2, 1, 0):
         wait_for(crossed.at[slot_of(m)], f_recv.at[m])
         result = kept_of(m)[...] + to_float(crossed[slot_of(m)])
         kept_of(m)[...] = result
+    wait_for(row_done.at[:, pl.ds(0, chunk * (grid_cols - 1))], a_recv.at[3])
+    self_total[4] = row_done[...]
     sums = []
     for m in (2, 1, 0):
         wait_for(crossed_small.at[m], f_recv.at[10 + m])
@@ -1449,8 +1551,10 @@
     out_total[...] = own_dot(narrow(sums[0]), win[1], 1, 0)
     input_parts[1] = sums[1]
     input_parts[0] = sums[2]
-
-    for k in range(7):
+    wait_for(cgfin.at[pl.ds(0, grid_rows - 1)], misc_recv.at[6])
+    color_out[...] = cgfin[...]
+
+    for k in (0, 1, 3, 4, 5, 6):
         wait_for(xbuf.at[k, 0, pl.ds(0, quads - 1)], x_send.at[k])
         wait_for(xbuf.at[k, 0], y_send.at[k])
     for k in range(2):
@@ -1460,14 +1564,17 @@
         wait_for(gsrc.at[k, :, pl.ds(0, chunk * (grid_cols - 1))], g_send.at[k])
     wait_for(mix_s.at[pl.ds(0, grid_cols - 1)], a_send.at[0])
     wait_for(dmix_b.at[pl.ds(0, grid_cols - 1)], a_send.at[1])
-    wait_for(dqkv_s.at[pl.ds(0, grid_cols - 1)], a_send.at[2])
+    for kind in range(3):
+        wait_for(dqkv_s.at[kind, pl.ds(0, grid_cols - 1)], a_send.at[7 + kind])
     wait_for(colbuf.at[pl.ds(0, grid_cols - 1)], misc_send.at[0])
-    wait_for(ivbuf.at[pl.ds(0, n_dev - 1)], misc_send.at[1])
+    wait_for(row_turned.at[pl.ds(0, own * (grid_cols - 1))], a_send.at[3])
     wait_for(lnbuf.at[pl.ds(0, grid_cols - 1)], misc_send.at[2])
     wait_for(cgbuf.at[pl.ds(0, grid_cols - 1)], misc_send.at[3])
     wait_for(colstage.at[pl.ds(0, grid_rows - 1)], misc_send.at[5])
     wait_for(cgfin.at[pl.ds(0, grid_rows - 1)], misc_send.at[6])
-    for m in (0, 1, 2, 4, 5, 6, 7, 8, 9):
+    wait_for(row_pair, r_send.at[8])
+    wait_for(row_hand, f_send.at[8])
+    for m in (0, 1, 2, 4, 5, 6, 7, 9):
         wait_for(paired.at[slot_of(m)], r_send.at[m])
         wait_for(handed.at[slot_of(m)], f_send.at[m])
     for m in range(3):
@@ -1515,7 +1622,7 @@
     lines = input_vectors[...]
     for k, target in enumerate((o_gain, o_bias)):
         wide = jnp.concatenate([lines[3 * k + t : 3 * k + t + 1] for t in range(3)], axis=1)
-        target[...] = by_channel(wide)
+        target[...] = by_channel(wide).reshape(-1)
     place = lax.axis_index("rows")
     width = vectors.shape[1]
     mine = pltpu.roll(vectors[...], lax.rem(width - place * own, width), 1)[:, :own]
@@ -1586,6 +1693,13 @@
         ((3, own, WIDE), bf16),
         ((3, own, WIDE), bf16),
         ((3, own, WIDE), f32),
+        ((2, chunk, width // grid_rows), bf16),
+        ((chunk, width // grid_rows), bf16),
+        ((chunk, width // grid_rows), bf16),
+        ((chunk, width // grid_rows), f32),
+        ((width // grid_rows, chunk), f32),
+        ((own, width), f32),
+        ((8, width), f32),
         ((grid_rows, 32, LANES), f32),
         ((grid_rows, 32, LANES), bf16),
         ((grid_rows, 32, LANES), bf16),
@@ -1600,7 +1714,7 @@
         ((tall, 2 * LANES), bf16),
         ((2, held_rows, 2 * LANES), bf16),
         ((STEPS_HELD, LANES, 2 * LANES), bf16),
-        ((STEPS_HELD, WIDE, 2 * LANES), bf16),
+        ((STEPS_HELD // 2, 2 * WIDE, 2 * LANES), bf16),
         ((tall, LANES), f32),
         ((held_rows, LANES), f32),
         ((blocks, tall, 2 * LANES), f32),
@@ -1609,25 +1723,23 @@
         ((grid_rows, 32, LANES), f32),
         ((grid_rows, 32, LANES), f32),
         ((9, rows, width), f32),
+        ((16, width), f32),
+        ((grid_cols, 16, chunk), f32),
+        ((grid_cols, 16, chunk), f32),
         ((8, width), f32),
-        ((8, width), f32),
-        ((grid_cols, 8, chunk), f32),
-        ((8, width), f32),
-        ((24, chunk), f32),
-        ((grid_rows, 24, chunk), f32),
-        ((8, LANES), f32),
-        ((n_dev, 8, LANES), f32),
-        ((3, grid_cols * rows, chunk), bf16),
+        ((32, chunk), f32),
+        ((grid_rows, 32, chunk), f32),
+        ((3, grid_cols, rows, chunk), bf16),
         ((grid_cols * rows, grid_cols * rows), f32),
         ((2, grid_cols * rows, grid_cols * rows), bf16),
         ((grid_cols, rows, chunk), bf16),
         ((rows, width), bf16),
         ((grid_cols, rows, chunk), bf16),
-        ((grid_cols, 3, rows, chunk), bf16),
+        ((3, grid_cols, rows, chunk), bf16),
         ((3, rows, width), bf16),
     ]
     scratch = [pltpu.VMEM(dims, kind) for dims, kind in scratch]
-    scratch += [dma((count,)) for count in (11, 10, 10, 10, 10, 12, 12, 3, 3, 13, 13, 13, 13, 7, 7)]
+    scratch += [dma((count,)) for count in (11, 10, 10, 10, 10, 12, 12, 10, 10, 13, 13, 13, 13, 7, 7)]
     outs = [
         ((rows, width), bf16),
         ((rows, width), f32),
@@ -1657,8 +1769,8 @@
         latents,
         cotangent,
         jnp.transpose(pixel_colors, (0, 3, 1, 2)),
-        in_gain.reshape(1, -1),
-        in_bias.reshape(1, -1),
+        in_gain,
+        in_bias,
         order,
         cross_gains,
         cross_biases,
@@ -1682,8 +1794,8 @@
         ((3, own, width), f32),
         ((own, width), f32),
         ((2, own, count), f32),
-        ((1, count), f32),
-        ((1, count), f32),
+        ((count,), f32),
+        ((count,), f32),
         ((2, own), f32),
         ((7, own), f32),
         ((5, own, width), f32),
@@ -1712,8 +1824,8 @@
         jnp.transpose(cross_total, (0, 2, 1)),
         jnp.transpose(out_total),
         jnp.transpose(input_total, (0, 2, 1)),
-        gain[0],
-        bias[0],
+        gain,
+        bias,
         cross_gain,
         cross_bias,
         jnp.transpose(self_total, (0, 2, 1)),

time: 143 us -> 124 us (0.87)
  Pallas kernels: 135 us -> 121 us
  other arithmetic: 2.55 us -> 0 us
  local copies, waits for them, and re-layouts: 5 us -> 2.5 us
    pallas_call x1, Pallas kernels: 132 us -> 118 us  [local_kernel(): pl.pallas_call(functools.partial(layer_kernel, sizes), out_shape=[shape(d...]
    pallas_call x2 -> x0, other arithmetic: 2.55 us -> none  [local_kernel(): pl.pallas_call(functools.partial(finish_kernel, own, tile_rows, tile_cols...]
    reshape x2 -> x0, local copies, waits for them, and re-layouts: 2.49 us -> none  [the longest x1 1.24 us: local_kernel(): in_gain.reshape(1, -1)]
where the time goes in v4:
time: 124 us
  Pallas kernels  121 us (98%)
  local copies, waits for them, and re-layouts  2.5 us (2%)
    pallas_call x1, Pallas kernels, local_kernel(): pl.pallas_call(functools.partial(layer_kernel, sizes), out_shape=[shape(d...  118 us
    pallas_call x1, Pallas kernels, local_kernel(): pl.pallas_call(functools.partial(finish_kernel, own, tile_rows, tile_cols...  2.94 us
    unnamed x1, local copies, waits for them, and re-layouts  2.5 us

profile of v4, /device:TPU:0, one launch (start us, length us, event | category | flops | bytes accessed | tf_op | source)
XLA Modules:
  0.0 124.0 jit_solution(15626372787420132771)
XLA Ops:
  0.6 2.5 %copy.37.w_input = bf16[2,261,1024]{2,1,0:T(8,128)(2,1)} copy(bf16[2,261,1024]{2,0,1:T(2,128)(2,1)} %param.29) | data formatting | bytes 2138112 | tf_op args[6]
  3.1 117.8 %shard_map.326 = (bf16[64,1024]{1,0:T(8,128)(2,1)}, f32[64,1024]{1,0:T(8,128)}, f32[4,32,128]{2,1,0:T(8,128)}, f32[3,32,1024]{2,1,0:T(8,128)}, f32[32,1024]{1,0:...) custom-call(s32[4,4]{1,0:T(4,128)} %boxes.1, ...), custom_call_target="tpu_custom_call" | custom-call | flops 20000000000 | bytes 40000000 | tf_op jit(solution)/shard_map/pallas_call | solution.py:1755
  120.9 2.9 %shard_map.327 = (bf16[64,1024]{1,0:T(8,128)(2,1)}, f32[64,1024]{1,0:T(8,128)}, f32[3,9,4,72]{3,2,1,0:T(4,128)}, f32[3,32,1024]{2,1,0:T(8,128)}, f32[32,1024]{1,...) custom-call(bf16[64,1024]{1,0:T(8,128)(2,1)} %get-tuple-element.38.l, ...), custom_call_target="tpu_custom_call" | custom-call | tf_op jit(solution)/shard_map/pallas_call | solution.py:1806

commit v5 on v4

--- a/solution.py
+++ b/solution.py
@@ -19,7 +19,7 @@
 NEG = -1e30
 FREQ_TOP = 112.0
 VMEM_BYTES = 63 * 1024 * 1024
-PLAN = {0: ((4, 4),), 1: ((1, 2),), 3: ((5, 2),), 4: ((5, 2),), 5: ((1, 2),), 8: ((3, 4),)}
+PLAN = {0: ((4, 4),), 2: ((3, 4),), 5: ((5, 1),), 6: ((5, 1),), 9: ((5, 2),)}
 
 
 def narrow(values):
@@ -510,6 +510,7 @@
 
 STEPS_HELD = 8
 GROUP = 4
+XS = {0: 0, 3: 1, 4: 2, 5: 3, 6: 4}
 LANES = 128
 MESH = pl.DeviceIdType.MESH
 WIDE = 3 * LANES
@@ -609,18 +610,19 @@
 
 def layer_kernel(
     sizes,
-    boxes, latents, cotangent, colors, in_gain, in_bias, order, cross_gains, cross_biases, self_gains,
-    self_biases, place, pick, spread, back,
+    boxes, latents, cotangent, colors, in_gain, in_bias, cross_gains, cross_biases, self_gains,
+    self_biases, far_order, far_place, far_pick, far_spread, far_back,
     w_cross, w_out, w_self, w_self_out, w_input,
     new_latents, latent_grad, color_out, cross_total, out_total, self_total, self_out_total,
     input_parts, vector_out, input_vector_out,
-    wts, win, win_raw, xbuf, xsmall, gsrc, gbuf, staged, paired, handed, crossed, staged_small, paired_small, handed_small, crossed_small, kept_small,
+    order, place, pick, spread, back, wts, win, win_raw, xbuf, xsmall, gsrc, gbuf, staged, paired, handed, crossed, staged_small, paired_small, handed_small, crossed_small, kept_small,
+    line_rows, line_hid, line_right, line_staged, line_near, line_hand, line_sums,
     row_pair, row_hand, row_cross, row_kept, row_turned, row_done, biases,
     color_lines, color_tiles, colstage, colbuf, img, img7, fa, ft, sl, ycoef, xcoef, yfeat, xfeat, mixrow,
     cgright, rowsum, colsum, cgacc, cgsend, cgbuf, cgsum, cgfin,
     act, lnvec, lnsend, lnbuf, biasvec, vecsend, vecbuf,
     heads, probs, prob_grad, mix_s, mix_b, dmix_b, dqkv_s, dqkv_b,
-    weight_sem, x_send, x_recv, y_send, y_recv, g_send, g_recv, a_send, a_recv, r_send, r_recv, f_send, f_recv,
+    fixed_sem, weight_sem, x_send, x_recv, y_send, y_recv, g_send, g_recv, a_send, a_recv, r_send, r_recv, f_send, f_recv, l_send, l_recv,
     misc_send, misc_recv,
 ):
     grid_rows, grid_cols, rows, steps, tile_rows, tile_cols = sizes
@@ -678,6 +680,10 @@
     loads.append(pltpu.make_async_copy(w_input, win_raw, weight_sem.at[10]))
     loads[CQ].start()
     loads[10].start()
+    fixed = ((far_order, order), (far_place, place), (far_pick, pick), (far_spread, spread), (far_back, back))
+    fixed = [pltpu.make_async_copy(src, dst, fixed_sem.at[k]) for k, (src, dst) in enumerate(fixed)]
+    for copy in fixed:
+        copy.start()
 
     color_lines[...] = jnp.zeros(color_lines.shape, f32)
     for channel in range(3):
@@ -689,6 +695,7 @@
     color_tiles[...] = narrow(color_lines[...])
     gc, bc = to_float(cross_gains[...]), to_float(cross_biases[...])
     gs, bs = to_float(self_gains[...]), to_float(self_biases[...])
+    fixed[0].wait()
     gains_here = [to_float(ref[...]).reshape(1, -1) for ref in (in_gain, in_bias)]
     gains_here = jnp.concatenate(gains_here + [jnp.zeros((6, in_gain.shape[0]), f32)], axis=0)
     gains_here = own_dot(narrow(gains_here), order[...], 1, 1)
@@ -697,7 +704,7 @@
     nq = norm_forward(lat, gc[0:1], bc[0:1])
     xbuf[0, core, quad] = nq
     cot_low = cotangent[...]
-    xbuf[6, core, quad] = cot_low
+    xbuf[XS[6], core, quad] = cot_low
     biases[...] = jnp.concatenate([bc, jnp.zeros((1, width), f32)], axis=0)
     pl.semaphore_wait(barrier, grid_cols + grid_rows - 2)
 
@@ -728,19 +735,19 @@
     sent = {}
 
     def spread_x(k):
-        x_spread(xbuf.at[k, core, quad], k)
+        x_spread(xbuf.at[XS[k], core, quad], k)
 
     def background(point):
         for k, count in PLAN.get(point, ()):
             for piece in range(sent.get(k, 0), sent.get(k, 0) + count):
-                x_spread(xbuf.at[k, core, quad, pl.ds(piece * 16, 16)], k)
+                x_spread(xbuf.at[XS[k], core, quad, pl.ds(piece * 16, 16)], k)
             sent[k] = sent.get(k, 0) + count
 
     def relay_x(k):
-        x_relay(xbuf.at[k, core], k)
+        x_relay(xbuf.at[XS[k], core], k)
 
     def have_x(k):
-        x_arrived(xbuf.at[k, 1 - core], k)
+        x_arrived(xbuf.at[XS[k], 1 - core], k)
 
     def to_plane(step):
         peer = lax.rem(j + step, grid_cols)
@@ -802,7 +809,7 @@
         return self_out_total
 
     def slot_of(m):
-        return m if m < 3 else m - 1
+        return 0 if m == 0 else m - 3
 
     def join(m):
         k = slot_of(m)
@@ -834,17 +841,85 @@
         lax.fori_loop(1, grid_cols, one, 0)
         row_done[:, lanes_of(j)] = row_turned[block_at(j)]
 
-    def recompute(source, target, k, bias):
-        half = grid_cols * rows // 2
+    def to_line(step):
+        part = lax.rem(z + step, grid_rows)
+        return part, {"rows": part}
+
+    def spread_line():
+        def one(step, carry):
+            part, where = to_line(step)
+            push(line_rows.at[z], line_rows.at[z], x_send.at[1], x_recv.at[1], where)
+            return carry
+
+        lax.fori_loop(1, grid_rows, one, 0)
+
+    def line_hidden(k, bias):
+        wait_for(line_rows.at[pl.ds(0, grid_rows - 1)], x_recv.at[1])
 
         def one(n, carry):
-            at = pl.ds(pl.multiple_of(lax.rem(n, 4) * 256, 256), 256)
-            x = xbuf[source, n // 4].reshape(half, width)
+            at = pl.ds(pl.multiple_of(n * 256, 256), 256)
+            x = line_rows[...].reshape(grid_rows * rows, width)
             pre = own_dot(x, wts[k, :, at], 1, 0) + bias[:, at]
-            xbuf[target, n // 4, :, :, at] = narrow(gelu_value(pre)).reshape(quads, rows, 256)
+            line_hid[:, :, at] = narrow(gelu_value(pre)).reshape(grid_rows, rows, 256)
             return carry
 
-        lax.fori_loop(0, 8, one, 0, unroll=2)
+        lax.fori_loop(0, width // 256, one, 0, unroll=2)
+
+    def spread_columns(m, values):
+        gsrc[m] = values
+
+        def one(step, carry):
+            part, where = to_line(step)
+            push(
+                gsrc.at[m, :, columns_of(part)], line_right.at[m - 1, z], g_send.at[m], g_recv.at[m], where
+            )
+            return carry
+
+        lax.fori_loop(1, grid_rows, one, 0)
+        line_right[m - 1, z] = gsrc[m, :, columns_of(z)]
+
+    def line_part(m, left):
+        wait_for(line_right.at[m - 1, pl.ds(0, grid_rows - 1)], g_recv.at[m])
+        size = width // grid_rows
+        turned = jnp.transpose(line_right[m - 1].reshape(grid_rows * rows, size))
+
+        def one(n, carry):
+            at = pl.ds(pl.multiple_of(n * 256, 256), 256)
+            block = left[:, :, at].reshape(grid_rows * rows, 256)
+            line_staged[m - 1, :, at] = narrow(own_dot(turned, block, 1, 0))
+            return carry
+
+        lax.fori_loop(0, width // 256, one, 0, unroll=4)
+
+        for q in range(quads):
+            push(
+                line_staged.at[m - 1, block_at(2 * q + 1 - core)], line_near.at[m - 1, q],
+                y_send.at[m], y_recv.at[m], {"cols": j + 1 - 2 * core},
+            )
+
+    def line_join(m):
+        wait_for(line_near.at[m - 1], y_recv.at[m])
+        for q in range(quads):
+            both = to_float(line_staged[m - 1, block_at(2 * q + core)]) + to_float(line_near[m - 1, q])
+            line_hand[m - 1, q] = narrow(both)
+
+        def give(step, carry):
+            q = lax.rem(quad + step, quads)
+            push(
+                line_hand.at[m - 1, q], line_sums.at[m - 1, quad], l_send.at[m - 1], l_recv.at[m - 1],
+                {"cols": 2 * q + core},
+            )
+            return carry
+
+        lax.fori_loop(1, quads, give, 0)
+        line_sums[m - 1, quad] = line_hand[m - 1, quad]
+
+    def line_total(m):
+        wait_for(line_sums.at[m - 1, pl.ds(0, quads - 1)], l_recv.at[m - 1])
+        result = to_float(line_sums[m - 1, 0])
+        for q in range(1, quads):
+            result = result + to_float(line_sums[m - 1, q])
+        cross_total[m] = result
 
     def join_small(m):
         join_parts(
@@ -910,7 +985,7 @@
     spread_x(6)
     loads[10].wait()
     for k in range(2):
-        win[k] = narrow(own_dot(order[...], win_raw[k], 1, 0))
+        win[k] = narrow(own_dot(order[...], win_raw[:, k, :], 1, 0))
     query_inputs = own_dot(query_low, win[0], 1, 1)
     spare = pl.ds(2 * LANES, 16)
     spare_row = lax.broadcasted_iota(jnp.int32, (16, width), 0)
@@ -989,6 +1064,8 @@
     half_lane = lax.broadcasted_iota(jnp.int32, (held_rows, LANES), 1) // rows
     xcoef[...] += jnp.where(half_lane == 0, col_out[0], col_out[1])
 
+    for copy in fixed[1:]:
+        copy.wait()
     wait_for(colbuf.at[pl.ds(0, grid_cols - 1)], misc_recv.at[0])
     for part in range(grid_rows):
         at = pl.ds(part * tile_rows, tile_rows)
@@ -1106,7 +1183,8 @@
     first = lat + tmp[...] + bc[4:5]
     act[FIRST] = first
     normed_c = norm_forward(first, gc[1:2], bc[1:2])
-    xbuf[1, core, quad] = normed_c
+    line_rows[z] = normed_c
+    spread_line()
     loads[C1].wait()
     times(normed_c, C1, tmp)
     pre = tmp[...] + bc[5:6]
@@ -1117,7 +1195,7 @@
     second = act[FIRST] + tmp[...] + bc[6:7]
     act[SECOND] = second
     normed_t = norm_forward(second, gs[0:1], bs[0:1])
-    xbuf[4, core, quad] = normed_t
+    xbuf[XS[4], core, quad] = normed_t
     mine = core * quads + quad
 
     def block_of(peer):
@@ -1187,13 +1265,13 @@
     loads[SO].wait()
     wait_for(mix_b.at[:, pl.ds(0, chunk * (grid_cols - 1))], a_recv.at[0])
     mixed_rows = mix_b[...]
-    xbuf[3, core, quad] = mixed_rows
+    xbuf[XS[3], core, quad] = mixed_rows
     times(mixed_rows, SO, tmp)
     relay_x(4)
     third = act[SECOND] + tmp[...] + bs[4:5]
     act[THIRD] = third
     normed_s = norm_forward(third, gs[1:2], bs[1:2])
-    xbuf[5, core, quad] = normed_s
+    xbuf[XS[5], core, quad] = normed_s
     background(2)
     loads[S1].wait()
     times(normed_s, S1, tmp)
@@ -1225,8 +1303,9 @@
     dmix_b[mine] = gsrc[12, :, lanes_of(j)]
     background(4)
     spread_g(4, pre_low)
+    line_hidden(C1, biases.at[5:6])
     have_x(6)
-    weight_part(8, have_g(5), xbuf.at[6])
+    weight_part(8, have_g(5), xbuf.at[XS[6]])
     spread_g(6, out_low)
     background(5)
     wait_for(dmix_b.at[pl.ds(0, grid_cols - 1)], a_recv.at[1])
@@ -1277,29 +1356,26 @@
     lax.fori_loop(0, head_rows // per, head_values, 0, unroll=2)
     from_heads(2)
     background(6)
-    join_rows(staged.at[slot_of(8)], 8)
     lax.fori_loop(0, head_rows // per, head_queries, 0, unroll=2)
     from_heads(0)
     background(7)
-    relay_x(5)
+    relay_x(3)
     lax.fori_loop(0, head_rows // per, head_keys, 0, unroll=2)
     from_heads(1)
     background(8)
-    relay_x(1)
+    join_rows(staged.at[slot_of(8)], 8)
 
     def column_sum(values):
         return jnp.sum(to_float(values), axis=0, keepdims=True)
 
-    have_x(5)
-    right = have_g(4)
-    bias_s5 = column_sum(right)
-    weight_part(7, right, xbuf.at[5])
+    have_x(3)
+    right = have_g(6)
+    bias_s4 = column_sum(right)
+    weight_part(9, right, xbuf.at[XS[3]])
     rows_back(2)
     times_t(dqkv_b[2], SV, tmp)
     rows_back(0)
     times_t(dqkv_b[0], SQ, tmp, True)
-    have_x(1)
-    recompute(1, 2, C1, biases.at[5:6])
     rows_back(1)
     times_t(dqkv_b[1], SK, tmp, True)
     background(9)
@@ -1307,29 +1383,16 @@
     gradient = act[GRAD] + d_rows
     act[GRAD] = gradient
     second_low = narrow(gradient)
-    spread_g(2, second_low)
+    spread_columns(2, second_low)
+    lnvec[9:10, :] = jnp.sum(gradient, axis=0, keepdims=True)
     background(10)
     times_t(second_low, C2, tmp)
     d_pre = tmp[...] * gelu_slope(act[PRE_C])
     pre_low = narrow(d_pre)
-    spread_g(1, pre_low)
+    spread_columns(1, pre_low)
+    lnvec[10:11, :] = jnp.sum(d_pre, axis=0, keepdims=True)
     background(11)
-    join(7)
-    relay_x(3)
-    times_t(pre_low, C1, tmp)
-    d_rows, lnvec[2:3, :], lnvec[3:4, :] = norm_gradient(act[FIRST], gc[1:2], tmp[...])
-    gradient = act[GRAD] + d_rows
-    act[GRAD] = gradient
-    out_low = narrow(gradient)
-    spread_g(3, out_low)
-    times_t(out_low, CO, tmp)
-    d_attended = narrow(tmp[...])
-    spread_g(8, d_attended)
-
-    have_x(3)
-    right = have_g(6)
-    bias_s4 = column_sum(right)
-    weight_part(9, right, xbuf.at[3])
+    join(9)
     have_x(4)
     for k in (2, 0, 1):
         right = have_g(9 + k)
@@ -1337,7 +1400,25 @@
             bias_s2 = column_sum(right)
         elif k == 2:
             bias_s3 = column_sum(right)
-        weight_part(4 + k, right, xbuf.at[4])
+        weight_part(4 + k, right, xbuf.at[XS[4]])
+    times_t(pre_low, C1, tmp)
+    d_rows, lnvec[2:3, :], lnvec[3:4, :] = norm_gradient(act[FIRST], gc[1:2], tmp[...])
+    gradient = act[GRAD] + d_rows
+    act[GRAD] = gradient
+    out_low = narrow(gradient)
+    spread_g(3, out_low)
+    relay_x(5)
+    times_t(out_low, CO, tmp)
+    d_attended = narrow(tmp[...])
+    spread_g(8, d_attended)
+    background(12)
+    line_part(2, line_hid)
+    line_part(1, line_rows)
+    line_join(2)
+    have_x(5)
+    right = have_g(4)
+    bias_s5 = column_sum(right)
+    weight_part(7, right, xbuf.at[XS[5]])
 
     grad_inputs = own_dot(d_attended, win[1], 1, 1)
     d_attended = to_float(d_attended)
@@ -1378,7 +1459,7 @@
         place_now = lax.rem(s, 6)
         line = pl.ds(pl.multiple_of((place_now // 2) * tall, 32), tall)
         lane = pl.ds(pl.multiple_of(lax.rem(place_now, 2) * WIDE, LANES), WIDE)
-        return wts.at[1 + s // 6, line, lane]
+        return wts.at[4 + s // 6, line, lane]
 
     def back_pass(s, carry):
         total, found = carry
@@ -1396,24 +1477,18 @@
         result = None
         for pair in range(block * STEPS_HELD // 2, min((block + 1) * STEPS_HELD, steps) // 2):
             line = pl.ds((pair % 3) * tall, tall)
-            left = wts[1 + pair // 3, line, pl.ds(0, 2 * WIDE)]
+            left = wts[4 + pair // 3, line, pl.ds(0, 2 * WIDE)]
             part = own_dot(left, cgright[pair % (STEPS_HELD // 2)], 1, 0)
             result = part if result is None else result + part
         cgacc[block] = result
 
     carry = (jnp.zeros((1, LANES), f32), jnp.zeros((8, LANES), f32))
     third_of = steps // 3
+    line_join(1)
     carry = in_groups(back_pass, 0, third_of, carry)
     finish_rows(8)
-    join(9)
-    right = have_g(2)
-    bias_c6 = column_sum(right)
-    weight_part(2, right, xbuf.at[2])
-    right = have_g(1)
-    bias_c5 = column_sum(right)
-    weight_part(1, right, xbuf.at[1])
+    join(6)
     carry = in_groups(back_pass, third_of, 2 * third_of, carry)
-    join(6)
     join(4)
     x_arrived(xsmall.at[0, 1 - core], 8)
     right = have_g(3)
@@ -1423,6 +1498,7 @@
     bias_c3 = column_sum(right)
     small_part(1, right, xsmall.at[0])
     total, found = in_groups(back_pass, 2 * third_of, steps, carry)
+    join(5)
     plain_scores = pixel_sums(found, 1.0) * score_scale
     total = total * score_scale
     score_total = fold(jnp.transpose(jnp.concatenate([total, jnp.zeros((LANES - 1, LANES), f32)], axis=0)))[:, 0:1]
@@ -1448,7 +1524,9 @@
     lnvec[8:9, :] = jnp.sum(to_float(cotangent[...]), axis=0, keepdims=True)
     lines = regroup(lnvec[...])
     for peer in range(grid_cols):
-        lnsend[peer] = jnp.concatenate([lines[:9, peer * chunk : (peer + 1) * chunk], shared], axis=0)
+        lnsend[peer] = jnp.concatenate(
+            [lines[:11, peer * chunk : (peer + 1) * chunk], shared, jnp.zeros((6, LANES), f32)], axis=0
+        )
 
     def send_ln(step, carry):
         peer, where = to_plane(step)
@@ -1457,7 +1535,7 @@
 
     lax.fori_loop(1, grid_cols, send_ln, 0)
     lnbuf[j] = lnsend[j]
-    join(5)
+    join(7)
     for block in range(0, blocks // 2):
         color_block(block)
     x_relay(xsmall.at[1, core], 9)
@@ -1469,9 +1547,7 @@
         color_block(block)
     x_arrived(xsmall.at[1, 1 - core], 9)
     small_part(0, have_g(7), xsmall.at[1])
-    join(2)
     color_block(blocks - 1)
-    join(1)
     for m in (2, 1):
         join_small(m)
 
@@ -1503,8 +1579,8 @@
         norms = norms + lnbuf[peer]
     vecsend[...] = jnp.concatenate(
         [
-            norms[:8], bias_c2, bias_c3, bias_c4, bias_c5, bias_c6, bias_s2, bias_s3,
-            bias_s4, bias_s5, norms[8:9], jnp.zeros((6, chunk), f32), norms[9:], jnp.zeros((1, chunk), f32),
+            norms[:8], bias_c2, bias_c3, bias_c4, norms[10:11], norms[9:10], bias_s2, bias_s3,
+            bias_s4, bias_s5, norms[8:9], jnp.zeros((6, chunk), f32), norms[11:18], jnp.zeros((1, chunk), f32),
         ],
         axis=0,
     )
@@ -1538,7 +1614,9 @@
         vectors = vectors + vecbuf[part]
     vector_out[...] = vectors[:24]
     input_vector_out[...] = vectors[24:]
-    for m in (7, 4, 5, 6, 9, 2, 1, 0):
+    for m in (2, 1):
+        line_total(m)
+    for m in (7, 4, 5, 6, 9, 0):
         wait_for(crossed.at[slot_of(m)], f_recv.at[m])
         result = kept_of(m)[...] + to_float(crossed[slot_of(m)])
         kept_of(m)[...] = result
@@ -1554,13 +1632,18 @@
     wait_for(cgfin.at[pl.ds(0, grid_rows - 1)], misc_recv.at[6])
     color_out[...] = cgfin[...]
 
-    for k in (0, 1, 3, 4, 5, 6):
-        wait_for(xbuf.at[k, 0, pl.ds(0, quads - 1)], x_send.at[k])
-        wait_for(xbuf.at[k, 0], y_send.at[k])
+    for k in (0, 3, 4, 5, 6):
+        wait_for(xbuf.at[XS[k], 0, pl.ds(0, quads - 1)], x_send.at[k])
+        wait_for(xbuf.at[XS[k], 0], y_send.at[k])
+    wait_for(line_rows.at[pl.ds(0, grid_rows - 1)], x_send.at[1])
+    for m in (1, 2):
+        wait_for(line_right.at[m - 1, pl.ds(0, grid_rows - 1)], g_send.at[m])
+        wait_for(line_near.at[m - 1], y_send.at[m])
+        wait_for(line_sums.at[m - 1, pl.ds(0, quads - 1)], l_send.at[m - 1])
     for k in range(2):
         wait_for(xsmall.at[k, 0, pl.ds(0, quads - 1)], x_send.at[8 + k])
         wait_for(xsmall.at[k, 0], y_send.at[8 + k])
-    for k in range(12):
+    for k in (0, 3, 4, 5, 6, 7, 8, 9, 10, 11):
         wait_for(gsrc.at[k, :, pl.ds(0, chunk * (grid_cols - 1))], g_send.at[k])
     wait_for(mix_s.at[pl.ds(0, grid_cols - 1)], a_send.at[0])
     wait_for(dmix_b.at[pl.ds(0, grid_cols - 1)], a_send.at[1])
@@ -1574,7 +1657,7 @@
     wait_for(cgfin.at[pl.ds(0, grid_rows - 1)], misc_send.at[6])
     wait_for(row_pair, r_send.at[8])
     wait_for(row_hand, f_send.at[8])
-    for m in (0, 1, 2, 4, 5, 6, 7, 9):
+    for m in (0, 4, 5, 6, 7, 9):
         wait_for(paired.at[slot_of(m)], r_send.at[m])
         wait_for(handed.at[slot_of(m)], f_send.at[m])
     for m in range(3):
@@ -1679,20 +1762,27 @@
     scratch = [
         ((10, width, width), bf16),
         ((2, WIDE, width), bf16),
-        (input_matrices.shape, bf16),
-        ((7, 2, quads, rows, width), bf16),
+        ((input_matrices.shape[1], 2, width), bf16),
+        ((5, 2, quads, rows, width), bf16),
         ((2, 2, quads, rows, WIDE), bf16),
         ((13, rows, width), bf16),
         ((12, 2, quads, rows, chunk), bf16),
-        ((9, chunk, width), bf16),
-        ((9, 2, own, width), bf16),
-        ((9, own, width), bf16),
-        ((9, own, width), bf16),
+        ((7, chunk, width), bf16),
+        ((7, 2, own, width), bf16),
+        ((7, own, width), bf16),
+        ((7, own, width), bf16),
         ((3, chunk, WIDE), bf16),
         ((3, 2, own, WIDE), bf16),
         ((3, own, WIDE), bf16),
         ((3, own, WIDE), bf16),
         ((3, own, WIDE), f32),
+        ((grid_rows, rows, width), bf16),
+        ((grid_rows, rows, width), bf16),
+        ((2, grid_rows, rows, width // grid_rows), bf16),
+        ((2, width // grid_rows, width), bf16),
+        ((2, quads, own, width), bf16),
+        ((2, quads, own, width), bf16),
+        ((2, quads, own, width), bf16),
         ((2, chunk, width // grid_rows), bf16),
         ((chunk, width // grid_rows), bf16),
         ((chunk, width // grid_rows), bf16),
@@ -1724,8 +1814,8 @@
         ((grid_rows, 32, LANES), f32),
         ((9, rows, width), f32),
         ((16, width), f32),
-        ((grid_cols, 16, chunk), f32),
-        ((grid_cols, 16, chunk), f32),
+        ((grid_cols, 24, chunk), f32),
+        ((grid_cols, 24, chunk), f32),
         ((8, width), f32),
         ((32, chunk), f32),
         ((grid_rows, 32, chunk), f32),
@@ -1738,8 +1828,10 @@
         ((3, grid_cols, rows, chunk), bf16),
         ((3, rows, width), bf16),
     ]
+    fixed = (order, place, pick, spread, back)
+    scratch = [(values.shape, bf16) for values in fixed] + scratch
     scratch = [pltpu.VMEM(dims, kind) for dims, kind in scratch]
-    scratch += [dma((count,)) for count in (11, 10, 10, 10, 10, 12, 12, 10, 10, 13, 13, 13, 13, 7, 7)]
+    scratch += [dma((count,)) for count in (5, 11, 10, 10, 10, 10, 12, 12, 10, 10, 13, 13, 13, 13, 2, 2, 7, 7)]
     outs = [
         ((rows, width), bf16),
         ((rows, width), f32),
@@ -1755,7 +1847,7 @@
     results = pl.pallas_call(
         functools.partial(layer_kernel, sizes),
         out_shape=[shape(dims, kind) for dims, kind in outs],
-        in_specs=[pl.BlockSpec(memory_space=pltpu.SMEM)] + [vmem] * 14 + [away] * 5,
+        in_specs=[pl.BlockSpec(memory_space=pltpu.SMEM)] + [vmem] * 9 + [away] * 10,
         out_specs=[vmem] * len(outs),
         scratch_shapes=scratch,
         compiler_params=pltpu.CompilerParams(
@@ -1771,20 +1863,16 @@
         jnp.transpose(pixel_colors, (0, 3, 1, 2)),
         in_gain,
         in_bias,
-        order,
         cross_gains,
         cross_biases,
         self_gains,
         self_biases,
-        place,
-        pick,
-        spread,
-        back,
+        *fixed,
         cross_matrices,
         cross_out,
         self_matrices,
         self_out,
-        input_matrices,
+        jnp.transpose(input_matrices, (1, 0, 2)),
     )
     count = input_matrices.shape[1]
     last = [

time: 124 us -> 111 us (0.90)
  Pallas kernels: 121 us -> 110 us
  local copies, waits for them, and re-layouts: 2.5 us -> 0 us
    pallas_call x1, Pallas kernels: 118 us -> 107 us  [local_kernel(): pl.pallas_call(functools.partial(layer_kernel, sizes), out_shape=[shape(d...]
    unnamed x1 -> x0, local copies, waits for them, and re-layouts: 2.5 us -> none
where the time goes in v5:
time: 111 us
  Pallas kernels  110 us (99%)
    pallas_call x1, Pallas kernels, local_kernel(): pl.pallas_call(functools.partial(layer_kernel, sizes), out_shape=[shape(d...  107 us
    pallas_call x1, Pallas kernels, local_kernel(): pl.pallas_call(functools.partial(finish_kernel, own, tile_rows, tile_cols...  2.94 us

profile of v5, /device:TPU:0, one launch (start us, length us, event | category | flops | bytes accessed | tf_op | source)
XLA Modules:
  0.0 110.8 jit_solution(3446637159838691303)
XLA Ops:
  0.7 107.0 %shard_map.326 = (bf16[64,1024]{1,0:T(8,128)(2,1)}, f32[64,1024]{1,0:T(8,128)}, f32[4,32,128]{2,1,0:T(8,128)}, f32[3,32,1024]{2,1,0:T(8,128)}, f32[32,1024]{1,0:...) custom-call(s32[4,4]{1,0:T(4,128)} %boxes.1, ...), custom_call_target="tpu_custom_call" | custom-call | flops 20000000000 | bytes 40000000 | tf_op jit(solution)/shard_map/pallas_call | solution.py:1847
  107.6 2.9 %shard_map.327 = (bf16[64,1024]{1,0:T(8,128)(2,1)}, f32[64,1024]{1,0:T(8,128)}, f32[3,9,4,72]{3,2,1,0:T(4,128)}, f32[3,32,1024]{2,1,0:T(8,128)}, f32[32,1024]{1,...) custom-call(bf16[64,1024]{1,0:T(8,128)(2,1)} %get-tuple-element.38.l, ...), custom_call_target="tpu_custom_call" | custom-call | tf_op jit(solution)/shard_map/pallas_call | solution.py:1894

commit v6 on v5

--- a/solution.py
+++ b/solution.py
@@ -19,7 +19,7 @@
 NEG = -1e30
 FREQ_TOP = 112.0
 VMEM_BYTES = 63 * 1024 * 1024
-PLAN = {0: ((4, 4),), 2: ((3, 4),), 5: ((5, 1),), 6: ((5, 1),), 9: ((5, 2),)}
+PLAN = {0: ((4, 4),), 2: ((3, 2),), 4: ((3, 2),), 9: ((5, 4),)}
 
 
 def narrow(values):
@@ -509,7 +509,7 @@
 
 
 STEPS_HELD = 8
-GROUP = 4
+GROUP = 12
 XS = {0: 0, 3: 1, 4: 2, 5: 3, 6: 4}
 LANES = 128
 MESH = pl.DeviceIdType.MESH
@@ -618,9 +618,9 @@
     order, place, pick, spread, back, wts, win, win_raw, xbuf, xsmall, gsrc, gbuf, staged, paired, handed, crossed, staged_small, paired_small, handed_small, crossed_small, kept_small,
     line_rows, line_hid, line_right, line_staged, line_near, line_hand, line_sums,
     row_pair, row_hand, row_cross, row_kept, row_turned, row_done, biases,
-    color_lines, color_tiles, colstage, colbuf, img, img7, fa, ft, sl, ycoef, xcoef, yfeat, xfeat, mixrow,
+    color_tiles, colstage, colbuf, img, img7, fa, ft, sl, ycoef, xcoef, yfeat, xfeat, mixrow,
     cgright, rowsum, colsum, cgacc, cgsend, cgbuf, cgsum, cgfin,
-    act, lnvec, lnsend, lnbuf, biasvec, vecsend, vecbuf,
+    act, lnvec, lnsend, lnbuf, vecsend, vecbuf,
     heads, probs, prob_grad, mix_s, mix_b, dmix_b, dqkv_s, dqkv_b,
     fixed_sem, weight_sem, x_send, x_recv, y_send, y_recv, g_send, g_recv, a_send, a_recv, r_send, r_recv, f_send, f_recv, l_send, l_recv,
     misc_send, misc_recv,
@@ -685,14 +685,14 @@
     for copy in fixed:
         copy.start()
 
-    color_lines[...] = jnp.zeros(color_lines.shape, f32)
+    cgsum[...] = jnp.zeros(cgsum.shape, f32)
     for channel in range(3):
         for col in range(tile_cols):
             line = channel * tile_cols + col
             shown = to_float(colors[channel, col])
             for image in range(grid_rows):
-                color_lines[image, line : line + 1, :tile_rows] = shown[image : image + 1]
-    color_tiles[...] = narrow(color_lines[...])
+                cgsum[image, line : line + 1, :tile_rows] = shown[image : image + 1]
+    color_tiles[...] = narrow(cgsum[...])
     gc, bc = to_float(cross_gains[...]), to_float(cross_biases[...])
     gs, bs = to_float(self_gains[...]), to_float(self_biases[...])
     fixed[0].wait()
@@ -963,7 +963,8 @@
 
         lax.fori_loop(0, width // 256, one, 0, unroll=4)
 
-    FIRST, SECOND, THIRD, PRE_C, PRE_S, TMP, ATT, GRAD, COT_BACK = range(9)
+    FIRST, SECOND, THIRD, PRE_C, PRE_S, TMP, ATT, GRAD = range(8)
+    COT_BACK = GRAD
     tmp = act.at[TMP]
 
     wait_for(colstage.at[pl.ds(0, grid_rows - 1)], misc_recv.at[5])
@@ -1790,7 +1791,6 @@
         ((width // grid_rows, chunk), f32),
         ((own, width), f32),
         ((8, width), f32),
-        ((grid_rows, 32, LANES), f32),
         ((grid_rows, 32, LANES), bf16),
         ((grid_rows, 32, LANES), bf16),
         ((grid_cols, grid_rows, 32, LANES), bf16),
@@ -1812,11 +1812,10 @@
         ((grid_cols, grid_rows, 32, LANES), bf16),
         ((grid_rows, 32, LANES), f32),
         ((grid_rows, 32, LANES), f32),
-        ((9, rows, width), f32),
+        ((8, rows, width), f32),
         ((16, width), f32),
         ((grid_cols, 24, chunk), f32),
         ((grid_cols, 24, chunk), f32),
-        ((8, width), f32),
         ((32, chunk), f32),
         ((grid_rows, 32, chunk), f32),
         ((3, grid_cols, rows, chunk), bf16),

time: 111 us -> 107 us (0.964)
  Pallas kernels: 110 us -> 106 us
    pallas_call x1, Pallas kernels: 107 us -> 103 us  [local_kernel(): pl.pallas_call(functools.partial(layer_kernel, sizes), out_shape=[shape(d...]
where the time goes in v6:
time: 107 us
  Pallas kernels  106 us (99%)
    pallas_call x1, Pallas kernels, local_kernel(): pl.pallas_call(functools.partial(layer_kernel, sizes), out_shape=[shape(d...  103 us
    pallas_call x1, Pallas kernels, local_kernel(): pl.pallas_call(functools.partial(finish_kernel, own, tile_rows, tile_cols...  2.94 us

profile of v6, /device:TPU:0, one launch (start us, length us, event | category | flops | bytes accessed | tf_op | source)
XLA Modules:
  0.0 106.7 jit_solution(5011651185261814541)
XLA Ops:
  0.7 102.9 %shard_map.326 = (bf16[64,1024]{1,0:T(8,128)(2,1)}, f32[64,1024]{1,0:T(8,128)}, f32[4,32,128]{2,1,0:T(8,128)}, f32[3,32,1024]{2,1,0:T(8,128)}, f32[32,1024]{1,0:...) custom-call(s32[4,4]{1,0:T(4,128)} %boxes.1, ...), custom_call_target="tpu_custom_call" | custom-call | flops 20000000000 | bytes 40000000 | tf_op jit(solution)/shard_map/pallas_call | solution.py:1846
  103.6 2.9 %shard_map.327 = (bf16[64,1024]{1,0:T(8,128)(2,1)}, f32[64,1024]{1,0:T(8,128)}, f32[3,9,4,72]{3,2,1,0:T(4,128)}, f32[3,32,1024]{2,1,0:T(8,128)}, f32[32,1024]{1,...) custom-call(bf16[64,1024]{1,0:T(8,128)(2,1)} %get-tuple-element.38.l, ...), custom_call_target="tpu_custom_call" | custom-call | tf_op jit(solution)/shard_map/pallas_call | solution.py:1893

commit v7 on v6

--- a/solution.py
+++ b/solution.py
@@ -1173,7 +1173,6 @@
     wide1 = lax.broadcasted_iota(jnp.int32, (rows, WIDE), 1)
     mixed_low = narrow(jnp.where(wide1 == 2 * LANES + 5, 1.0, plain_mixed * gin + bin_))
     xsmall[0, core, quad] = mixed_low
-    x_spread(xsmall.at[0, core, quad], 8)
     relay_x(0)
     relay_x(6)
     attended = own_dot(mixed_low, win[1], 1, 0)
@@ -1228,7 +1227,6 @@
     background(0)
     loads[S2].wait()
     times_t(cot_low, S2, act.at[COT_BACK])
-    x_relay(xsmall.at[0, core], 8)
     head_rows = grid_cols * rows
     per = 128
     each = per // rows
@@ -1380,6 +1378,7 @@
     rows_back(1)
     times_t(dqkv_b[1], SK, tmp, True)
     background(9)
+    x_spread(xsmall.at[0, core, quad], 8)
     d_rows, lnvec[4:5, :], lnvec[5:6, :] = norm_gradient(act[SECOND], gs[0:1], tmp[...])
     gradient = act[GRAD] + d_rows
     act[GRAD] = gradient
@@ -1486,6 +1485,7 @@
     carry = (jnp.zeros((1, LANES), f32), jnp.zeros((8, LANES), f32))
     third_of = steps // 3
     line_join(1)
+    x_relay(xsmall.at[0, core], 8)
     carry = in_groups(back_pass, 0, third_of, carry)
     finish_rows(8)
     join(6)
@@ -1505,16 +1505,16 @@
     score_total = fold(jnp.transpose(jnp.concatenate([total, jnp.zeros((LANES - 1, LANES), f32)], axis=0)))[:, 0:1]
     score_low = narrow(plain_scores * gin + score_total * bin_)
     xsmall[1, core, quad] = score_low
-    x_spread(xsmall.at[1, core, quad], 9)
 
     def d_query_part(n, carry):
         at = pl.ds(pl.multiple_of(n * 256, 256), 256)
         tmp[:, at] = own_dot(score_low, win[0, :, at], 1, 0)
         return carry
 
-    lax.fori_loop(0, width // 256, d_query_part, 0)
+    lax.fori_loop(0, width // 256, d_query_part, 0, unroll=4)
     query_grad_low = narrow(tmp[...])
     spread_g(0, query_grad_low)
+    x_spread(xsmall.at[1, core, quad], 9)
     gain_part = jnp.sum(query_inputs * plain_scores + grad_inputs * plain_mixed, axis=0, keepdims=True)
     bias_part = jnp.sum(query_inputs * score_total + grad_inputs, axis=0, keepdims=True)
     cuts = [part[:, k * LANES : (k + 1) * LANES] for part in (gain_part, bias_part) for k in range(3)]
@@ -1539,16 +1539,16 @@
     join(7)
     for block in range(0, blocks // 2):
         color_block(block)
-    x_relay(xsmall.at[1, core], 9)
     have_x(0)
     right = have_g(0)
     bias_c2 = column_sum(right)
     weight_part(0, right, xbuf.at[0])
+    x_relay(xsmall.at[1, core], 9)
     for block in range(blocks // 2, blocks - 1):
         color_block(block)
+    color_block(blocks - 1)
     x_arrived(xsmall.at[1, 1 - core], 9)
     small_part(0, have_g(7), xsmall.at[1])
-    color_block(blocks - 1)
     for m in (2, 1):
         join_small(m)
 

time: 107 us -> 107 us (level)
  no operation moved by 1% of the time
where the time goes in v7:
time: 107 us
  Pallas kernels  106 us (99%)
    pallas_call x1, Pallas kernels, local_kernel(): pl.pallas_call(functools.partial(layer_kernel, sizes), out_shape=[shape(d...  103 us
    pallas_call x1, Pallas kernels, local_kernel(): pl.pallas_call(functools.partial(finish_kernel, own, tile_rows, tile_cols...  2.94 us

profile of v7, /device:TPU:0, one launch (start us, length us, event | category | flops | bytes accessed | tf_op | source)
XLA Modules:
  0.0 106.6 jit_solution(8933625483095803587)
XLA Ops:
  0.7 102.8 %shard_map.326 = (bf16[64,1024]{1,0:T(8,128)(2,1)}, f32[64,1024]{1,0:T(8,128)}, f32[4,32,128]{2,1,0:T(8,128)}, f32[3,32,1024]{2,1,0:T(8,128)}, f32[32,1024]{1,0:...) custom-call(s32[4,4]{1,0:T(4,128)} %boxes.1, ...), custom_call_target="tpu_custom_call" | custom-call | flops 20000000000 | bytes 40000000 | tf_op jit(solution)/shard_map/pallas_call | solution.py:1846
  103.4 2.9 %shard_map.327 = (bf16[64,1024]{1,0:T(8,128)(2,1)}, f32[64,1024]{1,0:T(8,128)}, f32[3,9,4,72]{3,2,1,0:T(4,128)}, f32[3,32,1024]{2,1,0:T(8,128)}, f32[32,1024]{1,...) custom-call(bf16[64,1024]{1,0:T(8,128)(2,1)} %get-tuple-element.38.l, ...), custom_call_target="tpu_custom_call" | custom-call | tf_op jit(solution)/shard_map/pallas_call | solution.py:1893
